TPU v7x, 32 devices: a whole 2x2x4 slice. The times are simulated.
32 devices in a mesh: patch: 8 (over z, y), sub: 4 (over x, core).
Axes of the slice: x: 2, y: 2, z: 4, core: 2. Of those that a mesh axis runs over, the one named last changes fastest.
Arguments:
- pieces_image: float32 [4, 256, 8, 256], P('sub', 'patch'), may hold values from -6 to 6
- pieces_variance: float32 [4, 256, 8, 256], P('sub', 'patch'), may hold values from 0.5 to 2
- piece_patch: int32 [4, 256, 1], P('sub', 'patch'), may hold values from 0 to 7; in each aligned block of 32 rows (0 to 31, 32 to 63, ..., all dimensions but the last counted through in order) at most 8 rows name the same one
- piece_cell: int32 [4, 256], P('sub', 'patch'), may hold values from 0 to 31
- stamp_row: int32 [8, 48], P('patch', 'sub'), may hold values from 0 to 63
- stamp_col: int32 [8, 48], P('patch', 'sub'), may hold values from 0 to 255
- stamp_count: int32 [8, 4], P('patch', 'sub'), may hold values from 2 to 12, as said below
- warp_offsets: int32 [4], replicated, may hold values from 0 to 8
Outputs:
- difference: float32 [4, 8, 256, 256], P(None, 'patch', 'sub')
- significance: float32 [4, 8, 256, 256], P(None, 'patch', 'sub')
Inputs may be any that keep to these rules, and one draw needn't show every extreme that they name: `piece_patch`: the pieces of one device name the same patch at most 8 times, and in every draw some device names some patch exactly 8 times. `stamp_count`: stamps of a sub-tile whose index is this count or more are unused.
All inputs are finite; a program needn't handle non-finite values.
Results may differ from a plain program's by a relative error of at most 0.0003.
Values sent between devices are 32-bit elements; how exact they have to be, the bound alone decides.
No kernel may reach another device: no remote copies, remote signals or barrier semaphores. Data moves between devices by JAX's collectives and lax.ppermute only.
A program may use at most 64 MiB of HBM per device.

v0:
```python
import functools

import jax
import jax.numpy as jnp
import ml_dtypes
import numpy as np
from jax import lax
from jax.experimental import pallas as pl
from jax.experimental.pallas import tpu as pltpu
from jax.sharding import PartitionSpec as P

NCELL = 8
KR = 10
PR = 10
SH = 15
WARP = 4

SIGMAS = (0.75, 1.5, 3.0)
DEGREES = (4, 4, 3)
PSF_SIGMA = 2.0
SKY_VAR = 0.1
RIDGE = 0.5
EPS = 1e-05

F32 = jnp.float32
BF16 = jnp.bfloat16
LANES = 128
HALO = 24
EDGE = 16
BLOCK = 32
WINDOW = 64
VMEM_BYTES = 20 * 1024 * 1024

TILES = ((0, (0, 2)), (0, (1, 3, 4)), (1, (0, 2)), (1, (1, 3, 4)), (2, (0, 1, 3)), (2, (2,)))
SLOTS = 8 * len(TILES)
HALF = 64
TAP_FIRST = (0, DEGREES[0] + 1, DEGREES[0] + DEGREES[1] + 2)
TAP_COUNT = sum(DEGREES) + len(DEGREES)


def slot_table():
    result = {}
    for tile, (group, columns) in enumerate(TILES):
        slot = 8 * tile
        for column in columns:
            for row in range(DEGREES[group] + 1 - column):
                result[slot] = (TAP_FIRST[group] + row, TAP_FIRST[group] + column)
                slot += 1
    return result


SLOT_TAPS = slot_table()
ONE_SLOT = 8 * (len(TILES) - 1) + 2
SCI_SLOT = ONE_SLOT + 1
LIVE_SLOTS = sorted(SLOT_TAPS) + [ONE_SLOT]


def basis_taps():
    offset = np.arange(-KR, KR + 1, dtype=np.float64)
    rows = []
    for spread, degree in zip(SIGMAS, DEGREES):
        scaled = offset / spread
        envelope = np.exp(-0.5 * scaled * scaled)
        previous, current = np.zeros_like(scaled), np.ones_like(scaled)
        for term_no in range(degree + 1):
            rows.append(current * envelope)
            previous, current = current, scaled * current - term_no * previous
    taps = np.stack(rows)
    return taps / np.sqrt(np.sum(taps * taps, axis=1, keepdims=True))


def psf_taps():
    offset = np.arange(-PR, PR + 1, dtype=np.float64)
    values = np.exp(-0.5 * (offset / PSF_SIGMA) ** 2)
    return values / values.sum()


def band(taps, rows, columns, shift):
    radius = (taps.shape[-1] - 1) // 2
    offset = np.arange(columns)[None, :] - shift - np.arange(rows)[:, None]
    inside = np.abs(offset) <= radius
    return np.where(inside, taps[..., np.clip(offset + radius, 0, 2 * radius)], 0.0)


def halves(values):
    values = np.asarray(values, np.float32)
    high = values.astype(ml_dtypes.bfloat16)
    low = (values - high.astype(np.float32)).astype(ml_dtypes.bfloat16)
    return high, low


def tile_depth(tile, visits):
    depth = len(TILES[tile][1]) * WINDOW
    return depth + visits * BLOCK + 16 if tile == len(TILES) - 1 else depth


@functools.lru_cache(maxsize=None)
def constants(visits, row_count, col_count):
    taps = basis_taps()
    column_bands = np.stack([band(taps[t], col_count, col_count, 0).T for t in range(TAP_COUNT)])
    toeplitz = np.stack([band(taps[t], BLOCK, WINDOW, EDGE) for t in range(TAP_COUNT)])
    row_parts = []
    for tile, (group, columns) in enumerate(TILES):
        matrix = np.zeros((BLOCK, 8, tile_depth(tile, visits)))
        slot = 0
        for place, column in enumerate(columns):
            for row in range(DEGREES[group] + 1 - column):
                matrix[:, slot, place * WINDOW : (place + 1) * WINDOW] = toeplitz[TAP_FIRST[group] + row]
                slot += 1
        if tile == len(TILES) - 1:
            base = len(columns) * WINDOW
            for visit in range(visits):
                first = base + visit * BLOCK
                matrix[np.arange(BLOCK), slot + 1 + visit, first + np.arange(BLOCK)] = 1.0
            matrix[:, slot, base + visits * BLOCK] = 1.0
        row_parts.append(matrix.reshape(BLOCK * 8, -1))
    depth = col_count
    for tile, part in enumerate(row_parts):
        row_parts[tile] = np.pad(part, ((0, 0), (0, depth - part.shape[1])))
    design = np.stack(halves(np.concatenate([column_bands, np.stack(row_parts)])), axis=1)
    psf = psf_taps()
    filters = np.stack([half for power in (1, 2) for half in halves(band(psf**power, col_count, col_count, 0).T)])
    edges = np.stack(
        [half for power in (1, 2) for half in halves(band(psf**power, row_count, row_count + 2 * EDGE, EDGE))]
    )
    edges = np.pad(edges, ((0, 0), (0, 0), (0, -edges.shape[2] % LANES)))
    doubled = np.concatenate([toeplitz, toeplitz], axis=2).astype(np.float32)
    return design, filters, edges, doubled


def split(values):
    high = values.astype(BF16)
    return high, (values - high.astype(F32)).astype(BF16)


def mul(left, right):
    return jnp.dot(left, right, preferred_element_type=F32)


def mul3(left, right):
    return mul(left[0], right[0]) + mul(left[0], right[1]) + mul(left[1], right[0])


def mul_nt(left, right):
    return lax.dot_general(left, right, (((1,), (1,)), ((), ())), preferred_element_type=F32)


def fill(cfg, outs, source, chosen_ref, table_ref):
    patches, capacity = cfg
    me = lax.axis_index("patch")
    for block in range(patches):
        if len(outs) == 1:
            out, place, away = outs[0], block, block ^ me
        else:
            out, place, away = outs[block], 0, block
        for rank in range(capacity):
            piece = chosen_ref[away * capacity + rank]
            out[place, 2 * rank] = source[0, piece, :, :LANES]
            out[place, 2 * rank + 1] = source[0, piece, :, LANES:]
        if table_ref is not None:
            out[place, 2 * capacity] = jnp.broadcast_to(table_ref[pl.ds(away, 1), :], (8, LANES))


def start_copies(pairs, sems):
    copies = [pltpu.make_async_copy(source, place, sems.at[number]) for number, (source, place) in enumerate(pairs)]
    for copy in copies:
        copy.start()
    return copies


def pack_kernel(cfg, *refs):
    patches, capacity, pieces, blocks, slots = cfg
    sources, refs = refs[:7], refs[7:]
    outs, refs = refs[:blocks], refs[blocks:]
    stamp_out, warp_out, chosen_ref, table_ref, count_ref, *held = refs
    held, sems = held[:-1], held[-1]
    target_ref, cell_ref, row_ref, col_ref, live_ref, image_ref = held
    copies = start_copies(
        zip(sources, (target_ref, cell_ref, row_ref, col_ref, live_ref, image_ref, warp_out)), sems
    )
    me = lax.axis_index("patch")
    for entry in range(patches * capacity):
        chosen_ref[entry] = 0
    for entry in range(patches):
        count_ref[entry] = 0
    line = lax.broadcasted_iota(jnp.int32, table_ref.shape, 0)
    lane = lax.broadcasted_iota(jnp.int32, table_ref.shape, 1)
    copies[0].wait()
    copies[1].wait()
    table = jnp.full(table_ref.shape, -1.0, F32)
    for piece in range(pieces):
        away = target_ref[0, piece] ^ me
        rank = count_ref[away]
        count_ref[away] = rank + 1
        chosen_ref[away * capacity + rank] = piece
        value = cell_ref[0, piece].astype(F32)
        table = jnp.where((line == away) & (lane == rank), value, table)
    table_ref[...] = table
    for copy in copies[2:5]:
        copy.wait()
    live = lax.broadcasted_iota(jnp.int32, (1, slots), 1) < live_ref[0, 0]
    stamp_out[...] = jnp.zeros(stamp_out.shape, F32)
    stamp_out[0:1, :slots] = row_ref[...].astype(F32)
    stamp_out[1:2, :slots] = col_ref[...].astype(F32)
    stamp_out[2:3, :slots] = jnp.where(live, 1.0, 0.0)
    copies[5].wait()
    fill((patches, capacity), outs, image_ref, chosen_ref, table_ref)
    copies[6].wait()


def pack_more_kernel(cfg, chosen_ref, var_hbm, *refs):
    patches, capacity, blocks = cfg
    outs, (var_ref, sems) = refs[:blocks], refs[blocks:]
    (copy,) = start_copies([(var_hbm, var_ref)], sems)
    copy.wait()
    fill((patches, capacity), outs, var_ref, chosen_ref, None)


def assemble(cfg, blocks, cells_ref, total_ref, me):
    patches, capacity = cfg
    total_ref[...] = jnp.zeros(total_ref.shape, F32)
    for block in range(patches):
        if len(blocks) == 1:
            ref, place, away = blocks[0], block, block ^ me
        else:
            ref, place, away = blocks[block], 0, block
        for rank in range(capacity):
            cell = cells_ref[away * capacity + rank]
            total_ref[cell, 0] += ref[place, 2 * rank]
            total_ref[cell, 1] += ref[place, 2 * rank + 1]


def warped(total_ref, visit, warp_ref, row_count, col_count):
    first = visit * NCELL
    left = total_ref[first : first + NCELL, 0].reshape(row_count, LANES)
    right = total_ref[first : first + NCELL, 1].reshape(row_count, LANES)
    plane = jnp.concatenate([left, right], axis=1)
    offset = warp_ref[visit] - WARP
    moved = pltpu.roll(plane, lax.rem(col_count - offset, col_count), 1)
    source = lax.broadcasted_iota(jnp.int32, plane.shape, 1) + offset
    return jnp.where((source >= 0) & (source < col_count), moved, 0.0)


def image_kernel(cfg, warp_ref, stamp_ref, *refs):
    patches, capacity, visits, row_count, col_count, block_count = cfg
    blocks = refs[:block_count]
    sci_ref, up_ref, down_ref, cells_ref, total_ref, near_ref, sems = refs[block_count:]
    me = lax.axis_index("patch")
    copies = []
    for block in range(patches):
        ref, place = (blocks[0], block) if block_count == 1 else (blocks[block], 0)
        copies.append(
            pltpu.make_async_copy(
                ref.at[place, 2 * capacity, pl.ds(0, 1), :], near_ref.at[pl.ds(block, 1), :], sems.at[block]
            )
        )
    for copy in copies:
        copy.start()
    for copy in copies:
        copy.wait()
    for block in range(patches):
        away = block ^ me if block_count == 1 else block
        for rank in range(capacity):
            cell = near_ref[block, rank].astype(jnp.int32)
            cells_ref[away * capacity + rank] = jnp.where(cell < 0, visits * NCELL, cell)
    assemble((patches, capacity), blocks, cells_ref, total_ref, me)
    for visit in range(visits):
        plane = warped(total_ref, visit, warp_ref, row_count, col_count)
        sci_ref[visit] = plane
        up_ref[visit * HALO : (visit + 1) * HALO] = plane[:HALO]
        down_ref[visit * HALO : (visit + 1) * HALO] = plane[row_count - HALO :]
    first = visits * HALO
    for ref in (up_ref, down_ref):
        ref[first : first + 8, :LANES] = stamp_ref[...]
        ref[first : first + 8, LANES:] = jnp.zeros((8, col_count - LANES), F32)


def near_mask(stamps, shift, row_count, col_count):
    row_at = lax.broadcasted_iota(jnp.int32, (row_count, LANES), 0).astype(F32)
    col_at = lax.broadcasted_iota(jnp.int32, (col_count, LANES), 0).astype(F32)
    row_in = (jnp.abs(row_at - (stamps[0:1] + shift)) <= SH) & (stamps[2:3] > 0.5)
    col_in = jnp.abs(col_at - stamps[1:2]) <= SH
    return mul_nt(jnp.where(row_in, 1.0, 0.0).astype(BF16), jnp.where(col_in, 1.0, 0.0).astype(BF16))


def filter_columns(image, tap, held_ref):
    rows = image[0].shape[0]
    both = mul(jnp.concatenate(image, axis=0), held_ref[tap, 0])
    return split(both[:rows] + both[rows:] + mul(image[0], held_ref[tap, 1]))


def own_kernel(cfg, sci_ref, stamp_ref, fixed_ref, held_ref, high_ref, low_ref, hits_ref, sems):
    visits, row_count, col_count = cfg
    copies = start_copies([(fixed_ref.at[n], held_ref.at[n]) for n in range(TAP_COUNT + len(TILES))], sems)
    own = sci_ref[0]
    for visit in range(1, visits):
        own = own + sci_ref[visit]
    template = split(own * (1.0 / visits))
    hits_ref[...] = near_mask(stamp_ref[...], 0.0, row_count, col_count)
    for tap in range(TAP_COUNT):
        copies[tap].wait()
        high_ref[tap], low_ref[tap] = filter_columns(template, tap, held_ref)
    for copy in copies[TAP_COUNT:]:
        copy.wait()


def design_kernel(cfg, sci_ref, above_ref, below_ref, held_ref, own_high, own_low, hits_ref, *refs):
    visits, row_count, col_count = cfg
    design_ref, mask_ref, high_out, low_out, wide_out, high_ref, low_ref, wide_ref, sems = refs
    above = above_ref[0:HALO]
    below = below_ref[0:HALO]
    for visit in range(1, visits):
        above = above + above_ref[visit * HALO : (visit + 1) * HALO]
        below = below + below_ref[visit * HALO : (visit + 1) * HALO]
    rim = jnp.zeros((BLOCK - HALO, col_count), F32)
    template = split(jnp.concatenate([rim, above, below, rim], axis=0) * (1.0 / visits))
    for tap in range(TAP_COUNT):
        for ref, own, part in zip((high_ref, low_ref), (own_high, own_low), filter_columns(template, tap, held_ref)):
            ref[tap, :BLOCK] = part[:BLOCK]
            ref[tap, BLOCK : BLOCK + row_count] = own[tap]
            ref[tap, BLOCK + row_count :] = part[BLOCK:]
    for visit in range(visits):
        first = visit * HALO
        wide_ref[visit, :EDGE] = above_ref[first + HALO - EDGE : first + HALO]
        wide_ref[visit, EDGE : EDGE + row_count] = sci_ref[visit]
        wide_ref[visit, EDGE + row_count :] = below_ref[first : first + EDGE]
    copies = start_copies(((high_ref, high_out), (low_ref, low_out), (wide_ref, wide_out)), sems)
    for block in range(row_count // BLOCK):
        start = EDGE + block * BLOCK
        for tile, (group, columns) in enumerate(TILES):
            depth = tile_depth(tile, visits)
            rows = [held_ref[TAP_COUNT + tile, half, :, :depth] for half in range(2)]
            taps = [TAP_FIRST[group] + column for column in columns]
            high = [high_ref[tap, start : start + WINDOW] for tap in taps]
            low = [low_ref[tap, start : start + WINDOW] for tap in taps]
            if tile == len(TILES) - 1:
                for visit in range(visits):
                    pair = split(sci_ref[visit, block * BLOCK : (block + 1) * BLOCK])
                    high.append(pair[0])
                    low.append(pair[1])
                high.append(jnp.ones((16, col_count), BF16))
                low.append(jnp.zeros((16, col_count), BF16))
            both = mul(jnp.concatenate(rows, axis=0), jnp.concatenate(high, axis=0))
            part = both[: 8 * BLOCK] + both[8 * BLOCK :] + mul(rows[0], jnp.concatenate(low, axis=0))
            design_ref[block * BLOCK : (block + 1) * BLOCK, 8 * tile : 8 * tile + 8] = part.reshape(
                BLOCK, 8, col_count
            )
    first = visits * HALO
    hits = hits_ref[...]
    for ref, shift in ((above_ref, -row_count), (below_ref, row_count)):
        hits = hits + near_mask(ref[first : first + 8, :LANES], float(shift), row_count, col_count)
    mask_ref[...] = jnp.minimum(hits, 1.0)
    for copy in copies:
        copy.wait()


def gram_kernel(cfg, warp_ref, cells_ref, mask_ref, design_ref, *refs):
    patches, capacity, visits, row_count, col_count, block_count, step = cfg
    blocks = refs[:block_count]
    var_ref, down_ref, up_ref, gram_ref, total_ref, weight_ref, sum_ref = refs[block_count:]
    me = lax.axis_index("patch")
    assemble((patches, capacity), blocks, cells_ref, total_ref, me)
    shared = jnp.full((row_count, col_count), SKY_VAR, F32)
    for visit in range(visits):
        plane = warped(total_ref, visit, warp_ref, row_count, col_count)
        var_ref[visit] = plane
        shared = shared + plane * (1.0 / (visits * visits))
    mask = mask_ref[...]
    for visit in range(visits):
        weight_ref[visit] = mask / (var_ref[visit] + shared)
    sum_ref[...] = jnp.zeros(sum_ref.shape, F32)

    def body(number, carry):
        left, right = [], []
        for extra in range(step):
            row = number * step + extra
            design = design_ref[row]
            high, low = split(design)
            blank = jnp.zeros((HALF - SLOTS, col_count), BF16)
            right.append(jnp.concatenate([high, blank, low, blank], axis=0))
            scaled = [design * weight_ref[visit, pl.ds(row, 1), :] for visit in range(visits)]
            left.append(jnp.concatenate(split(jnp.concatenate(scaled, axis=0)), axis=0))
        sum_ref[...] += mul_nt(jnp.concatenate(left, axis=1), jnp.concatenate(right, axis=1))
        return carry

    lax.fori_loop(0, row_count // step, body, 0)
    lane = lax.broadcasted_iota(jnp.int32, (SLOTS, 2 * HALF), 1)
    both = []
    for visit in range(visits):
        first = visit * SLOTS
        second = (visits + visit) * SLOTS
        value = sum_ref[first : first + SLOTS] + sum_ref[second : second + SLOTS]
        both.append(value + pltpu.roll(value, HALF, 1))
    for pair in range(visits // 2):
        value = jnp.where(lane < HALF, both[2 * pair], both[2 * pair + 1])
        for ref in (gram_ref, down_ref, up_ref):
            ref[pair * SLOTS : (pair + 1) * SLOTS] = value
    first = visits // 2 * SLOTS
    for visit in range(visits):
        for part in range(col_count // LANES):
            place = first + (visit * (col_count // LANES) + part) * EDGE
            lanes = slice(part * LANES, (part + 1) * LANES)
            down_ref[place : place + EDGE] = var_ref[visit, row_count - EDGE :, lanes]
            up_ref[place : place + EDGE] = var_ref[visit, :EDGE, lanes]


def solve_kernel(cfg, var_ref, *refs):
    visits, row_count, col_count, subtiles, normalizer, gram_count = cfg
    grams = refs[:gram_count]
    fixed = refs[gram_count : gram_count + 6]
    diff_ref, sig_ref, *held, sems = refs[gram_count + 6 :]
    copies = start_copies(zip(fixed, held), sems)
    filter_ref, edge_ref, doubled_ref, wide_ref, high_ref, low_ref = held
    sub = lax.axis_index("sub")
    high_rows = row_count + 2 * EDGE
    parts = col_count // LANES
    first = visits // 2 * SLOTS

    def halo(ref, visit):
        pieces = [ref[first + (visit * parts + part) * EDGE :][:EDGE] for part in range(parts)]
        return jnp.concatenate(pieces, axis=1)

    from_above, from_below = grams[1], grams[-1]
    row_at = lax.broadcasted_iota(jnp.int32, (high_rows, col_count), 0) + sub * row_count - EDGE
    inside = (row_at >= 0) & (row_at < subtiles * row_count)
    spread = [
        jnp.concatenate([halo(from_above, visit), var_ref[visit], halo(from_below, visit)], axis=0)
        for visit in range(visits)
    ]
    shared = jnp.full((high_rows, col_count), SKY_VAR, F32)
    for visit in range(visits):
        shared = shared + spread[visit] * (1.0 / (visits * visits))
    inverse = [jnp.where(inside, 1.0 / (spread[visit] + shared), 0.0) for visit in range(visits)]

    def detected(images, kind):
        filtered = mul3(split(jnp.concatenate(images, axis=0)), (filter_ref[kind], filter_ref[kind + 1]))
        pair = split(filtered)
        rows = (edge_ref[kind, :, :high_rows], edge_ref[kind + 1, :, :high_rows])
        return [
            mul3(rows, (pair[0][v * high_rows : (v + 1) * high_rows], pair[1][v * high_rows : (v + 1) * high_rows]))
            for v in range(visits)
        ]

    for copy in copies[:3]:
        copy.wait()
    noise = detected(inverse, 2)

    lane = lax.broadcasted_iota(jnp.int32, (SLOTS, 2 * HALF), 1)
    line = lax.broadcasted_iota(jnp.int32, (SLOTS, 2 * HALF), 0)
    systems = []
    for pair in range(visits // 2):
        total = grams[0][pair * SLOTS : (pair + 1) * SLOTS]
        for ref in grams[1:]:
            total = total + ref[pair * SLOTS : (pair + 1) * SLOTS]
        diagonal = (lane == line) | (lane == line + HALF)
        systems.append(total + jnp.where(diagonal, RIDGE * total + RIDGE * EPS * normalizer, 0.0))
    for slot in LIVE_SLOTS:
        place = jnp.where(lane < HALF, slot, HALF + slot)
        for pair in range(visits // 2):
            matrix = systems[pair]
            column = jnp.take_along_axis(matrix, place, axis=1)
            row = matrix[slot : slot + 1] / column[slot : slot + 1]
            systems[pair] = jnp.where(line == slot, row, matrix - column * row)
    for copy in copies[3:]:
        copy.wait()
    left = []
    offsets = []
    half_lane = lax.broadcasted_iota(jnp.int32, (BLOCK, 2 * HALF), 1) < HALF
    for pair in range(visits // 2):
        wanted = SCI_SLOT + 2 * pair
        place = jnp.where(lane < HALF, wanted, HALF + wanted + 1)
        solved = jnp.take_along_axis(systems[pair], place, axis=1)
        mixes = [None] * TAP_COUNT
        for slot, (row_tap, col_tap) in SLOT_TAPS.items():
            term = solved[slot : slot + 1] * doubled_ref[row_tap]
            mixes[col_tap] = term if mixes[col_tap] is None else mixes[col_tap] + term
        own, other = [], []
        for tap in range(0, TAP_COUNT, 2):
            own.append(jnp.where(half_lane, mixes[tap], pltpu.roll(mixes[tap + 1], HALF, 1)))
            other.append(jnp.where(half_lane, pltpu.roll(mixes[tap], HALF, 1), mixes[tap + 1]))
        left += [jnp.concatenate(own, axis=1), jnp.concatenate(other, axis=1)]
        tail = solved[ONE_SLOT // 8 * 8 : ONE_SLOT // 8 * 8 + 8]
        for begin in (0, HALF):
            flat = jnp.take_along_axis(tail, jnp.full((8, LANES), begin, jnp.int32), axis=1)
            flat = flat[ONE_SLOT % 8 : ONE_SLOT % 8 + 1]
            offsets.append(jnp.concatenate([flat] * parts, axis=1))
    left = split(jnp.concatenate(left, axis=0))
    models = []
    for block in range(high_rows // BLOCK):
        start = block * BLOCK
        stack = tuple(
            jnp.concatenate([ref[tap, start : start + WINDOW] for tap in range(TAP_COUNT)], axis=0)
            for ref in (high_ref, low_ref)
        )
        models.append(mul3(left, stack))
    weighted = []
    for visit in range(visits):
        model = jnp.concatenate([part[visit * BLOCK : (visit + 1) * BLOCK] for part in models], axis=0)
        difference = wide_ref[visit] - model - offsets[visit]
        diff_ref[visit, 0] = difference[EDGE : EDGE + row_count]
        weighted.append(difference * inverse[visit])
    signal = detected(weighted, 0)
    for visit in range(visits):
        sig_ref[visit, 0] = signal[visit] * lax.rsqrt(noise[visit])


def vmem():
    return pl.BlockSpec(memory_space=pltpu.VMEM)


def smem():
    return pl.BlockSpec(memory_space=pltpu.SMEM)


def far():
    return pl.BlockSpec(memory_space=pltpu.HBM)


def in_hbm(array):
    return pltpu.with_memory_space_constraint(jnp.asarray(array), pltpu.HBM)


def call(kernel, outs, out_specs, in_specs, scratch):
    return pl.pallas_call(
        kernel,
        out_shape=outs,
        in_specs=in_specs,
        out_specs=out_specs,
        scratch_shapes=scratch,
        compiler_params=pltpu.CompilerParams(vmem_limit_bytes=VMEM_BYTES),
    )


def local(
    pieces_image,
    pieces_variance,
    piece_patch,
    piece_cell,
    stamp_row,
    stamp_col,
    stamp_count,
    warp_offsets,
):
    patches = lax.axis_size("patch")
    subtiles = lax.axis_size("sub")
    _, pieces, cell_rows, col_count = pieces_image.shape
    visits = warp_offsets.shape[0]
    row_count = cell_rows * NCELL
    slots = stamp_row.shape[1]
    capacity = max(2, 2 * pieces // patches)
    direct = patches <= 8
    units = 2 * capacity
    sds = jax.ShapeDtypeStruct
    design_fixed, filters, edges, doubled = constants(visits, row_count, col_count)

    image_blocks = var_blocks = 1

    def sent(blocks, depth):
        return [sds((1 if blocks > 1 else patches, depth, 8, LANES), F32)] * blocks

    *images, stamps, warps, chosen = call(
        functools.partial(pack_kernel, (patches, capacity, pieces, image_blocks, slots)),
        sent(image_blocks, units + 1)
        + [sds((8, LANES), F32), sds((visits,), jnp.int32), sds((patches * capacity,), jnp.int32)],
        [vmem()] * (image_blocks + 1) + [smem()] * 2,
        [far()] * 7,
        [
            pltpu.VMEM((-(-patches // 8) * 8, LANES), F32),
            pltpu.SMEM((patches,), jnp.int32),
            pltpu.SMEM((1, pieces), jnp.int32),
            pltpu.SMEM((1, pieces), jnp.int32),
            pltpu.VMEM((1, slots), jnp.int32),
            pltpu.VMEM((1, slots), jnp.int32),
            pltpu.SMEM((1, 1), jnp.int32),
            pltpu.VMEM(pieces_image.shape, F32),
            pltpu.SemaphoreType.DMA((7,)),
        ],
    )(
        in_hbm(piece_patch[:, :, 0]),
        in_hbm(piece_cell),
        in_hbm(stamp_row),
        in_hbm(stamp_col),
        stamp_count,
        in_hbm(pieces_image),
        in_hbm(warp_offsets),
    )

    def route(blocks, order):
        if len(blocks) == 1:
            return [lax.all_to_all(blocks[0], "patch", split_axis=0, concat_axis=0, tiled=True)]
        result = [blocks[0]] * patches
        for away in order:
            result[away] = lax.ppermute(blocks[away], "patch", [(i, i ^ away) for i in range(patches)])
        return result

    got = route(images, list(range(patches - 1, 0, -1)))
    variances = call(
        functools.partial(pack_more_kernel, (patches, capacity, var_blocks)),
        sent(var_blocks, units),
        [vmem()] * var_blocks,
        [smem(), far()],
        [pltpu.VMEM(pieces_image.shape, F32), pltpu.SemaphoreType.DMA((1,))],
    )(chosen, in_hbm(pieces_variance))
    got_var = route(variances, range(1, patches))

    side = sds((visits * HALO + 8, col_count), F32)
    science, up, down, cells = call(
        functools.partial(image_kernel, (patches, capacity, visits, row_count, col_count, image_blocks)),
        [sds((visits, row_count, col_count), F32), side, side, sds((patches * capacity,), jnp.int32)],
        [vmem(), vmem(), vmem(), smem()],
        [smem()] + [vmem()] * (1 + image_blocks),
        [
            pltpu.VMEM((visits * NCELL + 1, 2, 8, LANES), F32),
            pltpu.SMEM((patches, LANES), F32),
            pltpu.SemaphoreType.DMA((patches,)),
        ],
    )(warps, stamps, *got)
    above = lax.ppermute(down, "sub", [(i, i + 1) for i in range(subtiles - 1)])
    below = lax.ppermute(up, "sub", [(i + 1, i) for i in range(subtiles - 1)])

    field = sds((TAP_COUNT, row_count + 2 * BLOCK, col_count), BF16)
    own_field = sds((TAP_COUNT, row_count, col_count), BF16)
    plane = sds((row_count, col_count), F32)
    wide = sds((visits, row_count + 2 * EDGE, col_count), F32)
    held, own_high, own_low, hits = call(
        functools.partial(own_kernel, (visits, row_count, col_count)),
        [sds(design_fixed.shape, BF16), own_field, own_field, plane],
        [vmem()] * 4,
        [vmem(), vmem(), far()],
        [pltpu.SemaphoreType.DMA((design_fixed.shape[0],))],
    )(science, stamps, in_hbm(design_fixed))
    design, mask, high, low, wide_science = call(
        functools.partial(design_kernel, (visits, row_count, col_count)),
        [sds((row_count, SLOTS, col_count), F32), plane] + [pltpu.HBM(part.shape, part.dtype) for part in (field, field, wide)],
        [vmem()] * 2 + [far()] * 3,
        [vmem()] * 7,
        [pltpu.VMEM(part.shape, part.dtype) for part in (field, field, wide)] + [pltpu.SemaphoreType.DMA((3,))],
    )(science, above, below, held, own_high, own_low, hits)

    gram_rows = visits // 2 * SLOTS
    tail_rows = visits * EDGE * (col_count // LANES)
    step = 32
    variance, to_below, to_above, gram = call(
        functools.partial(gram_kernel, (patches, capacity, visits, row_count, col_count, var_blocks, step)),
        [
            sds((visits, row_count, col_count), F32),
            sds((gram_rows + tail_rows, LANES), F32),
            sds((gram_rows + tail_rows, LANES), F32),
            sds((gram_rows, LANES), F32),
        ],
        [vmem()] * 4,
        [smem(), smem(), vmem(), vmem()] + [vmem()] * var_blocks,
        [
            pltpu.VMEM((visits * NCELL + 1, 2, 8, LANES), F32),
            pltpu.VMEM((visits, row_count, col_count), F32),
            pltpu.VMEM((2 * visits * SLOTS, 2 * HALF), F32),
        ],
    )(warps, cells, mask, design, *got_var)
    grams = [gram]
    for shift in range(1, subtiles):
        sent = to_below if shift == 1 else to_above if shift == subtiles - 1 else gram
        grams.append(lax.ppermute(sent, "sub", [(i, (i + shift) % subtiles) for i in range(subtiles)]))

    normalizer = subtiles * slots * (2 * SH + 1) ** 2
    result = sds((visits, 1, row_count, col_count), F32)
    kept = [filters, edges, doubled, wide_science, high, low]
    return call(
        functools.partial(solve_kernel, (visits, row_count, col_count, subtiles, float(normalizer), len(grams))),
        [result, result],
        [vmem(), vmem()],
        [vmem()] * (1 + len(grams)) + [far()] * len(kept),
        [pltpu.VMEM(part.shape, part.dtype) for part in kept] + [pltpu.SemaphoreType.DMA((len(kept),))],
    )(variance, *grams, *[in_hbm(part) for part in kept])


def solution(mesh):
    in_specs = (
        P("sub", "patch", None, None),
        P("sub", "patch", None, None),
        P("sub", "patch", None),
        P("sub", "patch"),
        P("patch", "sub"),
        P("patch", "sub"),
        P("patch", "sub"),
        P(),
    )
    out_specs = (P(None, "patch", "sub", None), P(None, "patch", "sub", None))
    return jax.shard_map(local, mesh=mesh, in_specs=in_specs, out_specs=out_specs, check_vma=False)
```

profile of v0, /device:TPU:0, one launch (start us, length us, event | category | flops | bytes accessed | tf_op | source)
XLA Modules:
  0.0 64.1 jit_solution(8535328467011446338)
XLA Ops:
  1.3 1.9 %shard_map.131 = (f32[8,17,8,128]{3,2,1,0:T(8,128)}, f32[8,128]{1,0:T(8,128)S(1)}, s32[4]{0:T(128)S(1)}, s32[64]{0:T(128)S(1)}) custom-call(s32[1,32]{1,0:T(1,128)} %bitcast.1, s32[1,32]{1,0:T(1,128)} %refs_1_.1, s32[1,12]{1,0:T(1,128)} %refs_2_.1, s32[1,12]{1,0:T(1,128)} %refs_3_.1, s32[1,1]{1,0:T(1,128)S(6)} %copy.14.refs_4_, f32[1,32,8,256]{3,2,1,0:T(8,128)} %refs_5_.2, ...), custom_call_target="tpu_custom_call" | custom-call | tf_op jit(solution)/shard_map/pallas_call | solution.py:561
  3.2 7.3 %all-to-all-start = ((f32[8,17,8,128]{3,2,1,0:T(8,128)}), f32[8,17,8,128]{3,2,1,0:T(8,128)S(1)}, u32[]{:S(2)}, u32[]{:S(2)}) async-start(f32[8,17,8,128]{3,2,1,0:T(8,128)} %get-tuple-element.25), calls=%async_computation | async-start | bytes 1114112 | tf_op jit(solution)/shard_map/all_to_all | solution.py:590
  10.5 2.4 %shard_map.135 = f32[8,16,8,128]{3,2,1,0:T(8,128)} custom-call(s32[64]{0:T(128)S(1)} %get-tuple-element.36.chosen_ref, f32[1,32,8,256]{3,2,1,0:T(8,128)} %var_hbm.1), custom_call_target="tpu_custom_call" | custom-call | tf_op jit(solution)/shard_map/pallas_call | solution.py:597
  12.9 12.8 %all-to-all-done.refs_0_ = f32[8,17,8,128]{3,2,1,0:T(8,128)S(1)} async-done(((f32[8,17,8,128]{3,2,1,0:T(8,128)}), f32[8,17,8,128]{3,2,1,0:T(8,128)S(1)}, u32[]{:S(2)}, u32[]{:S(2)}) %all-to-all-start) | async-done | bytes 557088 | tf_op jit(solution)/shard_map/all_to_all | solution.py:590
  25.7 4.1 %all-to-all-start.1 = ((f32[8,16,8,128]{3,2,1,0:T(8,128)}), f32[8,16,8,128]{3,2,1,0:T(8,128)}, u32[]{:S(2)}, u32[]{:S(2)}) async-start(f32[8,16,8,128]{3,2,1,0:T(8,128)} %shard_map.135), calls=%async_computation.1 | async-start | bytes 1048576 | tf_op jit(solution)/shard_map/all_to_all | solution.py:590
  29.9 2.2 %shard_map.132 = (f32[4,64,256]{2,1,0:T(8,128)S(1)}, f32[104,256]{1,0:T(8,128)S(1)}, f32[104,256]{1,0:T(8,128)S(1)}, s32[64]{0:T(128)S(1)}) custom-call(s32[4]{0:T(128)S(1)} %get-tuple-element.23.warp_ref, f32[8,128]{1,0:T(8,128)S(1)} %get-tuple-element.24.stamp_ref, f32[8,17,8,128]{3,2,1,0:T(8,128)S(1)} %all-to-all-done.refs_0_), custom_call_target="tpu_custom_call" | custom-call | tf_op jit(solution)/shard_map/pallas_call | solution.py:607
  32.1 1.3 %collective-permute-start = (f32[104,256]{1,0:T(8,128)S(1)}, f32[104,256]{1,0:T(8,128)S(1)}, u32[]{:S(2)}, u32[]{:S(2)}) collective-permute-start(f32[104,256]{1,0:T(8,128)S(1)} %get-tuple-element.28), channel_id=1, source_target_pairs={{0,1},{1,2},{2,3},{4,5},{5,6},{6,7},{8,9},{9,10},{10,11},{12,13},{... | collective-permute-start | bytes 319496 | tf_op jit(solution)/shard_map/ppermute | solution.py:618
  33.4 1.3 %collective-permute-start.1 = (f32[104,256]{1,0:T(8,128)S(1)}, f32[104,256]{1,0:T(8,128)S(1)}, u32[]{:S(2)}, u32[]{:S(2)}) collective-permute-start(f32[104,256]{1,0:T(8,128)S(1)} %get-tuple-element.29), channel_id=1, source_target_pairs={{1,0},{2,1},{3,2},{5,4},{6,5},{7,6},{9,8},{10,9},{11,10},{13,12},{... | collective-permute-start | bytes 319496 | tf_op jit(solution)/shard_map/ppermute | solution.py:619
  34.7 4.0 %shard_map.133 = (bf16[20,2,256,256]{3,2,1,0:T(8,128)(2,1)S(1)}, bf16[14,64,256]{2,1,0:T(8,128)(2,1)S(1)}, bf16[14,64,256]{2,1,0:T(8,128)(2,1)S(1)}, f32[64,256]{1,0:T(8,128)S(1)}) custom-call(f32[4,64,256]{2,1,0:T(8,128)S(1)} %get-tuple-element.27.sci_ref, f32[8,128]{1,0:T(8,128)S(1)} %get-tuple-element.24.stamp_ref, ...), custom_call_target="tpu_custom_call" | custom-call | tf_op jit(solution)/shard_map/pallas_call | solution.py:625
  38.7 0.0 collective-permute-done.above_ref
  38.7 0.0 collective-permute-done.1.below_ref
  38.7 3.3 %shard_map.134 = (f32[64,48,256]{2,1,0:T(8,128)S(1)}, f32[64,256]{1,0:T(8,128)S(1)}, bf16[14,128,256]{2,1,0:T(8,128)(2,1)}, bf16[14,128,256]{2,1,0:T(8,128)(2,1)}, f32[4,96,256]{2,1,0:T(8,128)}) custom-call(f32[4,64,256]{2,1,0:T(8,128)S(1)} %get-tuple-element.27.sci_ref, f32[104,256]{1,0:T(8,128)S(1)} %collective-permute-done.above_ref, ...), custom_call_target="tpu_custom_call" | custom-call | tf_op jit(solution)/shard_map/pallas_call | solution.py:632
  42.0 2.2 %all-to-all-done.1.refs_0_ = f32[8,16,8,128]{3,2,1,0:T(8,128)} async-done(((f32[8,16,8,128]{3,2,1,0:T(8,128)}), f32[8,16,8,128]{3,2,1,0:T(8,128)}, u32[]{:S(2)}, u32[]{:S(2)}) %all-to-all-start.1) | async-done | bytes 524320 | tf_op jit(solution)/shard_map/all_to_all | solution.py:590
  44.1 5.3 %shard_map.136 = (f32[4,64,256]{2,1,0:T(8,128)S(1)}, f32[224,128]{1,0:T(8,128)S(1)}, f32[224,128]{1,0:T(8,128)S(1)}, f32[96,128]{1,0:T(8,128)S(1)}) custom-call(s32[4]{0:T(128)S(1)} %get-tuple-element.23.warp_ref, s32[64]{0:T(128)S(1)} %get-tuple-element.26.cells_ref, f32[64,256]{1,0:T(8,128)S(1)} %get-tuple-element.34.mask_ref, ...), custom_call_target="tpu_custom_call" | custom-call | tf_op jit(solution)/shard_map/pallas_call | solution.py:643
  49.5 1.2 %collective-permute-start.2 = (f32[224,128]{1,0:T(8,128)S(1)}, f32[224,128]{1,0:T(8,128)S(1)}, u32[]{:S(2)}, u32[]{:S(2)}) collective-permute-start(f32[224,128]{1,0:T(8,128)S(1)} %get-tuple-element.39), channel_id=1, source_target_pairs={{0,1},{1,2},{2,3},{3,0},{4,5},{5,6},{6,7},{7,4},{8,9},{9,10},{10,1... | collective-permute-start | bytes 344072 | tf_op jit(solution)/shard_map/ppermute | solution.py:662
  50.7 0.6 collective-permute-start.4
  51.3 2.3 %collective-permute-start.3 = (f32[96,128]{1,0:T(8,128)S(1)}, f32[96,128]{1,0:T(8,128)S(1)}, u32[]{:S(2)}, u32[]{:S(2)}) collective-permute-start(f32[96,128]{1,0:T(8,128)S(1)} %get-tuple-element.38.refs_0_), channel_id=1, source_target_pairs={{0,2},{1,3},{2,0},{3,1},{4,6},{5,7},{6,4},{7,5},{8,10},{9,11},{10,... | collective-permute-start | bytes 147464 | tf_op jit(solution)/shard_map/ppermute | solution.py:662
  53.6 3.3 %collective-permute-done.3.refs_2_ = f32[96,128]{1,0:T(8,128)S(1)} collective-permute-done((f32[96,128]{1,0:T(8,128)S(1)}, f32[96,128]{1,0:T(8,128)S(1)}, u32[]{:S(2)}, u32[]{:S(2)}) %collective-permute-start.3) | collective-permute-done | bytes 49184 | tf_op jit(solution)/shard_map/ppermute | solution.py:662
  56.9 0.0 collective-permute-done.2.refs_1_
  56.9 0.0 collective-permute-done.4.refs_3_
  56.9 7.2 %shard_map.137 = (f32[4,1,64,256]{3,2,1,0:T(8,128)}, f32[4,1,64,256]{3,2,1,0:T(8,128)}) custom-call(f32[4,64,256]{2,1,0:T(8,128)S(1)} %get-tuple-element.37.var_ref, f32[96,128]{1,0:T(8,128)S(1)} %get-tuple-element.38.refs_0_, f32[224,128]{1,0:T(8,128)S(1)} %collective-permute-done.2.refs_1_, f32[96,128]{1,0:T(8,128)S(1)} %collective-permute-done.3.refs_2_, ...), custom_call_target="tpu_custom_call" | custom-call | tf_op jit(solution)/shard_map/pallas_call | solution.py:667
Async XLA Ops:
  3.2 22.5 %all-to-all-start = ((f32[8,17,8,128]{3,2,1,0:T(8,128)}), f32[8,17,8,128]{3,2,1,0:T(8,128)S(1)}, u32[]{:S(2)}, u32[]{:S(2)}) async-start(f32[8,17,8,128]{3,2,1,0:T(8,128)} %get-tuple-element.25), calls=%async_computation | async-start | bytes 1114112 | tf_op jit(solution)/shard_map/all_to_all | solution.py:590
  25.7 18.5 %all-to-all-start.1 = ((f32[8,16,8,128]{3,2,1,0:T(8,128)}), f32[8,16,8,128]{3,2,1,0:T(8,128)}, u32[]{:S(2)}, u32[]{:S(2)}) async-start(f32[8,16,8,128]{3,2,1,0:T(8,128)} %shard_map.135), calls=%async_computation.1 | async-start | bytes 1048576 | tf_op jit(solution)/shard_map/all_to_all | solution.py:590
  32.1 6.6 %collective-permute-start = (f32[104,256]{1,0:T(8,128)S(1)}, f32[104,256]{1,0:T(8,128)S(1)}, u32[]{:S(2)}, u32[]{:S(2)}) collective-permute-start(f32[104,256]{1,0:T(8,128)S(1)} %get-tuple-element.28), channel_id=1, source_target_pairs={{0,1},{1,2},{2,3},{4,5},{5,6},{6,7},{8,9},{9,10},{10,11},{12,13},{... | collective-permute-start | bytes 319496 | tf_op jit(solution)/shard_map/ppermute | solution.py:618
  33.4 5.3 %collective-permute-start.1 = (f32[104,256]{1,0:T(8,128)S(1)}, f32[104,256]{1,0:T(8,128)S(1)}, u32[]{:S(2)}, u32[]{:S(2)}) collective-permute-start(f32[104,256]{1,0:T(8,128)S(1)} %get-tuple-element.29), channel_id=1, source_target_pairs={{1,0},{2,1},{3,2},{5,4},{6,5},{7,6},{9,8},{10,9},{11,10},{13,12},{... | collective-permute-start | bytes 319496 | tf_op jit(solution)/shard_map/ppermute | solution.py:619
  49.5 7.4 %collective-permute-start.2 = (f32[224,128]{1,0:T(8,128)S(1)}, f32[224,128]{1,0:T(8,128)S(1)}, u32[]{:S(2)}, u32[]{:S(2)}) collective-permute-start(f32[224,128]{1,0:T(8,128)S(1)} %get-tuple-element.39), channel_id=1, source_target_pairs={{0,1},{1,2},{2,3},{3,0},{4,5},{5,6},{6,7},{7,4},{8,9},{9,10},{10,1... | collective-permute-start | bytes 344072 | tf_op jit(solution)/shard_map/ppermute | solution.py:662
  50.7 6.2 %collective-permute-start.4 = (f32[224,128]{1,0:T(8,128)S(1)}, f32[224,128]{1,0:T(8,128)S(1)}, u32[]{:S(2)}, u32[]{:S(2)}) collective-permute-start(f32[224,128]{1,0:T(8,128)S(1)} %get-tuple-element.40), channel_id=1, source_target_pairs={{0,3},{1,0},{2,1},{3,2},{4,7},{5,4},{6,5},{7,6},{8,11},{9,8},{10,9... | collective-permute-start | bytes 344072 | tf_op jit(solution)/shard_map/ppermute | solution.py:662
  51.3 5.6 %collective-permute-start.3 = (f32[96,128]{1,0:T(8,128)S(1)}, f32[96,128]{1,0:T(8,128)S(1)}, u32[]{:S(2)}, u32[]{:S(2)}) collective-permute-start(f32[96,128]{1,0:T(8,128)S(1)} %get-tuple-element.38.refs_0_), channel_id=1, source_target_pairs={{0,2},{1,3},{2,0},{3,1},{4,6},{5,7},{6,4},{7,5},{8,10},{9,11},{10,... | collective-permute-start | bytes 147464 | tf_op jit(solution)/shard_map/ppermute | solution.py:662
where the time goes:
time: 64.6 us; the launch traced here: 64.1 us
  Pallas kernels  26.3 us (41%)
  waiting for transfers between devices  18.3 us (28%)
  starting transfers between devices  18.1 us (28%)
  between operations  1.37 us (2%)
    all_to_all x2, waiting for transfers between devices, route(): lax.all_to_all(blocks[0], 'patch', split_axis=0, concat_axis=0, tiled=True)  15 us
    all_to_all x2, starting transfers between devices, route(): lax.all_to_all(blocks[0], 'patch', split_axis=0, concat_axis=0, tiled=True)  11.4 us
    pallas_call x1, Pallas kernels, local(): call(functools.partial(solve_kernel, (visits, row_count, col_count, subti...  7.2 us
    pallas_call x1, Pallas kernels, local(): call(functools.partial(gram_kernel, (patches, capacity, visits, row_count...  5.35 us
    ppermute x3, starting transfers between devices, local(): lax.ppermute(sent, 'sub', [(i, (i + shift) % subtiles) for i in range(sub...  4.09 us
    pallas_call x1, Pallas kernels, local(): call(functools.partial(own_kernel, (visits, row_count, col_count)), [sds(...  4.01 us
    ppermute x3, waiting for transfers between devices, local(): lax.ppermute(sent, 'sub', [(i, (i + shift) % subtiles) for i in range(sub...  3.3 us
    pallas_call x1, Pallas kernels, local(): call(functools.partial(design_kernel, (visits, row_count, col_count)), [s...  3.26 us
  transfers between devices with their start and end apart: 7, of which 3 were waited for; matrix products, arithmetic and copies ran while one was open for 0% of the time, Pallas kernels for 18%

commit v1 on v0

--- a/solution.py
+++ b/solution.py
@@ -145,6 +145,11 @@
     return lax.dot_general(left, right, (((1,), (1,)), ((), ())), preferred_element_type=F32)
 
 
+def turn(patches):
+    near, far_half = list(range(1, patches // 2)), list(range(patches // 2, patches))
+    return [0, *near[:2], *far_half, *near[2:]]
+
+
 def fill(cfg, outs, source, chosen_ref, table_ref):
     patches, capacity = cfg
     me = lax.axis_index("patch")
@@ -152,7 +157,7 @@
         if len(outs) == 1:
             out, place, away = outs[0], block, block ^ me
         else:
-            out, place, away = outs[block], 0, block
+            out, place, away = outs[block], 0, turn(patches)[block]
         for rank in range(capacity):
             piece = chosen_ref[away * capacity + rank]
             out[place, 2 * rank] = source[0, piece, :, :LANES]
@@ -223,7 +228,7 @@
         if len(blocks) == 1:
             ref, place, away = blocks[0], block, block ^ me
         else:
-            ref, place, away = blocks[block], 0, block
+            ref, place, away = blocks[block], 0, turn(patches)[block]
         for rank in range(capacity):
             cell = cells_ref[away * capacity + rank]
             total_ref[cell, 0] += ref[place, 2 * rank]
@@ -259,7 +264,7 @@
     for copy in copies:
         copy.wait()
     for block in range(patches):
-        away = block ^ me if block_count == 1 else block
+        away = block ^ me if block_count == 1 else turn(patches)[block]
         for rank in range(capacity):
             cell = near_ref[block, rank].astype(jnp.int32)
             cells_ref[away * capacity + rank] = jnp.where(cell < 0, visits * NCELL, cell)
@@ -454,13 +459,32 @@
             total = total + ref[pair * SLOTS : (pair + 1) * SLOTS]
         diagonal = (lane == line) | (lane == line + HALF)
         systems.append(total + jnp.where(diagonal, RIDGE * total + RIDGE * EPS * normalizer, 0.0))
-    for slot in LIVE_SLOTS:
-        place = jnp.where(lane < HALF, slot, HALF + slot)
-        for pair in range(visits // 2):
-            matrix = systems[pair]
-            column = jnp.take_along_axis(matrix, place, axis=1)
-            row = matrix[slot : slot + 1] / column[slot : slot + 1]
-            systems[pair] = jnp.where(line == slot, row, matrix - column * row)
+    pairs = range(visits // 2)
+    tiles = [[matrix[8 * part : 8 * part + 8] for part in range(len(TILES))] for matrix in systems]
+    line, lane = line[:8], lane[:8]
+    for panel in range(len(TILES)):
+        slots = [slot for slot in LIVE_SLOTS if slot // 8 == panel]
+        place = {slot: jnp.where(lane < HALF, slot, HALF + slot) for slot in slots}
+        columns = [
+            {slot: [jnp.take_along_axis(tile, place[slot], axis=1) for tile in tiles[pair]] for slot in slots}
+            for pair in pairs
+        ]
+        for number, slot in enumerate(slots):
+            row = slot % 8
+            at_row = line == row
+            for pair in pairs:
+                column = columns[pair][slot]
+                scale = 1.0 / column[panel][row : row + 1]
+
+                def eliminate(parts):
+                    factor = parts[panel][row : row + 1] * scale
+                    done = [part - column[index] * factor for index, part in enumerate(parts)]
+                    done[panel] = jnp.where(at_row, factor, done[panel])
+                    return done
+
+                for later in slots[number + 1 :]:
+                    columns[pair][later] = eliminate(columns[pair][later])
+                tiles[pair] = eliminate(tiles[pair])
     for copy in copies[3:]:
         copy.wait()
     left = []
@@ -469,7 +493,7 @@
     for pair in range(visits // 2):
         wanted = SCI_SLOT + 2 * pair
         place = jnp.where(lane < HALF, wanted, HALF + wanted + 1)
-        solved = jnp.take_along_axis(systems[pair], place, axis=1)
+        solved = jnp.concatenate([jnp.take_along_axis(tile, place, axis=1) for tile in tiles[pair]], axis=0)
         mixes = [None] * TAP_COUNT
         for slot, (row_tap, col_tap) in SLOT_TAPS.items():
             term = solved[slot : slot + 1] * doubled_ref[row_tap]
@@ -531,6 +555,17 @@
     )
 
 
+def after(array, others):
+    return pl.pallas_call(
+        lambda *refs: None,
+        out_shape=[jax.ShapeDtypeStruct(array.shape, array.dtype)],
+        in_specs=[far()] * (1 + len(others)),
+        out_specs=[far()],
+        input_output_aliases={0: 0},
+        compiler_params=pltpu.CompilerParams(vmem_limit_bytes=1024 * 1024),
+    )(array, *others)
+
+
 def local(
     pieces_image,
     pieces_variance,
@@ -553,7 +588,8 @@
     sds = jax.ShapeDtypeStruct
     design_fixed, filters, edges, doubled = constants(visits, row_count, col_count)
 
-    image_blocks = var_blocks = 1
+    image_blocks = patches if direct else 1
+    var_blocks = 1
 
     def sent(blocks, depth):
         return [sds((1 if blocks > 1 else patches, depth, 8, LANES), F32)] * blocks
@@ -585,15 +621,15 @@
         in_hbm(warp_offsets),
     )
 
-    def route(blocks, order):
+    def route(blocks):
         if len(blocks) == 1:
             return [lax.all_to_all(blocks[0], "patch", split_axis=0, concat_axis=0, tiled=True)]
-        result = [blocks[0]] * patches
-        for away in order:
-            result[away] = lax.ppermute(blocks[away], "patch", [(i, i ^ away) for i in range(patches)])
+        result = list(blocks[:1])
+        for away, block in zip(turn(patches)[1:], blocks[1:]):
+            result.append(lax.ppermute(block, "patch", [(i, i ^ away) for i in range(patches)]))
         return result
 
-    got = route(images, list(range(patches - 1, 0, -1)))
+    got = route(images)
     variances = call(
         functools.partial(pack_more_kernel, (patches, capacity, var_blocks)),
         sent(var_blocks, units),
@@ -601,7 +637,9 @@
         [smem(), far()],
         [pltpu.VMEM(pieces_image.shape, F32), pltpu.SemaphoreType.DMA((1,))],
     )(chosen, in_hbm(pieces_variance))
-    got_var = route(variances, range(1, patches))
+    if direct:
+        variances = after(variances[0], got[1:])
+    got_var = route(variances)
 
     side = sds((visits * HALO + 8, col_count), F32)
     science, up, down, cells = call(

time: 64.6 us -> 58.5 us (0.906)
  waiting for transfers between devices: 18.3 us -> 8.31 us
  starting transfers between devices: 18.1 us -> 24.6 us
  Pallas kernels: 26.3 us -> 23.9 us
    all_to_all x2 -> x1, waiting for transfers between devices: 15 us -> 1.65 us  [route(): lax.all_to_all(blocks[0], 'patch', split_axis=0, concat_axis=0, tiled=True)]
    ppermute x0 -> x7, starting transfers between devices: none -> 12.3 us  [route(): lax.ppermute(block, 'patch', [(i, i ^ away) for i in range(patches)])]
    all_to_all x2 -> x1, starting transfers between devices: 11.4 us -> 5.07 us  [route(): lax.all_to_all(blocks[0], 'patch', split_axis=0, concat_axis=0, tiled=True)]
    ppermute x0 -> x7, waiting for transfers between devices: none -> 3.36 us  [route(): lax.ppermute(block, 'patch', [(i, i ^ away) for i in range(patches)])]
    pallas_call x1, Pallas kernels: 7.2 us -> 4.98 us  [local(): call(functools.partial(solve_kernel, (visits, row_count, col_count, subti...]
  transfers between devices with their start and end apart: 7 -> 13, of which waited for: 3 -> 6; matrix products, arithmetic and copies ran while one was open for 0% -> 0% of each run, Pallas kernels for 18% -> 20%
where the time goes in v1:
time: 58.5 us; the launch traced here: 58.2 us
  starting transfers between devices  24.6 us (42%)
  Pallas kernels  23.9 us (41%)
  waiting for transfers between devices  8.31 us (14%)
  between operations  1.37 us (2%)
    ppermute x7, starting transfers between devices, route(): lax.ppermute(block, 'patch', [(i, i ^ away) for i in range(patches)])  12.3 us
    pallas_call x1, Pallas kernels, local(): call(functools.partial(gram_kernel, (patches, capacity, visits, row_count...  5.33 us
    all_to_all x1, starting transfers between devices, route(): lax.all_to_all(blocks[0], 'patch', split_axis=0, concat_axis=0, tiled=True)  5.07 us
    pallas_call x1, Pallas kernels, local(): call(functools.partial(solve_kernel, (visits, row_count, col_count, subti...  4.98 us
    ppermute x3, starting transfers between devices, local(): lax.ppermute(sent, 'sub', [(i, (i + shift) % subtiles) for i in range(sub...  4.66 us
    pallas_call x1, Pallas kernels, local(): call(functools.partial(own_kernel, (visits, row_count, col_count)), [sds(...  4.01 us
    ppermute x7, waiting for transfers between devices, route(): lax.ppermute(block, 'patch', [(i, i ^ away) for i in range(patches)])  3.36 us
    ppermute x3, waiting for transfers between devices, local(): lax.ppermute(sent, 'sub', [(i, (i + shift) % subtiles) for i in range(sub...  3.3 us
  transfers between devices with their start and end apart: 13, of which 6 were waited for; matrix products, arithmetic and copies ran while one was open for 0% of the time, Pallas kernels for 20%

profile of v1, /device:TPU:0, one launch (start us, length us, event | category | flops | bytes accessed | tf_op | source)
XLA Modules:
  0.0 58.2 jit_solution(7387567841191767112)
XLA Ops:
  1.3 1.7 %shard_map.131 = (f32[1,17,8,128]{3,2,1,0:T(8,128)S(1)}, f32[1,17,8,128]{3,2,1,0:T(8,128)S(1)}, f32[1,17,8,128]{3,2,1,0:T(8,128)S(1)}, f32[1,17,8,128]{3,2,1,0:T...) custom-call(s32[1,32]{1,0:T(1,128)} %bitcast.1, ...), custom_call_target="tpu_custom_call" | custom-call | tf_op jit(solution)/shard_map/pallas_call | solution.py:597
  3.0 3.0 %collective-permute-start = (f32[1,17,8,128]{3,2,1,0:T(8,128)S(1)}, f32[1,17,8,128]{3,2,1,0:T(8,128)S(1)}, u32[]{:S(2)}, u32[]{:S(2)}) collective-permute-start(f32[1,17,8,128]{3,2,1,0:T(8,128)S(1)} %get-tuple-element.33), channel_id=1, source_target_pairs={{0,4},{4,0},{8,12},{12,8},{16,20},{20,16},{24,28},{28,24},{1,5},{5... | collective-permute-start | bytes 208904 | tf_op jit(solution)/shard_map/ppermute | solution.py:629
  6.0 1.6 %collective-permute-start.1 = (f32[1,17,8,128]{3,2,1,0:T(8,128)S(1)}, f32[1,17,8,128]{3,2,1,0:T(8,128)S(1)}, u32[]{:S(2)}, u32[]{:S(2)}) collective-permute-start(f32[1,17,8,128]{3,2,1,0:T(8,128)S(1)} %get-tuple-element.34), channel_id=1, source_target_pairs={{0,8},{4,12},{8,0},{12,4},{16,24},{20,28},{24,16},{28,20},{1,9},{5... | collective-permute-start | bytes 208904 | tf_op jit(solution)/shard_map/ppermute | solution.py:629
  7.6 2.6 %collective-permute-start.2 = (f32[1,17,8,128]{3,2,1,0:T(8,128)S(1)}, f32[1,17,8,128]{3,2,1,0:T(8,128)S(1)}, u32[]{:S(2)}, u32[]{:S(2)}) collective-permute-start(f32[1,17,8,128]{3,2,1,0:T(8,128)S(1)} %get-tuple-element.35), channel_id=1, source_target_pairs={{0,16},{4,20},{8,24},{12,28},{16,0},{20,4},{24,8},{28,12},{1,17},{... | collective-permute-start | bytes 208904 | tf_op jit(solution)/shard_map/ppermute | solution.py:629
  10.2 0.3 collective-permute-start.3
  10.5 2.5 %collective-permute-start.4 = (f32[1,17,8,128]{3,2,1,0:T(8,128)S(1)}, f32[1,17,8,128]{3,2,1,0:T(8,128)S(1)}, u32[]{:S(2)}, u32[]{:S(2)}) collective-permute-start(f32[1,17,8,128]{3,2,1,0:T(8,128)S(1)} %get-tuple-element.37), channel_id=1, source_target_pairs={{0,24},{4,28},{8,16},{12,20},{16,8},{20,12},{24,0},{28,4},{1,25},{... | collective-permute-start | bytes 208904 | tf_op jit(solution)/shard_map/ppermute | solution.py:629
  13.0 0.0 collective-permute-done.refs_1_
  13.0 2.3 %collective-permute-start.5 = (f32[1,17,8,128]{3,2,1,0:T(8,128)S(1)}, f32[1,17,8,128]{3,2,1,0:T(8,128)S(1)}, u32[]{:S(2)}, u32[]{:S(2)}) collective-permute-start(f32[1,17,8,128]{3,2,1,0:T(8,128)S(1)} %get-tuple-element.38), channel_id=1, source_target_pairs={{0,28},{4,24},{8,20},{12,16},{16,12},{20,8},{24,4},{28,0},{1,29},{... | collective-permute-start | bytes 208904 | tf_op jit(solution)/shard_map/ppermute | solution.py:629
  15.3 0.0 collective-permute-done.1.refs_2_
  15.3 0.0 collective-permute-start.6
  15.3 2.4 %shard_map.135.refs_0_ = f32[8,16,8,128]{3,2,1,0:T(8,128)} custom-call(s32[64]{0:T(128)S(1)} %get-tuple-element.50.chosen_ref, f32[1,32,8,256]{3,2,1,0:T(8,128)} %var_hbm.1), custom_call_target="tpu_custom_call" | custom-call | tf_op jit(solution)/shard_map/pallas_call | solution.py:633
  17.6 0.1 collective-permute-done.2.refs_3_
  17.7 1.5 %collective-permute-done.3.refs_4_ = f32[1,17,8,128]{3,2,1,0:T(8,128)S(1)} collective-permute-done((f32[1,17,8,128]{3,2,1,0:T(8,128)S(1)}, f32[1,17,8,128]{3,2,1,0:T(8,128)S(1)}, u32[]{:S(2)}, u32[]{:S(2)}) %collective-permute-start.3) | collective-permute-done | bytes 69664 | tf_op jit(solution)/shard_map/ppermute | solution.py:629
  19.2 0.0 collective-permute-done.4.refs_5_
  19.3 0.8 %collective-permute-done.5.refs_6_ = f32[1,17,8,128]{3,2,1,0:T(8,128)S(1)} collective-permute-done((f32[1,17,8,128]{3,2,1,0:T(8,128)S(1)}, f32[1,17,8,128]{3,2,1,0:T(8,128)S(1)}, u32[]{:S(2)}, u32[]{:S(2)}) %collective-permute-start.5) | collective-permute-done | bytes 69664 | tf_op jit(solution)/shard_map/ppermute | solution.py:629
  20.1 0.9 %collective-permute-done.6.refs_7_ = f32[1,17,8,128]{3,2,1,0:T(8,128)S(1)} collective-permute-done((f32[1,17,8,128]{3,2,1,0:T(8,128)S(1)}, f32[1,17,8,128]{3,2,1,0:T(8,128)S(1)}, u32[]{:S(2)}, u32[]{:S(2)}) %collective-permute-start.6) | collective-permute-done | bytes 69664 | tf_op jit(solution)/shard_map/ppermute | solution.py:629
  21.0 5.1 %all-to-all-start = ((f32[8,16,8,128]{3,2,1,0:T(8,128)}), f32[8,16,8,128]{3,2,1,0:T(8,128)}, u32[]{:S(2)}, u32[]{:S(2)}) async-start(f32[8,16,8,128]{3,2,1,0:T(8,128)} %shard_map.136), calls=%async_computation | async-start | bytes 1048576 | tf_op jit(solution)/shard_map/all_to_all | solution.py:626
  26.1 2.3 %shard_map.132 = (f32[4,64,256]{2,1,0:T(8,128)S(1)}, f32[104,256]{1,0:T(8,128)S(1)}, f32[104,256]{1,0:T(8,128)S(1)}, s32[64]{0:T(128)S(1)}) custom-call(s32[4]{0:T(128)S(1)} %get-tuple-element.30.warp_ref, f32[8,128]{1,0:T(8,128)S(1)} %get-tuple-element.31.stamp_ref, f32[1,17,8,128]{3,2,1,0:T(8,128)S(1)} %get-tuple-element.32.refs_0_, ...), custom_call_target="tpu_custom_call" | custom-call | tf_op jit(solution)/shard_map/pallas_call | solution.py:645
  28.3 1.3 %collective-permute-start.7 = (f32[104,256]{1,0:T(8,128)S(1)}, f32[104,256]{1,0:T(8,128)S(1)}, u32[]{:S(2)}, u32[]{:S(2)}) collective-permute-start(f32[104,256]{1,0:T(8,128)S(1)} %get-tuple-element.42), channel_id=1, source_target_pairs={{0,1},{1,2},{2,3},{4,5},{5,6},{6,7},{8,9},{9,10},{10,11},{12,13},{... | collective-permute-start | bytes 319496 | tf_op jit(solution)/shard_map/ppermute | solution.py:656
  29.7 1.3 %collective-permute-start.8 = (f32[104,256]{1,0:T(8,128)S(1)}, f32[104,256]{1,0:T(8,128)S(1)}, u32[]{:S(2)}, u32[]{:S(2)}) collective-permute-start(f32[104,256]{1,0:T(8,128)S(1)} %get-tuple-element.43), channel_id=1, source_target_pairs={{1,0},{2,1},{3,2},{5,4},{6,5},{7,6},{9,8},{10,9},{11,10},{13,12},{... | collective-permute-start | bytes 319496 | tf_op jit(solution)/shard_map/ppermute | solution.py:657
  31.0 4.0 %shard_map.133 = (bf16[20,2,256,256]{3,2,1,0:T(8,128)(2,1)S(1)}, bf16[14,64,256]{2,1,0:T(8,128)(2,1)S(1)}, bf16[14,64,256]{2,1,0:T(8,128)(2,1)S(1)}, f32[64,256]{1,0:T(8,128)S(1)}) custom-call(f32[4,64,256]{2,1,0:T(8,128)S(1)} %get-tuple-element.41.sci_ref, f32[8,128]{1,0:T(8,128)S(1)} %get-tuple-element.31.stamp_ref, ...), custom_call_target="tpu_custom_call" | custom-call | tf_op jit(solution)/shard_map/pallas_call | solution.py:663
  35.0 0.0 collective-permute-done.7.above_ref
  35.0 0.0 collective-permute-done.8.below_ref
  35.0 3.2 %shard_map.134 = (f32[64,48,256]{2,1,0:T(8,128)S(1)}, f32[64,256]{1,0:T(8,128)S(1)}, bf16[14,128,256]{2,1,0:T(8,128)(2,1)}, bf16[14,128,256]{2,1,0:T(8,128)(2,1)}, f32[4,96,256]{2,1,0:T(8,128)}) custom-call(f32[4,64,256]{2,1,0:T(8,128)S(1)} %get-tuple-element.41.sci_ref, f32[104,256]{1,0:T(8,128)S(1)} %collective-permute-done.7.above_ref, ...), custom_call_target="tpu_custom_call" | custom-call | tf_op jit(solution)/shard_map/pallas_call | solution.py:670
  38.2 1.6 %all-to-all-done.refs_0_ = f32[8,16,8,128]{3,2,1,0:T(8,128)} async-done(((f32[8,16,8,128]{3,2,1,0:T(8,128)}), f32[8,16,8,128]{3,2,1,0:T(8,128)}, u32[]{:S(2)}, u32[]{:S(2)}) %all-to-all-start) | async-done | bytes 524320 | tf_op jit(solution)/shard_map/all_to_all | solution.py:626
  39.9 5.3 %shard_map.137 = (f32[4,64,256]{2,1,0:T(8,128)S(1)}, f32[224,128]{1,0:T(8,128)S(1)}, f32[224,128]{1,0:T(8,128)S(1)}, f32[96,128]{1,0:T(8,128)S(1)}) custom-call(s32[4]{0:T(128)S(1)} %get-tuple-element.30.warp_ref, s32[64]{0:T(128)S(1)} %get-tuple-element.40.cells_ref, f32[64,256]{1,0:T(8,128)S(1)} %get-tuple-element.48.mask_ref, ...), custom_call_target="tpu_custom_call" | custom-call | tf_op jit(solution)/shard_map/pallas_call | solution.py:681
  45.2 1.7 %collective-permute-start.9 = (f32[224,128]{1,0:T(8,128)S(1)}, f32[224,128]{1,0:T(8,128)S(1)}, u32[]{:S(2)}, u32[]{:S(2)}) collective-permute-start(f32[224,128]{1,0:T(8,128)S(1)} %get-tuple-element.53), channel_id=1, source_target_pairs={{0,1},{1,2},{2,3},{3,0},{4,5},{5,6},{6,7},{7,4},{8,9},{9,10},{10,1... | collective-permute-start | bytes 344072 | tf_op jit(solution)/shard_map/ppermute | solution.py:700
  46.9 0.1 collective-permute-start.11
  47.0 2.9 %collective-permute-start.10 = (f32[96,128]{1,0:T(8,128)S(1)}, f32[96,128]{1,0:T(8,128)S(1)}, u32[]{:S(2)}, u32[]{:S(2)}) collective-permute-start(f32[96,128]{1,0:T(8,128)S(1)} %get-tuple-element.52.refs_0_), channel_id=1, source_target_pairs={{0,2},{1,3},{2,0},{3,1},{4,6},{5,7},{6,4},{7,5},{8,10},{9,11},{10,... | collective-permute-start | bytes 147464 | tf_op jit(solution)/shard_map/ppermute | solution.py:700
  49.9 3.3 %collective-permute-done.10.refs_2_ = f32[96,128]{1,0:T(8,128)S(1)} collective-permute-done((f32[96,128]{1,0:T(8,128)S(1)}, f32[96,128]{1,0:T(8,128)S(1)}, u32[]{:S(2)}, u32[]{:S(2)}) %collective-permute-start.10) | collective-permute-done | bytes 49184 | tf_op jit(solution)/shard_map/ppermute | solution.py:700
  53.2 0.0 collective-permute-done.11.refs_3_
  53.2 5.0 %shard_map.138 = (f32[4,1,64,256]{3,2,1,0:T(8,128)}, f32[4,1,64,256]{3,2,1,0:T(8,128)}) custom-call(f32[4,64,256]{2,1,0:T(8,128)S(1)} %get-tuple-element.51.var_ref, f32[96,128]{1,0:T(8,128)S(1)} %get-tuple-element.52.refs_0_, f32[224,128]{1,0:T(8,128)S(1)} %collective-permute-done.9.refs_1_, f32[96,128]{1,0:T(8,128)S(1)} %collective-permute-done.10.refs_2_, ...), custom_call_target="tpu_custom_call" | custom-call | tf_op jit(solution)/shard_map/pallas_call | solution.py:705
  (2 shorter events, 0.0 us)
Async XLA Ops:
  3.0 10.0 %collective-permute-start = (f32[1,17,8,128]{3,2,1,0:T(8,128)S(1)}, f32[1,17,8,128]{3,2,1,0:T(8,128)S(1)}, u32[]{:S(2)}, u32[]{:S(2)}) collective-permute-start(f32[1,17,8,128]{3,2,1,0:T(8,128)S(1)} %get-tuple-element.33), channel_id=1, source_target_pairs={{0,4},{4,0},{8,12},{12,8},{16,20},{20,16},{24,28},{28,24},{1,5},{5... | collective-permute-start | bytes 208904 | tf_op jit(solution)/shard_map/ppermute | solution.py:629
  6.0 9.2 %collective-permute-start.1 = (f32[1,17,8,128]{3,2,1,0:T(8,128)S(1)}, f32[1,17,8,128]{3,2,1,0:T(8,128)S(1)}, u32[]{:S(2)}, u32[]{:S(2)}) collective-permute-start(f32[1,17,8,128]{3,2,1,0:T(8,128)S(1)} %get-tuple-element.34), channel_id=1, source_target_pairs={{0,8},{4,12},{8,0},{12,4},{16,24},{20,28},{24,16},{28,20},{1,9},{5... | collective-permute-start | bytes 208904 | tf_op jit(solution)/shard_map/ppermute | solution.py:629
  7.6 10.1 %collective-permute-start.2 = (f32[1,17,8,128]{3,2,1,0:T(8,128)S(1)}, f32[1,17,8,128]{3,2,1,0:T(8,128)S(1)}, u32[]{:S(2)}, u32[]{:S(2)}) collective-permute-start(f32[1,17,8,128]{3,2,1,0:T(8,128)S(1)} %get-tuple-element.35), channel_id=1, source_target_pairs={{0,16},{4,20},{8,24},{12,28},{16,0},{20,4},{24,8},{28,12},{1,17},{... | collective-permute-start | bytes 208904 | tf_op jit(solution)/shard_map/ppermute | solution.py:629
  10.2 9.1 %collective-permute-start.3 = (f32[1,17,8,128]{3,2,1,0:T(8,128)S(1)}, f32[1,17,8,128]{3,2,1,0:T(8,128)S(1)}, u32[]{:S(2)}, u32[]{:S(2)}) collective-permute-start(f32[1,17,8,128]{3,2,1,0:T(8,128)S(1)} %get-tuple-element.36), channel_id=1, source_target_pairs={{0,20},{4,16},{8,28},{12,24},{16,4},{20,0},{24,12},{28,8},{1,21},{... | collective-permute-start | bytes 208904 | tf_op jit(solution)/shard_map/ppermute | solution.py:629
  10.5 8.8 %collective-permute-start.4 = (f32[1,17,8,128]{3,2,1,0:T(8,128)S(1)}, f32[1,17,8,128]{3,2,1,0:T(8,128)S(1)}, u32[]{:S(2)}, u32[]{:S(2)}) collective-permute-start(f32[1,17,8,128]{3,2,1,0:T(8,128)S(1)} %get-tuple-element.37), channel_id=1, source_target_pairs={{0,24},{4,28},{8,16},{12,20},{16,8},{20,12},{24,0},{28,4},{1,25},{... | collective-permute-start | bytes 208904 | tf_op jit(solution)/shard_map/ppermute | solution.py:629
  13.0 7.1 %collective-permute-start.5 = (f32[1,17,8,128]{3,2,1,0:T(8,128)S(1)}, f32[1,17,8,128]{3,2,1,0:T(8,128)S(1)}, u32[]{:S(2)}, u32[]{:S(2)}) collective-permute-start(f32[1,17,8,128]{3,2,1,0:T(8,128)S(1)} %get-tuple-element.38), channel_id=1, source_target_pairs={{0,28},{4,24},{8,20},{12,16},{16,12},{20,8},{24,4},{28,0},{1,29},{... | collective-permute-start | bytes 208904 | tf_op jit(solution)/shard_map/ppermute | solution.py:629
  15.3 5.7 %collective-permute-start.6 = (f32[1,17,8,128]{3,2,1,0:T(8,128)S(1)}, f32[1,17,8,128]{3,2,1,0:T(8,128)S(1)}, u32[]{:S(2)}, u32[]{:S(2)}) collective-permute-start(f32[1,17,8,128]{3,2,1,0:T(8,128)S(1)} %get-tuple-element.39), channel_id=1, source_target_pairs={{0,12},{4,8},{8,4},{12,0},{16,28},{20,24},{24,20},{28,16},{1,13},{... | collective-permute-start | bytes 208904 | tf_op jit(solution)/shard_map/ppermute | solution.py:629
  21.0 18.9 %all-to-all-start = ((f32[8,16,8,128]{3,2,1,0:T(8,128)}), f32[8,16,8,128]{3,2,1,0:T(8,128)}, u32[]{:S(2)}, u32[]{:S(2)}) async-start(f32[8,16,8,128]{3,2,1,0:T(8,128)} %shard_map.136), calls=%async_computation | async-start | bytes 1048576 | tf_op jit(solution)/shard_map/all_to_all | solution.py:626
  28.3 6.6 %collective-permute-start.7 = (f32[104,256]{1,0:T(8,128)S(1)}, f32[104,256]{1,0:T(8,128)S(1)}, u32[]{:S(2)}, u32[]{:S(2)}) collective-permute-start(f32[104,256]{1,0:T(8,128)S(1)} %get-tuple-element.42), channel_id=1, source_target_pairs={{0,1},{1,2},{2,3},{4,5},{5,6},{6,7},{8,9},{9,10},{10,11},{12,13},{... | collective-permute-start | bytes 319496 | tf_op jit(solution)/shard_map/ppermute | solution.py:656
  29.7 5.3 %collective-permute-start.8 = (f32[104,256]{1,0:T(8,128)S(1)}, f32[104,256]{1,0:T(8,128)S(1)}, u32[]{:S(2)}, u32[]{:S(2)}) collective-permute-start(f32[104,256]{1,0:T(8,128)S(1)} %get-tuple-element.43), channel_id=1, source_target_pairs={{1,0},{2,1},{3,2},{5,4},{6,5},{7,6},{9,8},{10,9},{11,10},{13,12},{... | collective-permute-start | bytes 319496 | tf_op jit(solution)/shard_map/ppermute | solution.py:657
  45.2 8.0 %collective-permute-start.9 = (f32[224,128]{1,0:T(8,128)S(1)}, f32[224,128]{1,0:T(8,128)S(1)}, u32[]{:S(2)}, u32[]{:S(2)}) collective-permute-start(f32[224,128]{1,0:T(8,128)S(1)} %get-tuple-element.53), channel_id=1, source_target_pairs={{0,1},{1,2},{2,3},{3,0},{4,5},{5,6},{6,7},{7,4},{8,9},{9,10},{10,1... | collective-permute-start | bytes 344072 | tf_op jit(solution)/shard_map/ppermute | solution.py:700
  46.9 6.3 %collective-permute-start.11 = (f32[224,128]{1,0:T(8,128)S(1)}, f32[224,128]{1,0:T(8,128)S(1)}, u32[]{:S(2)}, u32[]{:S(2)}) collective-permute-start(f32[224,128]{1,0:T(8,128)S(1)} %get-tuple-element.54), channel_id=1, source_target_pairs={{0,3},{1,0},{2,1},{3,2},{4,7},{5,4},{6,5},{7,6},{8,11},{9,8},{10,9... | collective-permute-start | bytes 344072 | tf_op jit(solution)/shard_map/ppermute | solution.py:700
  47.0 6.2 %collective-permute-start.10 = (f32[96,128]{1,0:T(8,128)S(1)}, f32[96,128]{1,0:T(8,128)S(1)}, u32[]{:S(2)}, u32[]{:S(2)}) collective-permute-start(f32[96,128]{1,0:T(8,128)S(1)} %get-tuple-element.52.refs_0_), channel_id=1, source_target_pairs={{0,2},{1,3},{2,0},{3,1},{4,6},{5,7},{6,4},{7,5},{8,10},{9,11},{10,... | collective-permute-start | bytes 147464 | tf_op jit(solution)/shard_map/ppermute | solution.py:700

commit v2 on v1

--- a/solution.py
+++ b/solution.py
@@ -249,8 +249,9 @@
 def image_kernel(cfg, warp_ref, stamp_ref, *refs):
     patches, capacity, visits, row_count, col_count, block_count = cfg
     blocks = refs[:block_count]
-    sci_ref, up_ref, down_ref, cells_ref, total_ref, near_ref, sems = refs[block_count:]
+    sci_ref, near_out, far_out, cells_ref, total_ref, near_ref, sems = refs[block_count:]
     me = lax.axis_index("patch")
+    odd = lax.axis_index("sub") % 2 == 1
     copies = []
     for block in range(patches):
         ref, place = (blocks[0], block) if block_count == 1 else (blocks[block], 0)
@@ -272,10 +273,11 @@
     for visit in range(visits):
         plane = warped(total_ref, visit, warp_ref, row_count, col_count)
         sci_ref[visit] = plane
-        up_ref[visit * HALO : (visit + 1) * HALO] = plane[:HALO]
-        down_ref[visit * HALO : (visit + 1) * HALO] = plane[row_count - HALO :]
+        top, bottom = plane[:HALO], plane[row_count - HALO :]
+        near_out[visit * HALO : (visit + 1) * HALO] = jnp.where(odd, top, bottom)
+        far_out[visit * HALO : (visit + 1) * HALO] = jnp.where(odd, bottom, top)
     first = visits * HALO
-    for ref in (up_ref, down_ref):
+    for ref in (near_out, far_out):
         ref[first : first + 8, :LANES] = stamp_ref[...]
         ref[first : first + 8, LANES:] = jnp.zeros((8, col_count - LANES), F32)
 
@@ -309,14 +311,19 @@
         copy.wait()
 
 
-def design_kernel(cfg, sci_ref, above_ref, below_ref, held_ref, own_high, own_low, hits_ref, *refs):
+def design_kernel(cfg, sci_ref, far_ref, near_ref, held_ref, own_high, own_low, hits_ref, *refs):
     visits, row_count, col_count = cfg
     design_ref, mask_ref, high_out, low_out, wide_out, high_ref, low_ref, wide_ref, sems = refs
-    above = above_ref[0:HALO]
-    below = below_ref[0:HALO]
+    odd = lax.axis_index("sub") % 2 == 1
+
+    def beside(first, count, lanes=slice(None)):
+        near, far = near_ref[first : first + count, lanes], far_ref[first : first + count, lanes]
+        return jnp.where(odd, near, far), jnp.where(odd, far, near)
+
+    above, below = beside(0, HALO)
     for visit in range(1, visits):
-        above = above + above_ref[visit * HALO : (visit + 1) * HALO]
-        below = below + below_ref[visit * HALO : (visit + 1) * HALO]
+        more = beside(visit * HALO, HALO)
+        above, below = above + more[0], below + more[1]
     rim = jnp.zeros((BLOCK - HALO, col_count), F32)
     template = split(jnp.concatenate([rim, above, below, rim], axis=0) * (1.0 / visits))
     for tap in range(TAP_COUNT):
@@ -326,9 +333,9 @@
             ref[tap, BLOCK + row_count :] = part[BLOCK:]
     for visit in range(visits):
         first = visit * HALO
-        wide_ref[visit, :EDGE] = above_ref[first + HALO - EDGE : first + HALO]
+        wide_ref[visit, :EDGE] = beside(first + HALO - EDGE, EDGE)[0]
         wide_ref[visit, EDGE : EDGE + row_count] = sci_ref[visit]
-        wide_ref[visit, EDGE + row_count :] = below_ref[first : first + EDGE]
+        wide_ref[visit, EDGE + row_count :] = beside(first, EDGE)[1]
     copies = start_copies(((high_ref, high_out), (low_ref, low_out), (wide_ref, wide_out)), sems)
     for block in range(row_count // BLOCK):
         start = EDGE + block * BLOCK
@@ -352,8 +359,8 @@
             )
     first = visits * HALO
     hits = hits_ref[...]
-    for ref, shift in ((above_ref, -row_count), (below_ref, row_count)):
-        hits = hits + near_mask(ref[first : first + 8, :LANES], float(shift), row_count, col_count)
+    for stamps, shift in zip(beside(first, 8, slice(LANES)), (-row_count, row_count)):
+        hits = hits + near_mask(stamps, float(shift), row_count, col_count)
     mask_ref[...] = jnp.minimum(hits, 1.0)
     for copy in copies:
         copy.wait()
@@ -362,8 +369,9 @@
 def gram_kernel(cfg, warp_ref, cells_ref, mask_ref, design_ref, *refs):
     patches, capacity, visits, row_count, col_count, block_count, step = cfg
     blocks = refs[:block_count]
-    var_ref, down_ref, up_ref, gram_ref, total_ref, weight_ref, sum_ref = refs[block_count:]
+    var_ref, near_ref, far_ref, gram_ref, total_ref, weight_ref, sum_ref = refs[block_count:]
     me = lax.axis_index("patch")
+    odd = lax.axis_index("sub") % 2 == 1
     assemble((patches, capacity), blocks, cells_ref, total_ref, me)
     shared = jnp.full((row_count, col_count), SKY_VAR, F32)
     for visit in range(visits):
@@ -374,6 +382,11 @@
     for visit in range(visits):
         weight_ref[visit] = mask / (var_ref[visit] + shared)
     sum_ref[...] = jnp.zeros(sum_ref.shape, F32)
+
+    body_rows, tail = 8 * (len(TILES) - 1), ONE_SLOT % 8 + 1
+    rows = visits * body_rows + visits // 2 * 8
+    kept = 2 * LANES - 2 * SLOTS - 16
+    at_first = lax.broadcasted_iota(jnp.int32, (8, col_count), 0) < tail
 
     def body(number, carry):
         left, right = [], []
@@ -381,39 +394,50 @@
             row = number * step + extra
             design = design_ref[row]
             high, low = split(design)
-            blank = jnp.zeros((HALF - SLOTS, col_count), BF16)
-            right.append(jnp.concatenate([high, blank, low, blank], axis=0))
-            scaled = [design * weight_ref[visit, pl.ds(row, 1), :] for visit in range(visits)]
-            left.append(jnp.concatenate(split(jnp.concatenate(scaled, axis=0)), axis=0))
+            weights = [weight_ref[visit, pl.ds(row, 1), :] for visit in range(visits)]
+            scaled = [design[:body_rows] * weight for weight in weights]
+            last = design[body_rows:]
+            moved = pltpu.roll(last, tail, 0)
+            for pair in range(visits // 2):
+                scaled.append(jnp.where(at_first, last * weights[2 * pair], moved * weights[2 * pair + 1]))
+            scaled_high, scaled_low = split(jnp.concatenate(scaled, axis=0))
+            blank = jnp.zeros((16, col_count), BF16)
+            right.append(jnp.concatenate([high, low, scaled_low[:kept], blank], axis=0))
+            left.append(jnp.concatenate([scaled_high, high, scaled_low[kept:]], axis=0))
         sum_ref[...] += mul_nt(jnp.concatenate(left, axis=1), jnp.concatenate(right, axis=1))
         return carry
 
     lax.fori_loop(0, row_count // step, body, 0)
+    depth = sum_ref.shape[0]
+    main = sum_ref[:rows, :LANES]
+    turned = jnp.transpose(sum_ref[depth - LANES :, :])[2 * SLOTS : 2 * SLOTS + kept]
+    turned = pltpu.roll(turned, depth - rows, 1)
+    main = main + pltpu.roll(main, LANES - SLOTS, 1)
+    main = main + jnp.concatenate([turned, sum_ref[rows + SLOTS :, :LANES]], axis=0)
     lane = lax.broadcasted_iota(jnp.int32, (SLOTS, 2 * HALF), 1)
-    both = []
-    for visit in range(visits):
-        first = visit * SLOTS
-        second = (visits + visit) * SLOTS
-        value = sum_ref[first : first + SLOTS] + sum_ref[second : second + SLOTS]
-        both.append(value + pltpu.roll(value, HALF, 1))
     for pair in range(visits // 2):
-        value = jnp.where(lane < HALF, both[2 * pair], both[2 * pair + 1])
-        for ref in (gram_ref, down_ref, up_ref):
+        ends = main[visits * body_rows + 8 * pair :][:8]
+        both = []
+        for visit, end in ((2 * pair, ends), (2 * pair + 1, pltpu.roll(ends, 8 - tail, 0))):
+            both.append(jnp.concatenate([main[visit * body_rows : (visit + 1) * body_rows], end], axis=0))
+        value = jnp.where(lane < HALF, both[0], pltpu.roll(both[1], HALF, 1))
+        for ref in (gram_ref, near_ref, far_ref):
             ref[pair * SLOTS : (pair + 1) * SLOTS] = value
     first = visits // 2 * SLOTS
     for visit in range(visits):
         for part in range(col_count // LANES):
-            place = first + (visit * (col_count // LANES) + part) * EDGE
+            place = first + (visit * (col_count // LANES) + part) * PR
             lanes = slice(part * LANES, (part + 1) * LANES)
-            down_ref[place : place + EDGE] = var_ref[visit, row_count - EDGE :, lanes]
-            up_ref[place : place + EDGE] = var_ref[visit, :EDGE, lanes]
+            top, bottom = var_ref[visit, :PR, lanes], var_ref[visit, row_count - PR :, lanes]
+            near_ref[place : place + PR] = jnp.where(odd, top, bottom)
+            far_ref[place : place + PR] = jnp.where(odd, bottom, top)
 
 
 def solve_kernel(cfg, var_ref, *refs):
     visits, row_count, col_count, subtiles, normalizer, gram_count = cfg
     grams = refs[:gram_count]
     fixed = refs[gram_count : gram_count + 6]
-    diff_ref, sig_ref, *held, sems = refs[gram_count + 6 :]
+    diff_ref, sig_ref, spread_ref, *held, sems = refs[gram_count + 6 :]
     copies = start_copies(zip(fixed, held), sems)
     filter_ref, edge_ref, doubled_ref, wide_ref, high_ref, low_ref = held
     sub = lax.axis_index("sub")
@@ -421,17 +445,21 @@
     parts = col_count // LANES
     first = visits // 2 * SLOTS
 
-    def halo(ref, visit):
-        pieces = [ref[first + (visit * parts + part) * EDGE :][:EDGE] for part in range(parts)]
-        return jnp.concatenate(pieces, axis=1)
-
-    from_above, from_below = grams[1], grams[-1]
+    from_far, from_near = grams[1], grams[3]
+    odd = sub % 2 == 1
+    for visit in range(visits):
+        spread_ref[visit, :EDGE] = jnp.zeros((EDGE, col_count), F32)
+        spread_ref[visit, EDGE + row_count :] = jnp.zeros((EDGE, col_count), F32)
+        spread_ref[visit, EDGE : EDGE + row_count] = var_ref[visit]
+        for part in range(parts):
+            place = first + (visit * parts + part) * PR
+            lanes = slice(part * LANES, (part + 1) * LANES)
+            near, far = from_near[place : place + PR], from_far[place : place + PR]
+            spread_ref[visit, EDGE - PR : EDGE, lanes] = jnp.where(odd, near, far)
+            spread_ref[visit, EDGE + row_count : EDGE + row_count + PR, lanes] = jnp.where(odd, far, near)
     row_at = lax.broadcasted_iota(jnp.int32, (high_rows, col_count), 0) + sub * row_count - EDGE
     inside = (row_at >= 0) & (row_at < subtiles * row_count)
-    spread = [
-        jnp.concatenate([halo(from_above, visit), var_ref[visit], halo(from_below, visit)], axis=0)
-        for visit in range(visits)
-    ]
+    spread = [spread_ref[visit] for visit in range(visits)]
     shared = jnp.full((high_rows, col_count), SKY_VAR, F32)
     for visit in range(visits):
         shared = shared + spread[visit] * (1.0 / (visits * visits))
@@ -445,10 +473,6 @@
             mul3(rows, (pair[0][v * high_rows : (v + 1) * high_rows], pair[1][v * high_rows : (v + 1) * high_rows]))
             for v in range(visits)
         ]
-
-    for copy in copies[:3]:
-        copy.wait()
-    noise = detected(inverse, 2)
 
     lane = lax.broadcasted_iota(jnp.int32, (SLOTS, 2 * HALF), 1)
     line = lax.broadcasted_iota(jnp.int32, (SLOTS, 2 * HALF), 0)
@@ -463,6 +487,10 @@
     tiles = [[matrix[8 * part : 8 * part + 8] for part in range(len(TILES))] for matrix in systems]
     line, lane = line[:8], lane[:8]
     for panel in range(len(TILES)):
+        if panel == len(TILES) // 2:
+            for copy in copies[:3]:
+                copy.wait()
+            noise = detected(inverse, 2)
         slots = [slot for slot in LIVE_SLOTS if slot // 8 == panel]
         place = {slot: jnp.where(lane < HALF, slot, HALF + slot) for slot in slots}
         columns = [
@@ -642,7 +670,7 @@
     got_var = route(variances)
 
     side = sds((visits * HALO + 8, col_count), F32)
-    science, up, down, cells = call(
+    science, to_near, to_far, cells = call(
         functools.partial(image_kernel, (patches, capacity, visits, row_count, col_count, image_blocks)),
         [sds((visits, row_count, col_count), F32), side, side, sds((patches * capacity,), jnp.int32)],
         [vmem(), vmem(), vmem(), smem()],
@@ -653,8 +681,9 @@
             pltpu.SemaphoreType.DMA((patches,)),
         ],
     )(warps, stamps, *got)
-    above = lax.ppermute(down, "sub", [(i, i + 1) for i in range(subtiles - 1)])
-    below = lax.ppermute(up, "sub", [(i + 1, i) for i in range(subtiles - 1)])
+    beside = [(i, i ^ 3) for i in range(subtiles) if abs(i - (i ^ 3)) == 1]
+    from_far = lax.ppermute(to_far, "sub", beside)
+    from_near = lax.ppermute(to_near, "sub", [(i, i ^ 1) for i in range(subtiles)])
 
     field = sds((TAP_COUNT, row_count + 2 * BLOCK, col_count), BF16)
     own_field = sds((TAP_COUNT, row_count, col_count), BF16)
@@ -673,12 +702,13 @@
         [vmem()] * 2 + [far()] * 3,
         [vmem()] * 7,
         [pltpu.VMEM(part.shape, part.dtype) for part in (field, field, wide)] + [pltpu.SemaphoreType.DMA((3,))],
-    )(science, above, below, held, own_high, own_low, hits)
+    )(science, from_far, from_near, held, own_high, own_low, hits)
 
     gram_rows = visits // 2 * SLOTS
-    tail_rows = visits * EDGE * (col_count // LANES)
+    tail_rows = visits * PR * (col_count // LANES)
     step = 32
-    variance, to_below, to_above, gram = call(
+    gram_depth = 2 * visits * (8 * len(TILES) - 4) + 3 * SLOTS + 16 - 2 * LANES
+    variance, to_near, to_far, gram = call(
         functools.partial(gram_kernel, (patches, capacity, visits, row_count, col_count, var_blocks, step)),
         [
             sds((visits, row_count, col_count), F32),
@@ -691,13 +721,12 @@
         [
             pltpu.VMEM((visits * NCELL + 1, 2, 8, LANES), F32),
             pltpu.VMEM((visits, row_count, col_count), F32),
-            pltpu.VMEM((2 * visits * SLOTS, 2 * HALF), F32),
+            pltpu.VMEM((gram_depth, 2 * LANES), F32),
         ],
     )(warps, cells, mask, design, *got_var)
     grams = [gram]
-    for shift in range(1, subtiles):
-        sent = to_below if shift == 1 else to_above if shift == subtiles - 1 else gram
-        grams.append(lax.ppermute(sent, "sub", [(i, (i + shift) % subtiles) for i in range(subtiles)]))
+    for away, part in ((3, to_far), (2, gram), (1, to_near)):
+        grams.append(lax.ppermute(part, "sub", [(i, i ^ away) for i in range(subtiles)]))
 
     normalizer = subtiles * slots * (2 * SH + 1) ** 2
     result = sds((visits, 1, row_count, col_count), F32)
@@ -707,7 +736,7 @@
         [result, result],
         [vmem(), vmem()],
         [vmem()] * (1 + len(grams)) + [far()] * len(kept),
-        [pltpu.VMEM(part.shape, part.dtype) for part in kept] + [pltpu.SemaphoreType.DMA((len(kept),))],
+        [pltpu.VMEM(wide.shape, F32)] + [pltpu.VMEM(part.shape, part.dtype) for part in kept] + [pltpu.SemaphoreType.DMA((len(kept),))],
     )(variance, *grams, *[in_hbm(part) for part in kept])
 
 

time: 58.5 us -> 55.2 us (0.944)
  starting transfers between devices: 24.6 us -> 23.1 us
  Pallas kernels: 23.9 us -> 22.5 us
    ppermute x5, starting transfers between devices: 7.25 us -> 5.8 us  [the longest x1 2.93 us: local(): lax.ppermute(to_near, 'sub', [(i, i ^ 1) for i in range(subtiles)])]
    all_to_all x1, waiting for transfers between devices: 1.65 us -> 0.65 us  [route(): lax.all_to_all(blocks[0], 'patch', split_axis=0, concat_axis=0, tiled=True)]
    pallas_call x1, Pallas kernels: 5.33 us -> 4.43 us  [local(): call(functools.partial(gram_kernel, (patches, capacity, visits, row_count...]
  transfers between devices with their start and end apart: 13 -> 13, of which waited for: 6 -> 6; matrix products, arithmetic and copies ran while one was open for 0% -> 0% of each run, Pallas kernels for 20% -> 22%
where the time goes in v2:
time: 55.2 us; the launch traced here: 54.9 us
  starting transfers between devices  23.1 us (42%)
  Pallas kernels  22.5 us (41%)
  waiting for transfers between devices  7.86 us (14%)
  between operations  1.37 us (2%)
    ppermute x7, starting transfers between devices, route(): lax.ppermute(block, 'patch', [(i, i ^ away) for i in range(patches)])  12.3 us
    all_to_all x1, starting transfers between devices, route(): lax.all_to_all(blocks[0], 'patch', split_axis=0, concat_axis=0, tiled=True)  5.07 us
    pallas_call x1, Pallas kernels, local(): call(functools.partial(solve_kernel, (visits, row_count, col_count, subti...  4.53 us
    pallas_call x1, Pallas kernels, local(): call(functools.partial(gram_kernel, (patches, capacity, visits, row_count...  4.43 us
    pallas_call x1, Pallas kernels, local(): call(functools.partial(own_kernel, (visits, row_count, col_count)), [sds(...  4 us
    ppermute x3, waiting for transfers between devices, local(): lax.ppermute(part, 'sub', [(i, i ^ away) for i in range(subtiles)])  3.84 us
    ppermute x7, waiting for transfers between devices, route(): lax.ppermute(block, 'patch', [(i, i ^ away) for i in range(patches)])  3.36 us
    pallas_call x1, Pallas kernels, local(): call(functools.partial(design_kernel, (visits, row_count, col_count)), [s...  3.23 us
  transfers between devices with their start and end apart: 13, of which 6 were waited for; matrix products, arithmetic and copies ran while one was open for 0% of the time, Pallas kernels for 22%

profile of v2, /device:TPU:0, one launch (start us, length us, event | category | flops | bytes accessed | tf_op | source)
XLA Modules:
  0.0 54.9 jit_solution(11803321081976042662)
XLA Ops:
  1.3 1.7 %shard_map.131 = (f32[1,17,8,128]{3,2,1,0:T(8,128)S(1)}, f32[1,17,8,128]{3,2,1,0:T(8,128)S(1)}, f32[1,17,8,128]{3,2,1,0:T(8,128)S(1)}, f32[1,17,8,128]{3,2,1,0:T...) custom-call(s32[1,32]{1,0:T(1,128)} %bitcast.1, ...), custom_call_target="tpu_custom_call" | custom-call | tf_op jit(solution)/shard_map/pallas_call | solution.py:625
  3.0 3.0 %collective-permute-start = (f32[1,17,8,128]{3,2,1,0:T(8,128)S(1)}, f32[1,17,8,128]{3,2,1,0:T(8,128)S(1)}, u32[]{:S(2)}, u32[]{:S(2)}) collective-permute-start(f32[1,17,8,128]{3,2,1,0:T(8,128)S(1)} %get-tuple-element.33), channel_id=1, source_target_pairs={{0,4},{4,0},{8,12},{12,8},{16,20},{20,16},{24,28},{28,24},{1,5},{5... | collective-permute-start | bytes 208904 | tf_op jit(solution)/shard_map/ppermute | solution.py:657
  6.0 1.6 %collective-permute-start.1 = (f32[1,17,8,128]{3,2,1,0:T(8,128)S(1)}, f32[1,17,8,128]{3,2,1,0:T(8,128)S(1)}, u32[]{:S(2)}, u32[]{:S(2)}) collective-permute-start(f32[1,17,8,128]{3,2,1,0:T(8,128)S(1)} %get-tuple-element.34), channel_id=1, source_target_pairs={{0,8},{4,12},{8,0},{12,4},{16,24},{20,28},{24,16},{28,20},{1,9},{5... | collective-permute-start | bytes 208904 | tf_op jit(solution)/shard_map/ppermute | solution.py:657
  7.6 2.6 %collective-permute-start.2 = (f32[1,17,8,128]{3,2,1,0:T(8,128)S(1)}, f32[1,17,8,128]{3,2,1,0:T(8,128)S(1)}, u32[]{:S(2)}, u32[]{:S(2)}) collective-permute-start(f32[1,17,8,128]{3,2,1,0:T(8,128)S(1)} %get-tuple-element.35), channel_id=1, source_target_pairs={{0,16},{4,20},{8,24},{12,28},{16,0},{20,4},{24,8},{28,12},{1,17},{... | collective-permute-start | bytes 208904 | tf_op jit(solution)/shard_map/ppermute | solution.py:657
  10.2 0.3 collective-permute-start.3
  10.5 2.5 %collective-permute-start.4 = (f32[1,17,8,128]{3,2,1,0:T(8,128)S(1)}, f32[1,17,8,128]{3,2,1,0:T(8,128)S(1)}, u32[]{:S(2)}, u32[]{:S(2)}) collective-permute-start(f32[1,17,8,128]{3,2,1,0:T(8,128)S(1)} %get-tuple-element.37), channel_id=1, source_target_pairs={{0,24},{4,28},{8,16},{12,20},{16,8},{20,12},{24,0},{28,4},{1,25},{... | collective-permute-start | bytes 208904 | tf_op jit(solution)/shard_map/ppermute | solution.py:657
  13.0 0.0 collective-permute-done.refs_1_
  13.0 2.3 %collective-permute-start.5 = (f32[1,17,8,128]{3,2,1,0:T(8,128)S(1)}, f32[1,17,8,128]{3,2,1,0:T(8,128)S(1)}, u32[]{:S(2)}, u32[]{:S(2)}) collective-permute-start(f32[1,17,8,128]{3,2,1,0:T(8,128)S(1)} %get-tuple-element.38), channel_id=1, source_target_pairs={{0,28},{4,24},{8,20},{12,16},{16,12},{20,8},{24,4},{28,0},{1,29},{... | collective-permute-start | bytes 208904 | tf_op jit(solution)/shard_map/ppermute | solution.py:657
  15.3 0.0 collective-permute-done.1.refs_2_
  15.3 0.0 collective-permute-start.6
  15.3 2.4 %shard_map.135.refs_0_ = f32[8,16,8,128]{3,2,1,0:T(8,128)} custom-call(s32[64]{0:T(128)S(1)} %get-tuple-element.50.chosen_ref, f32[1,32,8,256]{3,2,1,0:T(8,128)} %var_hbm.1), custom_call_target="tpu_custom_call" | custom-call | tf_op jit(solution)/shard_map/pallas_call | solution.py:661
  17.6 0.1 collective-permute-done.2.refs_3_
  17.7 1.5 %collective-permute-done.3.refs_4_ = f32[1,17,8,128]{3,2,1,0:T(8,128)S(1)} collective-permute-done((f32[1,17,8,128]{3,2,1,0:T(8,128)S(1)}, f32[1,17,8,128]{3,2,1,0:T(8,128)S(1)}, u32[]{:S(2)}, u32[]{:S(2)}) %collective-permute-start.3) | collective-permute-done | bytes 69664 | tf_op jit(solution)/shard_map/ppermute | solution.py:657
  19.2 0.0 collective-permute-done.4.refs_5_
  19.3 0.8 %collective-permute-done.5.refs_6_ = f32[1,17,8,128]{3,2,1,0:T(8,128)S(1)} collective-permute-done((f32[1,17,8,128]{3,2,1,0:T(8,128)S(1)}, f32[1,17,8,128]{3,2,1,0:T(8,128)S(1)}, u32[]{:S(2)}, u32[]{:S(2)}) %collective-permute-start.5) | collective-permute-done | bytes 69664 | tf_op jit(solution)/shard_map/ppermute | solution.py:657
  20.1 0.9 %collective-permute-done.6.refs_7_ = f32[1,17,8,128]{3,2,1,0:T(8,128)S(1)} collective-permute-done((f32[1,17,8,128]{3,2,1,0:T(8,128)S(1)}, f32[1,17,8,128]{3,2,1,0:T(8,128)S(1)}, u32[]{:S(2)}, u32[]{:S(2)}) %collective-permute-start.6) | collective-permute-done | bytes 69664 | tf_op jit(solution)/shard_map/ppermute | solution.py:657
  21.0 5.1 %all-to-all-start = ((f32[8,16,8,128]{3,2,1,0:T(8,128)}), f32[8,16,8,128]{3,2,1,0:T(8,128)}, u32[]{:S(2)}, u32[]{:S(2)}) async-start(f32[8,16,8,128]{3,2,1,0:T(8,128)} %shard_map.136), calls=%async_computation | async-start | bytes 1048576 | tf_op jit(solution)/shard_map/all_to_all | solution.py:654
  26.1 2.3 %shard_map.132 = (f32[4,64,256]{2,1,0:T(8,128)S(1)}, f32[104,256]{1,0:T(8,128)S(1)}, f32[104,256]{1,0:T(8,128)S(1)}, s32[64]{0:T(128)S(1)}) custom-call(s32[4]{0:T(128)S(1)} %get-tuple-element.30.warp_ref, f32[8,128]{1,0:T(8,128)S(1)} %get-tuple-element.31.stamp_ref, f32[1,17,8,128]{3,2,1,0:T(8,128)S(1)} %get-tuple-element.32.refs_0_, ...), custom_call_target="tpu_custom_call" | custom-call | tf_op jit(solution)/shard_map/pallas_call | solution.py:673
  28.3 0.7 %collective-permute-start.7 = (f32[104,256]{1,0:T(8,128)S(1)}, f32[104,256]{1,0:T(8,128)S(1)}, u32[]{:S(2)}, u32[]{:S(2)}) collective-permute-start(f32[104,256]{1,0:T(8,128)S(1)} %get-tuple-element.42), channel_id=1, source_target_pairs={{1,2},{2,1},{5,6},{6,5},{9,10},{10,9},{13,14},{14,13},{17,18},{18,... | collective-permute-start | bytes 319496 | tf_op jit(solution)/shard_map/ppermute | solution.py:685
  29.0 2.9 %collective-permute-start.8 = (f32[104,256]{1,0:T(8,128)S(1)}, f32[104,256]{1,0:T(8,128)S(1)}, u32[]{:S(2)}, u32[]{:S(2)}) collective-permute-start(f32[104,256]{1,0:T(8,128)S(1)} %get-tuple-element.43), channel_id=1, source_target_pairs={{0,1},{1,0},{2,3},{3,2},{4,5},{5,4},{6,7},{7,6},{8,9},{9,8},{10,11... | collective-permute-start | bytes 319496 | tf_op jit(solution)/shard_map/ppermute | solution.py:686
  32.0 4.0 %shard_map.133 = (bf16[20,2,256,256]{3,2,1,0:T(8,128)(2,1)S(1)}, bf16[14,64,256]{2,1,0:T(8,128)(2,1)S(1)}, bf16[14,64,256]{2,1,0:T(8,128)(2,1)S(1)}, f32[64,256]{1,0:T(8,128)S(1)}) custom-call(f32[4,64,256]{2,1,0:T(8,128)S(1)} %get-tuple-element.41.sci_ref, f32[8,128]{1,0:T(8,128)S(1)} %get-tuple-element.31.stamp_ref, ...), custom_call_target="tpu_custom_call" | custom-call | tf_op jit(solution)/shard_map/pallas_call | solution.py:692
  36.0 0.0 collective-permute-done.8.near_ref
  36.0 3.2 %shard_map.134 = (f32[64,48,256]{2,1,0:T(8,128)S(1)}, f32[64,256]{1,0:T(8,128)S(1)}, bf16[14,128,256]{2,1,0:T(8,128)(2,1)}, bf16[14,128,256]{2,1,0:T(8,128)(2,1)}, f32[4,96,256]{2,1,0:T(8,128)}) custom-call(f32[4,64,256]{2,1,0:T(8,128)S(1)} %get-tuple-element.41.sci_ref, f32[104,256]{1,0:T(8,128)S(1)} %collective-permute-done.7.far_ref, ...), custom_call_target="tpu_custom_call" | custom-call | tf_op jit(solution)/shard_map/pallas_call | solution.py:699
  39.2 0.7 %all-to-all-done.refs_0_ = f32[8,16,8,128]{3,2,1,0:T(8,128)} async-done(((f32[8,16,8,128]{3,2,1,0:T(8,128)}), f32[8,16,8,128]{3,2,1,0:T(8,128)}, u32[]{:S(2)}, u32[]{:S(2)}) %all-to-all-start) | async-done | bytes 524320 | tf_op jit(solution)/shard_map/all_to_all | solution.py:654
  39.9 4.4 %shard_map.137 = (f32[4,64,256]{2,1,0:T(8,128)S(1)}, f32[176,128]{1,0:T(8,128)S(1)}, f32[176,128]{1,0:T(8,128)S(1)}, f32[96,128]{1,0:T(8,128)S(1)}) custom-call(s32[4]{0:T(128)S(1)} %get-tuple-element.30.warp_ref, s32[64]{0:T(128)S(1)} %get-tuple-element.40.cells_ref, f32[64,256]{1,0:T(8,128)S(1)} %get-tuple-element.48.mask_ref, ...), custom_call_target="tpu_custom_call" | custom-call | tf_op jit(solution)/shard_map/pallas_call | solution.py:711
  44.3 0.1 collective-permute-start.9
  44.4 1.6 %collective-permute-start.11 = (f32[176,128]{1,0:T(8,128)S(1)}, f32[176,128]{1,0:T(8,128)S(1)}, u32[]{:S(2)}, u32[]{:S(2)}) collective-permute-start(f32[176,128]{1,0:T(8,128)S(1)} %get-tuple-element.54), channel_id=1, source_target_pairs={{0,1},{1,0},{2,3},{3,2},{4,5},{5,4},{6,7},{7,6},{8,9},{9,8},{10,11... | collective-permute-start | bytes 270344 | tf_op jit(solution)/shard_map/ppermute | solution.py:729
  46.0 0.5 collective-permute-start.10
  46.5 3.8 %collective-permute-done.10.refs_2_ = f32[96,128]{1,0:T(8,128)S(1)} collective-permute-done((f32[96,128]{1,0:T(8,128)S(1)}, f32[96,128]{1,0:T(8,128)S(1)}, u32[]{:S(2)}, u32[]{:S(2)}) %collective-permute-start.10) | collective-permute-done | bytes 49184 | tf_op jit(solution)/shard_map/ppermute | solution.py:729
  50.4 0.0 collective-permute-done.9.refs_1_
  50.4 0.0 collective-permute-done.11.refs_3_
  50.4 4.5 %shard_map.138 = (f32[4,1,64,256]{3,2,1,0:T(8,128)}, f32[4,1,64,256]{3,2,1,0:T(8,128)}) custom-call(f32[4,64,256]{2,1,0:T(8,128)S(1)} %get-tuple-element.51.var_ref, f32[96,128]{1,0:T(8,128)S(1)} %get-tuple-element.52.refs_0_, f32[176,128]{1,0:T(8,128)S(1)} %collective-permute-done.9.refs_1_, f32[96,128]{1,0:T(8,128)S(1)} %collective-permute-done.10.refs_2_, ...), custom_call_target="tpu_custom_call" | custom-call | tf_op jit(solution)/shard_map/pallas_call | solution.py:734
  (2 shorter events, 0.0 us)
Async XLA Ops:
  3.0 10.0 %collective-permute-start = (f32[1,17,8,128]{3,2,1,0:T(8,128)S(1)}, f32[1,17,8,128]{3,2,1,0:T(8,128)S(1)}, u32[]{:S(2)}, u32[]{:S(2)}) collective-permute-start(f32[1,17,8,128]{3,2,1,0:T(8,128)S(1)} %get-tuple-element.33), channel_id=1, source_target_pairs={{0,4},{4,0},{8,12},{12,8},{16,20},{20,16},{24,28},{28,24},{1,5},{5... | collective-permute-start | bytes 208904 | tf_op jit(solution)/shard_map/ppermute | solution.py:657
  6.0 9.2 %collective-permute-start.1 = (f32[1,17,8,128]{3,2,1,0:T(8,128)S(1)}, f32[1,17,8,128]{3,2,1,0:T(8,128)S(1)}, u32[]{:S(2)}, u32[]{:S(2)}) collective-permute-start(f32[1,17,8,128]{3,2,1,0:T(8,128)S(1)} %get-tuple-element.34), channel_id=1, source_target_pairs={{0,8},{4,12},{8,0},{12,4},{16,24},{20,28},{24,16},{28,20},{1,9},{5... | collective-permute-start | bytes 208904 | tf_op jit(solution)/shard_map/ppermute | solution.py:657
  7.6 10.1 %collective-permute-start.2 = (f32[1,17,8,128]{3,2,1,0:T(8,128)S(1)}, f32[1,17,8,128]{3,2,1,0:T(8,128)S(1)}, u32[]{:S(2)}, u32[]{:S(2)}) collective-permute-start(f32[1,17,8,128]{3,2,1,0:T(8,128)S(1)} %get-tuple-element.35), channel_id=1, source_target_pairs={{0,16},{4,20},{8,24},{12,28},{16,0},{20,4},{24,8},{28,12},{1,17},{... | collective-permute-start | bytes 208904 | tf_op jit(solution)/shard_map/ppermute | solution.py:657
  10.2 9.1 %collective-permute-start.3 = (f32[1,17,8,128]{3,2,1,0:T(8,128)S(1)}, f32[1,17,8,128]{3,2,1,0:T(8,128)S(1)}, u32[]{:S(2)}, u32[]{:S(2)}) collective-permute-start(f32[1,17,8,128]{3,2,1,0:T(8,128)S(1)} %get-tuple-element.36), channel_id=1, source_target_pairs={{0,20},{4,16},{8,28},{12,24},{16,4},{20,0},{24,12},{28,8},{1,21},{... | collective-permute-start | bytes 208904 | tf_op jit(solution)/shard_map/ppermute | solution.py:657
  10.5 8.8 %collective-permute-start.4 = (f32[1,17,8,128]{3,2,1,0:T(8,128)S(1)}, f32[1,17,8,128]{3,2,1,0:T(8,128)S(1)}, u32[]{:S(2)}, u32[]{:S(2)}) collective-permute-start(f32[1,17,8,128]{3,2,1,0:T(8,128)S(1)} %get-tuple-element.37), channel_id=1, source_target_pairs={{0,24},{4,28},{8,16},{12,20},{16,8},{20,12},{24,0},{28,4},{1,25},{... | collective-permute-start | bytes 208904 | tf_op jit(solution)/shard_map/ppermute | solution.py:657
  13.0 7.1 %collective-permute-start.5 = (f32[1,17,8,128]{3,2,1,0:T(8,128)S(1)}, f32[1,17,8,128]{3,2,1,0:T(8,128)S(1)}, u32[]{:S(2)}, u32[]{:S(2)}) collective-permute-start(f32[1,17,8,128]{3,2,1,0:T(8,128)S(1)} %get-tuple-element.38), channel_id=1, source_target_pairs={{0,28},{4,24},{8,20},{12,16},{16,12},{20,8},{24,4},{28,0},{1,29},{... | collective-permute-start | bytes 208904 | tf_op jit(solution)/shard_map/ppermute | solution.py:657
  15.3 5.7 %collective-permute-start.6 = (f32[1,17,8,128]{3,2,1,0:T(8,128)S(1)}, f32[1,17,8,128]{3,2,1,0:T(8,128)S(1)}, u32[]{:S(2)}, u32[]{:S(2)}) collective-permute-start(f32[1,17,8,128]{3,2,1,0:T(8,128)S(1)} %get-tuple-element.39), channel_id=1, source_target_pairs={{0,12},{4,8},{8,4},{12,0},{16,28},{20,24},{24,20},{28,16},{1,13},{... | collective-permute-start | bytes 208904 | tf_op jit(solution)/shard_map/ppermute | solution.py:657
  21.0 18.9 %all-to-all-start = ((f32[8,16,8,128]{3,2,1,0:T(8,128)}), f32[8,16,8,128]{3,2,1,0:T(8,128)}, u32[]{:S(2)}, u32[]{:S(2)}) async-start(f32[8,16,8,128]{3,2,1,0:T(8,128)} %shard_map.136), calls=%async_computation | async-start | bytes 1048576 | tf_op jit(solution)/shard_map/all_to_all | solution.py:654
  28.3 7.6 %collective-permute-start.7 = (f32[104,256]{1,0:T(8,128)S(1)}, f32[104,256]{1,0:T(8,128)S(1)}, u32[]{:S(2)}, u32[]{:S(2)}) collective-permute-start(f32[104,256]{1,0:T(8,128)S(1)} %get-tuple-element.42), channel_id=1, source_target_pairs={{1,2},{2,1},{5,6},{6,5},{9,10},{10,9},{13,14},{14,13},{17,18},{18,... | collective-permute-start | bytes 319496 | tf_op jit(solution)/shard_map/ppermute | solution.py:685
  29.0 7.0 %collective-permute-start.8 = (f32[104,256]{1,0:T(8,128)S(1)}, f32[104,256]{1,0:T(8,128)S(1)}, u32[]{:S(2)}, u32[]{:S(2)}) collective-permute-start(f32[104,256]{1,0:T(8,128)S(1)} %get-tuple-element.43), channel_id=1, source_target_pairs={{0,1},{1,0},{2,3},{3,2},{4,5},{5,4},{6,7},{7,6},{8,9},{9,8},{10,11... | collective-permute-start | bytes 319496 | tf_op jit(solution)/shard_map/ppermute | solution.py:686
  44.3 6.0 %collective-permute-start.9 = (f32[176,128]{1,0:T(8,128)S(1)}, f32[176,128]{1,0:T(8,128)S(1)}, u32[]{:S(2)}, u32[]{:S(2)}) collective-permute-start(f32[176,128]{1,0:T(8,128)S(1)} %get-tuple-element.53), channel_id=1, source_target_pairs={{0,3},{1,2},{2,1},{3,0},{4,7},{5,6},{6,5},{7,4},{8,11},{9,10},{10,... | collective-permute-start | bytes 270344 | tf_op jit(solution)/shard_map/ppermute | solution.py:729
  44.4 6.0 %collective-permute-start.11 = (f32[176,128]{1,0:T(8,128)S(1)}, f32[176,128]{1,0:T(8,128)S(1)}, u32[]{:S(2)}, u32[]{:S(2)}) collective-permute-start(f32[176,128]{1,0:T(8,128)S(1)} %get-tuple-element.54), channel_id=1, source_target_pairs={{0,1},{1,0},{2,3},{3,2},{4,5},{5,4},{6,7},{7,6},{8,9},{9,8},{10,11... | collective-permute-start | bytes 270344 | tf_op jit(solution)/shard_map/ppermute | solution.py:729
  46.0 4.3 %collective-permute-start.10 = (f32[96,128]{1,0:T(8,128)S(1)}, f32[96,128]{1,0:T(8,128)S(1)}, u32[]{:S(2)}, u32[]{:S(2)}) collective-permute-start(f32[96,128]{1,0:T(8,128)S(1)} %get-tuple-element.52.refs_0_), channel_id=1, source_target_pairs={{0,2},{1,3},{2,0},{3,1},{4,6},{5,7},{6,4},{7,5},{8,10},{9,11},{10,... | collective-permute-start | bytes 147464 | tf_op jit(solution)/shard_map/ppermute | solution.py:729

commit v3 on v2

--- a/solution.py
+++ b/solution.py
@@ -146,8 +146,8 @@
 
 
 def turn(patches):
-    near, far_half = list(range(1, patches // 2)), list(range(patches // 2, patches))
-    return [0, *near[:2], *far_half, *near[2:]]
+    half = patches // 2
+    return [0, *(away for step in range(half) for away in (half + step, step + 1))][:patches]
 
 
 def fill(cfg, outs, source, chosen_ref, table_ref):
@@ -296,22 +296,15 @@
     return split(both[:rows] + both[rows:] + mul(image[0], held_ref[tap, 1]))
 
 
-def own_kernel(cfg, sci_ref, stamp_ref, fixed_ref, held_ref, high_ref, low_ref, hits_ref, sems):
-    visits, row_count, col_count = cfg
+def fetch_kernel(cfg, stamp_ref, fixed_ref, held_ref, hits_ref, sems):
+    row_count, col_count = cfg
     copies = start_copies([(fixed_ref.at[n], held_ref.at[n]) for n in range(TAP_COUNT + len(TILES))], sems)
-    own = sci_ref[0]
-    for visit in range(1, visits):
-        own = own + sci_ref[visit]
-    template = split(own * (1.0 / visits))
     hits_ref[...] = near_mask(stamp_ref[...], 0.0, row_count, col_count)
-    for tap in range(TAP_COUNT):
-        copies[tap].wait()
-        high_ref[tap], low_ref[tap] = filter_columns(template, tap, held_ref)
-    for copy in copies[TAP_COUNT:]:
+    for copy in copies:
         copy.wait()
 
 
-def design_kernel(cfg, sci_ref, far_ref, near_ref, held_ref, own_high, own_low, hits_ref, *refs):
+def design_kernel(cfg, sci_ref, far_ref, near_ref, held_ref, hits_ref, *refs):
     visits, row_count, col_count = cfg
     design_ref, mask_ref, high_out, low_out, wide_out, high_ref, low_ref, wide_ref, sems = refs
     odd = lax.axis_index("sub") % 2 == 1
@@ -321,16 +314,14 @@
         return jnp.where(odd, near, far), jnp.where(odd, far, near)
 
     above, below = beside(0, HALO)
+    own = sci_ref[0]
     for visit in range(1, visits):
         more = beside(visit * HALO, HALO)
-        above, below = above + more[0], below + more[1]
+        above, own, below = above + more[0], own + sci_ref[visit], below + more[1]
     rim = jnp.zeros((BLOCK - HALO, col_count), F32)
-    template = split(jnp.concatenate([rim, above, below, rim], axis=0) * (1.0 / visits))
+    template = split(jnp.concatenate([rim, above, own, below, rim], axis=0) * (1.0 / visits))
     for tap in range(TAP_COUNT):
-        for ref, own, part in zip((high_ref, low_ref), (own_high, own_low), filter_columns(template, tap, held_ref)):
-            ref[tap, :BLOCK] = part[:BLOCK]
-            ref[tap, BLOCK : BLOCK + row_count] = own[tap]
-            ref[tap, BLOCK + row_count :] = part[BLOCK:]
+        high_ref[tap], low_ref[tap] = filter_columns(template, tap, held_ref)
     for visit in range(visits):
         first = visit * HALO
         wide_ref[visit, :EDGE] = beside(first + HALO - EDGE, EDGE)[0]
@@ -437,8 +428,9 @@
     visits, row_count, col_count, subtiles, normalizer, gram_count = cfg
     grams = refs[:gram_count]
     fixed = refs[gram_count : gram_count + 6]
-    diff_ref, sig_ref, spread_ref, *held, sems = refs[gram_count + 6 :]
+    diff_out, sig_out, spread_ref, diff_ref, sig_ref, *held, sems, out_sems = refs[gram_count + 6 :]
     copies = start_copies(zip(fixed, held), sems)
+    results = []
     filter_ref, edge_ref, doubled_ref, wide_ref, high_ref, low_ref = held
     sub = lax.axis_index("sub")
     high_rows = row_count + 2 * EDGE
@@ -549,11 +541,17 @@
     for visit in range(visits):
         model = jnp.concatenate([part[visit * BLOCK : (visit + 1) * BLOCK] for part in models], axis=0)
         difference = wide_ref[visit] - model - offsets[visit]
-        diff_ref[visit, 0] = difference[EDGE : EDGE + row_count]
+        diff_ref[visit] = difference[EDGE : EDGE + row_count]
+        results.append(pltpu.make_async_copy(diff_ref.at[visit], diff_out.at[visit, 0], out_sems.at[visit]))
+        results[-1].start()
         weighted.append(difference * inverse[visit])
     signal = detected(weighted, 0)
     for visit in range(visits):
-        sig_ref[visit, 0] = signal[visit] * lax.rsqrt(noise[visit])
+        sig_ref[visit] = signal[visit] * lax.rsqrt(noise[visit])
+        results.append(pltpu.make_async_copy(sig_ref.at[visit], sig_out.at[visit, 0], out_sems.at[visits + visit]))
+        results[-1].start()
+    for copy in results:
+        copy.wait()
 
 
 def vmem():
@@ -686,23 +684,22 @@
     from_near = lax.ppermute(to_near, "sub", [(i, i ^ 1) for i in range(subtiles)])
 
     field = sds((TAP_COUNT, row_count + 2 * BLOCK, col_count), BF16)
-    own_field = sds((TAP_COUNT, row_count, col_count), BF16)
     plane = sds((row_count, col_count), F32)
     wide = sds((visits, row_count + 2 * EDGE, col_count), F32)
-    held, own_high, own_low, hits = call(
-        functools.partial(own_kernel, (visits, row_count, col_count)),
-        [sds(design_fixed.shape, BF16), own_field, own_field, plane],
-        [vmem()] * 4,
-        [vmem(), vmem(), far()],
+    held, hits = call(
+        functools.partial(fetch_kernel, (row_count, col_count)),
+        [sds(design_fixed.shape, BF16), plane],
+        [vmem()] * 2,
+        [vmem(), far()],
         [pltpu.SemaphoreType.DMA((design_fixed.shape[0],))],
-    )(science, stamps, in_hbm(design_fixed))
+    )(stamps, in_hbm(design_fixed))
     design, mask, high, low, wide_science = call(
         functools.partial(design_kernel, (visits, row_count, col_count)),
         [sds((row_count, SLOTS, col_count), F32), plane] + [pltpu.HBM(part.shape, part.dtype) for part in (field, field, wide)],
         [vmem()] * 2 + [far()] * 3,
-        [vmem()] * 7,
+        [vmem()] * 5,
         [pltpu.VMEM(part.shape, part.dtype) for part in (field, field, wide)] + [pltpu.SemaphoreType.DMA((3,))],
-    )(science, from_far, from_near, held, own_high, own_low, hits)
+    )(science, from_far, from_near, held, hits)
 
     gram_rows = visits // 2 * SLOTS
     tail_rows = visits * PR * (col_count // LANES)
@@ -734,9 +731,12 @@
     return call(
         functools.partial(solve_kernel, (visits, row_count, col_count, subtiles, float(normalizer), len(grams))),
         [result, result],
-        [vmem(), vmem()],
+        [far(), far()],
         [vmem()] * (1 + len(grams)) + [far()] * len(kept),
-        [pltpu.VMEM(wide.shape, F32)] + [pltpu.VMEM(part.shape, part.dtype) for part in kept] + [pltpu.SemaphoreType.DMA((len(kept),))],
+        [pltpu.VMEM(wide.shape, F32)]
+        + [pltpu.VMEM((visits, row_count, col_count), F32)] * 2
+        + [pltpu.VMEM(part.shape, part.dtype) for part in kept]
+        + [pltpu.SemaphoreType.DMA((len(kept),)), pltpu.SemaphoreType.DMA((2 * visits,))],
     )(variance, *grams, *[in_hbm(part) for part in kept])
 
 

time: 55.2 us -> 53.9 us (0.976)
  Pallas kernels: 22.5 us -> 20.6 us
  starting transfers between devices: 23.1 us -> 24.3 us
  waiting for transfers between devices: 7.86 us -> 7.29 us
    ppermute x7, starting transfers between devices: 12.3 us -> 14.3 us  [route(): lax.ppermute(block, 'patch', [(i, i ^ away) for i in range(patches)])]
    ppermute x7, waiting for transfers between devices: 3.36 us -> 1.88 us  [route(): lax.ppermute(block, 'patch', [(i, i ^ away) for i in range(patches)])]
    pallas_call x1, Pallas kernels: 4 us -> 2.63 us  [local(): call(functools.partial(fetch_kernel, (row_count, col_count)), [sds(design...]
    all_to_all x1, starting transfers between devices: 5.07 us -> 4.15 us  [route(): lax.all_to_all(blocks[0], 'patch', split_axis=0, concat_axis=0, tiled=True)]
    all_to_all x1, waiting for transfers between devices: 0.65 us -> 1.57 us  [route(): lax.all_to_all(blocks[0], 'patch', split_axis=0, concat_axis=0, tiled=True)]
  transfers between devices with their start and end apart: 13 -> 13, of which waited for: 6 -> 3; matrix products, arithmetic and copies ran while one was open for 0% -> 0% of each run, Pallas kernels for 22% -> 19%
where the time goes in v3:
time: 53.9 us; the launch traced here: 53.5 us
  starting transfers between devices  24.3 us (45%)
  Pallas kernels  20.6 us (38%)
  waiting for transfers between devices  7.29 us (14%)
  between operations  1.41 us (3%)
    ppermute x7, starting transfers between devices, route(): lax.ppermute(block, 'patch', [(i, i ^ away) for i in range(patches)])  14.3 us
    pallas_call x1, Pallas kernels, local(): call(functools.partial(solve_kernel, (visits, row_count, col_count, subti...  4.53 us
    pallas_call x1, Pallas kernels, local(): call(functools.partial(gram_kernel, (patches, capacity, visits, row_count...  4.32 us
    all_to_all x1, starting transfers between devices, route(): lax.all_to_all(blocks[0], 'patch', split_axis=0, concat_axis=0, tiled=True)  4.15 us
    ppermute x3, waiting for transfers between devices, local(): lax.ppermute(part, 'sub', [(i, i ^ away) for i in range(subtiles)])  3.84 us
    ppermute x1, starting transfers between devices, local(): lax.ppermute(to_near, 'sub', [(i, i ^ 1) for i in range(subtiles)])  2.92 us
    pallas_call x1, Pallas kernels, local(): call(functools.partial(design_kernel, (visits, row_count, col_count)), [s...  2.87 us
    pallas_call x1, Pallas kernels, local(): call(functools.partial(fetch_kernel, (row_count, col_count)), [sds(design...  2.63 us
  transfers between devices with their start and end apart: 13, of which 3 were waited for; matrix products, arithmetic and copies ran while one was open for 0% of the time, Pallas kernels for 19%

profile of v3, /device:TPU:0, one launch (start us, length us, event | category | flops | bytes accessed | tf_op | source)
XLA Modules:
  0.0 53.5 jit_solution(14537001560399175041)
XLA Ops:
  1.3 1.7 %shard_map.131 = (f32[1,17,8,128]{3,2,1,0:T(8,128)S(1)}, f32[1,17,8,128]{3,2,1,0:T(8,128)S(1)}, f32[1,17,8,128]{3,2,1,0:T(8,128)S(1)}, f32[1,17,8,128]{3,2,1,0:T...) custom-call(s32[1,32]{1,0:T(1,128)} %bitcast.1, ...), custom_call_target="tpu_custom_call" | custom-call | tf_op jit(solution)/shard_map/pallas_call | solution.py:623
  3.0 4.1 %collective-permute-start = (f32[1,17,8,128]{3,2,1,0:T(8,128)S(1)}, f32[1,17,8,128]{3,2,1,0:T(8,128)S(1)}, u32[]{:S(2)}, u32[]{:S(2)}) collective-permute-start(f32[1,17,8,128]{3,2,1,0:T(8,128)S(1)} %get-tuple-element.31), channel_id=1, source_target_pairs={{0,16},{4,20},{8,24},{12,28},{16,0},{20,4},{24,8},{28,12},{1,17},{... | collective-permute-start | bytes 208904 | tf_op jit(solution)/shard_map/ppermute | solution.py:655
  7.1 1.5 %collective-permute-start.1 = (f32[1,17,8,128]{3,2,1,0:T(8,128)S(1)}, f32[1,17,8,128]{3,2,1,0:T(8,128)S(1)}, u32[]{:S(2)}, u32[]{:S(2)}) collective-permute-start(f32[1,17,8,128]{3,2,1,0:T(8,128)S(1)} %get-tuple-element.32), channel_id=1, source_target_pairs={{0,4},{4,0},{8,12},{12,8},{16,20},{20,16},{24,28},{28,24},{1,5},{5... | collective-permute-start | bytes 208904 | tf_op jit(solution)/shard_map/ppermute | solution.py:655
  8.6 0.0 collective-permute-start.2
  8.6 1.8 %collective-permute-start.3 = (f32[1,17,8,128]{3,2,1,0:T(8,128)S(1)}, f32[1,17,8,128]{3,2,1,0:T(8,128)S(1)}, u32[]{:S(2)}, u32[]{:S(2)}) collective-permute-start(f32[1,17,8,128]{3,2,1,0:T(8,128)S(1)} %get-tuple-element.34), channel_id=1, source_target_pairs={{0,8},{4,12},{8,0},{12,4},{16,24},{20,28},{24,16},{28,20},{1,9},{5... | collective-permute-start | bytes 208904 | tf_op jit(solution)/shard_map/ppermute | solution.py:655
  10.5 2.5 %collective-permute-start.4 = (f32[1,17,8,128]{3,2,1,0:T(8,128)S(1)}, f32[1,17,8,128]{3,2,1,0:T(8,128)S(1)}, u32[]{:S(2)}, u32[]{:S(2)}) collective-permute-start(f32[1,17,8,128]{3,2,1,0:T(8,128)S(1)} %get-tuple-element.35), channel_id=1, source_target_pairs={{0,24},{4,28},{8,16},{12,20},{16,8},{20,12},{24,0},{28,4},{1,25},{... | collective-permute-start | bytes 208904 | tf_op jit(solution)/shard_map/ppermute | solution.py:655
  13.0 0.0 collective-permute-done.refs_1_
  13.0 1.6 %collective-permute-start.5 = (f32[1,17,8,128]{3,2,1,0:T(8,128)S(1)}, f32[1,17,8,128]{3,2,1,0:T(8,128)S(1)}, u32[]{:S(2)}, u32[]{:S(2)}) collective-permute-start(f32[1,17,8,128]{3,2,1,0:T(8,128)S(1)} %get-tuple-element.36), channel_id=1, source_target_pairs={{0,12},{4,8},{8,4},{12,0},{16,28},{20,24},{24,20},{28,16},{1,13},{... | collective-permute-start | bytes 208904 | tf_op jit(solution)/shard_map/ppermute | solution.py:655
  14.6 0.0 collective-permute-done.1.refs_2_
  14.6 2.7 %collective-permute-start.6 = (f32[1,17,8,128]{3,2,1,0:T(8,128)S(1)}, f32[1,17,8,128]{3,2,1,0:T(8,128)S(1)}, u32[]{:S(2)}, u32[]{:S(2)}) collective-permute-start(f32[1,17,8,128]{3,2,1,0:T(8,128)S(1)} %get-tuple-element.37), channel_id=1, source_target_pairs={{0,28},{4,24},{8,20},{12,16},{16,12},{20,8},{24,4},{28,0},{1,29},{... | collective-permute-start | bytes 208904 | tf_op jit(solution)/shard_map/ppermute | solution.py:655
  17.3 2.4 %shard_map.135.refs_0_ = f32[8,16,8,128]{3,2,1,0:T(8,128)} custom-call(s32[64]{0:T(128)S(1)} %get-tuple-element.46.chosen_ref, f32[1,32,8,256]{3,2,1,0:T(8,128)} %var_hbm.1), custom_call_target="tpu_custom_call" | custom-call | tf_op jit(solution)/shard_map/pallas_call | solution.py:659
  19.7 0.0 collective-permute-done.2.refs_3_
  19.7 0.0 collective-permute-done.3.refs_4_
  19.7 0.0 collective-permute-done.4.refs_5_
  19.7 0.0 collective-permute-done.5.refs_6_
  19.7 1.9 %collective-permute-done.6.refs_7_ = f32[1,17,8,128]{3,2,1,0:T(8,128)S(1)} collective-permute-done((f32[1,17,8,128]{3,2,1,0:T(8,128)S(1)}, f32[1,17,8,128]{3,2,1,0:T(8,128)S(1)}, u32[]{:S(2)}, u32[]{:S(2)}) %collective-permute-start.6) | collective-permute-done | bytes 69664 | tf_op jit(solution)/shard_map/ppermute | solution.py:655
  21.6 4.2 %all-to-all-start = ((f32[8,16,8,128]{3,2,1,0:T(8,128)}), f32[8,16,8,128]{3,2,1,0:T(8,128)}, u32[]{:S(2)}, u32[]{:S(2)}) async-start(f32[8,16,8,128]{3,2,1,0:T(8,128)} %shard_map.136), calls=%async_computation | async-start | bytes 1048576 | tf_op jit(solution)/shard_map/all_to_all | solution.py:652
  25.8 2.2 %shard_map.132 = (f32[4,64,256]{2,1,0:T(8,128)S(1)}, f32[104,256]{1,0:T(8,128)S(1)}, f32[104,256]{1,0:T(8,128)S(1)}, s32[64]{0:T(128)S(1)}) custom-call(s32[4]{0:T(128)S(1)} %get-tuple-element.28.warp_ref, f32[8,128]{1,0:T(8,128)S(1)} %get-tuple-element.29.stamp_ref, f32[1,17,8,128]{3,2,1,0:T(8,128)S(1)} %get-tuple-element.30.refs_0_, ...), custom_call_target="tpu_custom_call" | custom-call | tf_op jit(solution)/shard_map/pallas_call | solution.py:671
  27.9 0.7 %collective-permute-start.7 = (f32[104,256]{1,0:T(8,128)S(1)}, f32[104,256]{1,0:T(8,128)S(1)}, u32[]{:S(2)}, u32[]{:S(2)}) collective-permute-start(f32[104,256]{1,0:T(8,128)S(1)} %get-tuple-element.40), channel_id=1, source_target_pairs={{1,2},{2,1},{5,6},{6,5},{9,10},{10,9},{13,14},{14,13},{17,18},{18,... | collective-permute-start | bytes 319496 | tf_op jit(solution)/shard_map/ppermute | solution.py:683
  28.6 2.9 %collective-permute-start.8 = (f32[104,256]{1,0:T(8,128)S(1)}, f32[104,256]{1,0:T(8,128)S(1)}, u32[]{:S(2)}, u32[]{:S(2)}) collective-permute-start(f32[104,256]{1,0:T(8,128)S(1)} %get-tuple-element.41), channel_id=1, source_target_pairs={{0,1},{1,0},{2,3},{3,2},{4,5},{5,4},{6,7},{7,6},{8,9},{9,8},{10,11... | collective-permute-start | bytes 319496 | tf_op jit(solution)/shard_map/ppermute | solution.py:684
  31.5 2.6 %shard_map.133 = (bf16[20,2,256,256]{3,2,1,0:T(8,128)(2,1)S(1)}, f32[64,256]{1,0:T(8,128)S(1)}) custom-call(f32[8,128]{1,0:T(8,128)S(1)} %get-tuple-element.29.stamp_ref, bf16[20,2,256,256]{3,2,1,0:T(8,128)(2,1)} %constant.8.clone.fixed_ref), custom_call_target="tpu_custom_call" | custom-call | tf_op jit(solution)/shard_map/pallas_call | solution.py:689
  34.2 0.0 collective-permute-done.7.far_ref
  34.2 2.9 %shard_map.134 = (f32[64,48,256]{2,1,0:T(8,128)S(1)}, f32[64,256]{1,0:T(8,128)S(1)}, bf16[14,128,256]{2,1,0:T(8,128)(2,1)}, bf16[14,128,256]{2,1,0:T(8,128)(2,1)}, f32[4,96,256]{2,1,0:T(8,128)}) custom-call(f32[4,64,256]{2,1,0:T(8,128)S(1)} %get-tuple-element.39.sci_ref, f32[104,256]{1,0:T(8,128)S(1)} %collective-permute-done.7.far_ref, ...), custom_call_target="tpu_custom_call" | custom-call | tf_op jit(solution)/shard_map/pallas_call | solution.py:696
  37.1 1.6 %all-to-all-done.refs_0_ = f32[8,16,8,128]{3,2,1,0:T(8,128)} async-done(((f32[8,16,8,128]{3,2,1,0:T(8,128)}), f32[8,16,8,128]{3,2,1,0:T(8,128)}, u32[]{:S(2)}, u32[]{:S(2)}) %all-to-all-start) | async-done | bytes 524320 | tf_op jit(solution)/shard_map/all_to_all | solution.py:652
  38.6 4.3 %shard_map.137 = (f32[4,64,256]{2,1,0:T(8,128)S(1)}, f32[176,128]{1,0:T(8,128)S(1)}, f32[176,128]{1,0:T(8,128)S(1)}, f32[96,128]{1,0:T(8,128)S(1)}) custom-call(s32[4]{0:T(128)S(1)} %get-tuple-element.28.warp_ref, s32[64]{0:T(128)S(1)} %get-tuple-element.38.cells_ref, f32[64,256]{1,0:T(8,128)S(1)} %get-tuple-element.44.mask_ref, ...), custom_call_target="tpu_custom_call" | custom-call | tf_op jit(solution)/shard_map/pallas_call | solution.py:708
  43.0 0.1 collective-permute-start.9
  43.1 1.6 %collective-permute-start.11 = (f32[176,128]{1,0:T(8,128)S(1)}, f32[176,128]{1,0:T(8,128)S(1)}, u32[]{:S(2)}, u32[]{:S(2)}) collective-permute-start(f32[176,128]{1,0:T(8,128)S(1)} %get-tuple-element.50), channel_id=1, source_target_pairs={{0,1},{1,0},{2,3},{3,2},{4,5},{5,4},{6,7},{7,6},{8,9},{9,8},{10,11... | collective-permute-start | bytes 270344 | tf_op jit(solution)/shard_map/ppermute | solution.py:726
  44.7 0.5 collective-permute-start.10
  45.2 3.8 %collective-permute-done.10.refs_2_ = f32[96,128]{1,0:T(8,128)S(1)} collective-permute-done((f32[96,128]{1,0:T(8,128)S(1)}, f32[96,128]{1,0:T(8,128)S(1)}, u32[]{:S(2)}, u32[]{:S(2)}) %collective-permute-start.10) | collective-permute-done | bytes 49184 | tf_op jit(solution)/shard_map/ppermute | solution.py:726
  49.0 0.0 collective-permute-done.9.refs_1_
  49.0 0.0 collective-permute-done.11.refs_3_
  49.0 4.5 %shard_map.138 = (f32[4,1,64,256]{3,2,1,0:T(8,128)}, f32[4,1,64,256]{3,2,1,0:T(8,128)}) custom-call(f32[4,64,256]{2,1,0:T(8,128)S(1)} %get-tuple-element.47.var_ref, f32[96,128]{1,0:T(8,128)S(1)} %get-tuple-element.48.refs_0_, f32[176,128]{1,0:T(8,128)S(1)} %collective-permute-done.9.refs_1_, f32[96,128]{1,0:T(8,128)S(1)} %collective-permute-done.10.refs_2_, ...), custom_call_target="tpu_custom_call" | custom-call | tf_op jit(solution)/shard_map/pallas_call | solution.py:731
  (2 shorter events, 0.0 us)
Async XLA Ops:
  3.0 10.0 %collective-permute-start = (f32[1,17,8,128]{3,2,1,0:T(8,128)S(1)}, f32[1,17,8,128]{3,2,1,0:T(8,128)S(1)}, u32[]{:S(2)}, u32[]{:S(2)}) collective-permute-start(f32[1,17,8,128]{3,2,1,0:T(8,128)S(1)} %get-tuple-element.31), channel_id=1, source_target_pairs={{0,16},{4,20},{8,24},{12,28},{16,0},{20,4},{24,8},{28,12},{1,17},{... | collective-permute-start | bytes 208904 | tf_op jit(solution)/shard_map/ppermute | solution.py:655
  7.1 7.5 %collective-permute-start.1 = (f32[1,17,8,128]{3,2,1,0:T(8,128)S(1)}, f32[1,17,8,128]{3,2,1,0:T(8,128)S(1)}, u32[]{:S(2)}, u32[]{:S(2)}) collective-permute-start(f32[1,17,8,128]{3,2,1,0:T(8,128)S(1)} %get-tuple-element.32), channel_id=1, source_target_pairs={{0,4},{4,0},{8,12},{12,8},{16,20},{20,16},{24,28},{28,24},{1,5},{5... | collective-permute-start | bytes 208904 | tf_op jit(solution)/shard_map/ppermute | solution.py:655
  8.6 11.1 %collective-permute-start.2 = (f32[1,17,8,128]{3,2,1,0:T(8,128)S(1)}, f32[1,17,8,128]{3,2,1,0:T(8,128)S(1)}, u32[]{:S(2)}, u32[]{:S(2)}) collective-permute-start(f32[1,17,8,128]{3,2,1,0:T(8,128)S(1)} %get-tuple-element.33), channel_id=1, source_target_pairs={{0,20},{4,16},{8,28},{12,24},{16,4},{20,0},{24,12},{28,8},{1,21},{... | collective-permute-start | bytes 208904 | tf_op jit(solution)/shard_map/ppermute | solution.py:655
  8.6 11.1 %collective-permute-start.3 = (f32[1,17,8,128]{3,2,1,0:T(8,128)S(1)}, f32[1,17,8,128]{3,2,1,0:T(8,128)S(1)}, u32[]{:S(2)}, u32[]{:S(2)}) collective-permute-start(f32[1,17,8,128]{3,2,1,0:T(8,128)S(1)} %get-tuple-element.34), channel_id=1, source_target_pairs={{0,8},{4,12},{8,0},{12,4},{16,24},{20,28},{24,16},{28,20},{1,9},{5... | collective-permute-start | bytes 208904 | tf_op jit(solution)/shard_map/ppermute | solution.py:655
  10.5 9.2 %collective-permute-start.4 = (f32[1,17,8,128]{3,2,1,0:T(8,128)S(1)}, f32[1,17,8,128]{3,2,1,0:T(8,128)S(1)}, u32[]{:S(2)}, u32[]{:S(2)}) collective-permute-start(f32[1,17,8,128]{3,2,1,0:T(8,128)S(1)} %get-tuple-element.35), channel_id=1, source_target_pairs={{0,24},{4,28},{8,16},{12,20},{16,8},{20,12},{24,0},{28,4},{1,25},{... | collective-permute-start | bytes 208904 | tf_op jit(solution)/shard_map/ppermute | solution.py:655
  13.0 6.8 %collective-permute-start.5 = (f32[1,17,8,128]{3,2,1,0:T(8,128)S(1)}, f32[1,17,8,128]{3,2,1,0:T(8,128)S(1)}, u32[]{:S(2)}, u32[]{:S(2)}) collective-permute-start(f32[1,17,8,128]{3,2,1,0:T(8,128)S(1)} %get-tuple-element.36), channel_id=1, source_target_pairs={{0,12},{4,8},{8,4},{12,0},{16,28},{20,24},{24,20},{28,16},{1,13},{... | collective-permute-start | bytes 208904 | tf_op jit(solution)/shard_map/ppermute | solution.py:655
  14.6 7.0 %collective-permute-start.6 = (f32[1,17,8,128]{3,2,1,0:T(8,128)S(1)}, f32[1,17,8,128]{3,2,1,0:T(8,128)S(1)}, u32[]{:S(2)}, u32[]{:S(2)}) collective-permute-start(f32[1,17,8,128]{3,2,1,0:T(8,128)S(1)} %get-tuple-element.37), channel_id=1, source_target_pairs={{0,28},{4,24},{8,20},{12,16},{16,12},{20,8},{24,4},{28,0},{1,29},{... | collective-permute-start | bytes 208904 | tf_op jit(solution)/shard_map/ppermute | solution.py:655
  21.6 17.0 %all-to-all-start = ((f32[8,16,8,128]{3,2,1,0:T(8,128)}), f32[8,16,8,128]{3,2,1,0:T(8,128)}, u32[]{:S(2)}, u32[]{:S(2)}) async-start(f32[8,16,8,128]{3,2,1,0:T(8,128)} %shard_map.136), calls=%async_computation | async-start | bytes 1048576 | tf_op jit(solution)/shard_map/all_to_all | solution.py:652
  27.9 6.2 %collective-permute-start.7 = (f32[104,256]{1,0:T(8,128)S(1)}, f32[104,256]{1,0:T(8,128)S(1)}, u32[]{:S(2)}, u32[]{:S(2)}) collective-permute-start(f32[104,256]{1,0:T(8,128)S(1)} %get-tuple-element.40), channel_id=1, source_target_pairs={{1,2},{2,1},{5,6},{6,5},{9,10},{10,9},{13,14},{14,13},{17,18},{18,... | collective-permute-start | bytes 319496 | tf_op jit(solution)/shard_map/ppermute | solution.py:683
  28.6 5.6 %collective-permute-start.8 = (f32[104,256]{1,0:T(8,128)S(1)}, f32[104,256]{1,0:T(8,128)S(1)}, u32[]{:S(2)}, u32[]{:S(2)}) collective-permute-start(f32[104,256]{1,0:T(8,128)S(1)} %get-tuple-element.41), channel_id=1, source_target_pairs={{0,1},{1,0},{2,3},{3,2},{4,5},{5,4},{6,7},{7,6},{8,9},{9,8},{10,11... | collective-permute-start | bytes 319496 | tf_op jit(solution)/shard_map/ppermute | solution.py:684
  43.0 6.0 %collective-permute-start.9 = (f32[176,128]{1,0:T(8,128)S(1)}, f32[176,128]{1,0:T(8,128)S(1)}, u32[]{:S(2)}, u32[]{:S(2)}) collective-permute-start(f32[176,128]{1,0:T(8,128)S(1)} %get-tuple-element.49), channel_id=1, source_target_pairs={{0,3},{1,2},{2,1},{3,0},{4,7},{5,6},{6,5},{7,4},{8,11},{9,10},{10,... | collective-permute-start | bytes 270344 | tf_op jit(solution)/shard_map/ppermute | solution.py:726
  43.1 6.0 %collective-permute-start.11 = (f32[176,128]{1,0:T(8,128)S(1)}, f32[176,128]{1,0:T(8,128)S(1)}, u32[]{:S(2)}, u32[]{:S(2)}) collective-permute-start(f32[176,128]{1,0:T(8,128)S(1)} %get-tuple-element.50), channel_id=1, source_target_pairs={{0,1},{1,0},{2,3},{3,2},{4,5},{5,4},{6,7},{7,6},{8,9},{9,8},{10,11... | collective-permute-start | bytes 270344 | tf_op jit(solution)/shard_map/ppermute | solution.py:726
  44.7 4.4 %collective-permute-start.10 = (f32[96,128]{1,0:T(8,128)S(1)}, f32[96,128]{1,0:T(8,128)S(1)}, u32[]{:S(2)}, u32[]{:S(2)}) collective-permute-start(f32[96,128]{1,0:T(8,128)S(1)} %get-tuple-element.48.refs_0_), channel_id=1, source_target_pairs={{0,2},{1,3},{2,0},{3,1},{4,6},{5,7},{6,4},{7,5},{8,10},{9,11},{10,... | collective-permute-start | bytes 147464 | tf_op jit(solution)/shard_map/ppermute | solution.py:726

commit v4 on v3

--- a/solution.py
+++ b/solution.py
@@ -31,8 +31,15 @@
 WINDOW = 64
 VMEM_BYTES = 20 * 1024 * 1024
 
-TILES = ((0, (0, 2)), (0, (1, 3, 4)), (1, (0, 2)), (1, (1, 3, 4)), (2, (0, 1, 3)), (2, (2,)))
-SLOTS = 8 * len(TILES)
+TILES = (
+    ((0, 0, range(5)), (0, 2, range(3))),
+    ((0, 1, range(4)), (0, 3, range(2)), (0, 4, range(1)), (2, 2, range(1))),
+    ((1, 0, range(5)), (1, 2, range(3))),
+    ((1, 1, range(4)), (1, 3, range(2)), (1, 4, range(1)), (2, 2, range(1, 2))),
+    ((2, 0, range(4)), (2, 1, range(3)), (2, 3, range(1))),
+)
+BASIS = 8 * len(TILES)
+SLOTS = BASIS + 8
 HALF = 64
 TAP_FIRST = (0, DEGREES[0] + 1, DEGREES[0] + DEGREES[1] + 2)
 TAP_COUNT = sum(DEGREES) + len(DEGREES)
@@ -40,17 +47,14 @@
 
 def slot_table():
     result = {}
-    for tile, (group, columns) in enumerate(TILES):
-        slot = 8 * tile
-        for column in columns:
-            for row in range(DEGREES[group] + 1 - column):
-                result[slot] = (TAP_FIRST[group] + row, TAP_FIRST[group] + column)
-                slot += 1
+    for tile, entries in enumerate(TILES):
+        taps = [(TAP_FIRST[group] + row, TAP_FIRST[group] + column) for group, column, rows in entries for row in rows]
+        result.update({8 * tile + place: pair for place, pair in enumerate(taps)})
     return result
 
 
 SLOT_TAPS = slot_table()
-ONE_SLOT = 8 * (len(TILES) - 1) + 2
+ONE_SLOT = BASIS
 SCI_SLOT = ONE_SLOT + 1
 LIVE_SLOTS = sorted(SLOT_TAPS) + [ONE_SLOT]
 
@@ -89,30 +93,19 @@
     return high, low
 
 
-def tile_depth(tile, visits):
-    depth = len(TILES[tile][1]) * WINDOW
-    return depth + visits * BLOCK + 16 if tile == len(TILES) - 1 else depth
-
-
 @functools.lru_cache(maxsize=None)
 def constants(visits, row_count, col_count):
     taps = basis_taps()
     column_bands = np.stack([band(taps[t], col_count, col_count, 0).T for t in range(TAP_COUNT)])
     toeplitz = np.stack([band(taps[t], BLOCK, WINDOW, EDGE) for t in range(TAP_COUNT)])
     row_parts = []
-    for tile, (group, columns) in enumerate(TILES):
-        matrix = np.zeros((BLOCK, 8, tile_depth(tile, visits)))
+    for entries in TILES:
+        matrix = np.zeros((BLOCK, 8, len(entries) * WINDOW))
         slot = 0
-        for place, column in enumerate(columns):
-            for row in range(DEGREES[group] + 1 - column):
+        for place, (group, _, rows) in enumerate(entries):
+            for row in rows:
                 matrix[:, slot, place * WINDOW : (place + 1) * WINDOW] = toeplitz[TAP_FIRST[group] + row]
                 slot += 1
-        if tile == len(TILES) - 1:
-            base = len(columns) * WINDOW
-            for visit in range(visits):
-                first = base + visit * BLOCK
-                matrix[np.arange(BLOCK), slot + 1 + visit, first + np.arange(BLOCK)] = 1.0
-            matrix[:, slot, base + visits * BLOCK] = 1.0
         row_parts.append(matrix.reshape(BLOCK * 8, -1))
     depth = col_count
     for tile, part in enumerate(row_parts):
@@ -330,19 +323,11 @@
     copies = start_copies(((high_ref, high_out), (low_ref, low_out), (wide_ref, wide_out)), sems)
     for block in range(row_count // BLOCK):
         start = EDGE + block * BLOCK
-        for tile, (group, columns) in enumerate(TILES):
-            depth = tile_depth(tile, visits)
-            rows = [held_ref[TAP_COUNT + tile, half, :, :depth] for half in range(2)]
-            taps = [TAP_FIRST[group] + column for column in columns]
+        for tile, entries in enumerate(TILES):
+            rows = [held_ref[TAP_COUNT + tile, half, :, : len(entries) * WINDOW] for half in range(2)]
+            taps = [TAP_FIRST[group] + column for group, column, _ in entries]
             high = [high_ref[tap, start : start + WINDOW] for tap in taps]
             low = [low_ref[tap, start : start + WINDOW] for tap in taps]
-            if tile == len(TILES) - 1:
-                for visit in range(visits):
-                    pair = split(sci_ref[visit, block * BLOCK : (block + 1) * BLOCK])
-                    high.append(pair[0])
-                    low.append(pair[1])
-                high.append(jnp.ones((16, col_count), BF16))
-                low.append(jnp.zeros((16, col_count), BF16))
             both = mul(jnp.concatenate(rows, axis=0), jnp.concatenate(high, axis=0))
             part = both[: 8 * BLOCK] + both[8 * BLOCK :] + mul(rows[0], jnp.concatenate(low, axis=0))
             design_ref[block * BLOCK : (block + 1) * BLOCK, 8 * tile : 8 * tile + 8] = part.reshape(
@@ -357,7 +342,7 @@
         copy.wait()
 
 
-def gram_kernel(cfg, warp_ref, cells_ref, mask_ref, design_ref, *refs):
+def gram_kernel(cfg, warp_ref, cells_ref, mask_ref, sci_ref, design_ref, *refs):
     patches, capacity, visits, row_count, col_count, block_count, step = cfg
     blocks = refs[:block_count]
     var_ref, near_ref, far_ref, gram_ref, total_ref, weight_ref, sum_ref = refs[block_count:]
@@ -374,23 +359,23 @@
         weight_ref[visit] = mask / (var_ref[visit] + shared)
     sum_ref[...] = jnp.zeros(sum_ref.shape, F32)
 
-    body_rows, tail = 8 * (len(TILES) - 1), ONE_SLOT % 8 + 1
-    rows = visits * body_rows + visits // 2 * 8
+    rows = visits * BASIS + visits // 2 * 8
     kept = 2 * LANES - 2 * SLOTS - 16
-    at_first = lax.broadcasted_iota(jnp.int32, (8, col_count), 0) < tail
+    line = lax.broadcasted_iota(jnp.int32, (8, col_count), 0)
 
     def body(number, carry):
         left, right = [], []
         for extra in range(step):
             row = number * step + extra
             design = design_ref[row]
-            high, low = split(design)
+            last = jnp.ones((8, col_count), F32)
+            for visit in range(visits):
+                last = jnp.where(line == SCI_SLOT - BASIS + visit, sci_ref[visit, pl.ds(row, 1), :], last)
+            high, low = split(jnp.concatenate([design, last], axis=0))
             weights = [weight_ref[visit, pl.ds(row, 1), :] for visit in range(visits)]
-            scaled = [design[:body_rows] * weight for weight in weights]
-            last = design[body_rows:]
-            moved = pltpu.roll(last, tail, 0)
+            scaled = [design * weight for weight in weights]
             for pair in range(visits // 2):
-                scaled.append(jnp.where(at_first, last * weights[2 * pair], moved * weights[2 * pair + 1]))
+                scaled.append(jnp.where(line == 0, weights[2 * pair], weights[2 * pair + 1]))
             scaled_high, scaled_low = split(jnp.concatenate(scaled, axis=0))
             blank = jnp.zeros((16, col_count), BF16)
             right.append(jnp.concatenate([high, low, scaled_low[:kept], blank], axis=0))
@@ -407,10 +392,10 @@
     main = main + jnp.concatenate([turned, sum_ref[rows + SLOTS :, :LANES]], axis=0)
     lane = lax.broadcasted_iota(jnp.int32, (SLOTS, 2 * HALF), 1)
     for pair in range(visits // 2):
-        ends = main[visits * body_rows + 8 * pair :][:8]
+        ends = main[visits * BASIS + 8 * pair :][:8]
         both = []
-        for visit, end in ((2 * pair, ends), (2 * pair + 1, pltpu.roll(ends, 8 - tail, 0))):
-            both.append(jnp.concatenate([main[visit * body_rows : (visit + 1) * body_rows], end], axis=0))
+        for visit, end in ((2 * pair, ends), (2 * pair + 1, pltpu.roll(ends, 7, 0))):
+            both.append(jnp.concatenate([main[visit * BASIS : (visit + 1) * BASIS], end], axis=0))
         value = jnp.where(lane < HALF, both[0], pltpu.roll(both[1], HALF, 1))
         for ref in (gram_ref, near_ref, far_ref):
             ref[pair * SLOTS : (pair + 1) * SLOTS] = value
@@ -476,10 +461,10 @@
         diagonal = (lane == line) | (lane == line + HALF)
         systems.append(total + jnp.where(diagonal, RIDGE * total + RIDGE * EPS * normalizer, 0.0))
     pairs = range(visits // 2)
-    tiles = [[matrix[8 * part : 8 * part + 8] for part in range(len(TILES))] for matrix in systems]
+    tiles = [[matrix[8 * part : 8 * part + 8] for part in range(SLOTS // 8)] for matrix in systems]
     line, lane = line[:8], lane[:8]
-    for panel in range(len(TILES)):
-        if panel == len(TILES) // 2:
+    for panel in range(SLOTS // 8):
+        if panel == 3:
             for copy in copies[:3]:
                 copy.wait()
             noise = detected(inverse, 2)
@@ -695,7 +680,7 @@
     )(stamps, in_hbm(design_fixed))
     design, mask, high, low, wide_science = call(
         functools.partial(design_kernel, (visits, row_count, col_count)),
-        [sds((row_count, SLOTS, col_count), F32), plane] + [pltpu.HBM(part.shape, part.dtype) for part in (field, field, wide)],
+        [sds((row_count, BASIS, col_count), F32), plane] + [pltpu.HBM(part.shape, part.dtype) for part in (field, field, wide)],
         [vmem()] * 2 + [far()] * 3,
         [vmem()] * 5,
         [pltpu.VMEM(part.shape, part.dtype) for part in (field, field, wide)] + [pltpu.SemaphoreType.DMA((3,))],
@@ -704,7 +689,7 @@
     gram_rows = visits // 2 * SLOTS
     tail_rows = visits * PR * (col_count // LANES)
     step = 32
-    gram_depth = 2 * visits * (8 * len(TILES) - 4) + 3 * SLOTS + 16 - 2 * LANES
+    gram_depth = 2 * visits * (BASIS + 4) + 3 * SLOTS + 16 - 2 * LANES
     variance, to_near, to_far, gram = call(
         functools.partial(gram_kernel, (patches, capacity, visits, row_count, col_count, var_blocks, step)),
         [
@@ -714,13 +699,13 @@
             sds((gram_rows, LANES), F32),
         ],
         [vmem()] * 4,
-        [smem(), smem(), vmem(), vmem()] + [vmem()] * var_blocks,
+        [smem(), smem()] + [vmem()] * (3 + var_blocks),
         [
             pltpu.VMEM((visits * NCELL + 1, 2, 8, LANES), F32),
             pltpu.VMEM((visits, row_count, col_count), F32),
             pltpu.VMEM((gram_depth, 2 * LANES), F32),
         ],
-    )(warps, cells, mask, design, *got_var)
+    )(warps, cells, mask, science, design, *got_var)
     grams = [gram]
     for away, part in ((3, to_far), (2, gram), (1, to_near)):
         grams.append(lax.ppermute(part, "sub", [(i, i ^ away) for i in range(subtiles)]))

time: 53.9 us -> 53 us (0.983)
  waiting for transfers between devices: 7.29 us -> 6.5 us
    all_to_all x1, waiting for transfers between devices: 1.57 us -> 0.76 us  [route(): lax.all_to_all(blocks[0], 'patch', split_axis=0, concat_axis=0, tiled=True)]
  transfers between devices with their start and end apart: 13 -> 13, of which waited for: 3 -> 3; matrix products, arithmetic and copies ran while one was open for 0% -> 0% of each run, Pallas kernels for 19% -> 20%
where the time goes in v4:
time: 53 us; the launch traced here: 52.7 us
  starting transfers between devices  24.2 us (46%)
  Pallas kernels  20.6 us (39%)
  waiting for transfers between devices  6.5 us (12%)
  between operations  1.39 us (3%)
    ppermute x7, starting transfers between devices, route(): lax.ppermute(block, 'patch', [(i, i ^ away) for i in range(patches)])  14.3 us
    pallas_call x1, Pallas kernels, local(): call(functools.partial(solve_kernel, (visits, row_count, col_count, subti...  4.49 us
    all_to_all x1, starting transfers between devices, route(): lax.all_to_all(blocks[0], 'patch', split_axis=0, concat_axis=0, tiled=True)  4.12 us
    pallas_call x1, Pallas kernels, local(): call(functools.partial(gram_kernel, (patches, capacity, visits, row_count...  3.94 us
    ppermute x3, waiting for transfers between devices, local(): lax.ppermute(part, 'sub', [(i, i ^ away) for i in range(subtiles)])  3.84 us
    pallas_call x1, Pallas kernels, local(): call(functools.partial(design_kernel, (visits, row_count, col_count)), [s...  3.3 us
    ppermute x1, starting transfers between devices, local(): lax.ppermute(to_near, 'sub', [(i, i ^ 1) for i in range(subtiles)])  2.92 us
    pallas_call x1, Pallas kernels, local(): call(functools.partial(fetch_kernel, (row_count, col_count)), [sds(design...  2.54 us
  transfers between devices with their start and end apart: 13, of which 3 were waited for; matrix products, arithmetic and copies ran while one was open for 0% of the time, Pallas kernels for 20%

profile of v4, /device:TPU:0, one launch (start us, length us, event | category | flops | bytes accessed | tf_op | source)
XLA Modules:
  0.0 52.7 jit_solution(2801476837476909515)
XLA Ops:
  1.3 1.7 %shard_map.131 = (f32[1,17,8,128]{3,2,1,0:T(8,128)S(1)}, f32[1,17,8,128]{3,2,1,0:T(8,128)S(1)}, f32[1,17,8,128]{3,2,1,0:T(8,128)S(1)}, f32[1,17,8,128]{3,2,1,0:T...) custom-call(s32[1,32]{1,0:T(1,128)} %bitcast.1, ...), custom_call_target="tpu_custom_call" | custom-call | tf_op jit(solution)/shard_map/pallas_call | solution.py:608
  3.0 4.1 %collective-permute-start = (f32[1,17,8,128]{3,2,1,0:T(8,128)S(1)}, f32[1,17,8,128]{3,2,1,0:T(8,128)S(1)}, u32[]{:S(2)}, u32[]{:S(2)}) collective-permute-start(f32[1,17,8,128]{3,2,1,0:T(8,128)S(1)} %get-tuple-element.31), channel_id=1, source_target_pairs={{0,16},{4,20},{8,24},{12,28},{16,0},{20,4},{24,8},{28,12},{1,17},{... | collective-permute-start | bytes 208904 | tf_op jit(solution)/shard_map/ppermute | solution.py:640
  7.1 1.5 %collective-permute-start.1 = (f32[1,17,8,128]{3,2,1,0:T(8,128)S(1)}, f32[1,17,8,128]{3,2,1,0:T(8,128)S(1)}, u32[]{:S(2)}, u32[]{:S(2)}) collective-permute-start(f32[1,17,8,128]{3,2,1,0:T(8,128)S(1)} %get-tuple-element.32), channel_id=1, source_target_pairs={{0,4},{4,0},{8,12},{12,8},{16,20},{20,16},{24,28},{28,24},{1,5},{5... | collective-permute-start | bytes 208904 | tf_op jit(solution)/shard_map/ppermute | solution.py:640
  8.6 0.0 collective-permute-start.2
  8.6 1.8 %collective-permute-start.3 = (f32[1,17,8,128]{3,2,1,0:T(8,128)S(1)}, f32[1,17,8,128]{3,2,1,0:T(8,128)S(1)}, u32[]{:S(2)}, u32[]{:S(2)}) collective-permute-start(f32[1,17,8,128]{3,2,1,0:T(8,128)S(1)} %get-tuple-element.34), channel_id=1, source_target_pairs={{0,8},{4,12},{8,0},{12,4},{16,24},{20,28},{24,16},{28,20},{1,9},{5... | collective-permute-start | bytes 208904 | tf_op jit(solution)/shard_map/ppermute | solution.py:640
  10.5 2.5 %collective-permute-start.4 = (f32[1,17,8,128]{3,2,1,0:T(8,128)S(1)}, f32[1,17,8,128]{3,2,1,0:T(8,128)S(1)}, u32[]{:S(2)}, u32[]{:S(2)}) collective-permute-start(f32[1,17,8,128]{3,2,1,0:T(8,128)S(1)} %get-tuple-element.35), channel_id=1, source_target_pairs={{0,24},{4,28},{8,16},{12,20},{16,8},{20,12},{24,0},{28,4},{1,25},{... | collective-permute-start | bytes 208904 | tf_op jit(solution)/shard_map/ppermute | solution.py:640
  13.0 0.0 collective-permute-done.refs_1_
  13.0 1.6 %collective-permute-start.5 = (f32[1,17,8,128]{3,2,1,0:T(8,128)S(1)}, f32[1,17,8,128]{3,2,1,0:T(8,128)S(1)}, u32[]{:S(2)}, u32[]{:S(2)}) collective-permute-start(f32[1,17,8,128]{3,2,1,0:T(8,128)S(1)} %get-tuple-element.36), channel_id=1, source_target_pairs={{0,12},{4,8},{8,4},{12,0},{16,28},{20,24},{24,20},{28,16},{1,13},{... | collective-permute-start | bytes 208904 | tf_op jit(solution)/shard_map/ppermute | solution.py:640
  14.6 0.0 collective-permute-done.1.refs_2_
  14.6 2.7 %collective-permute-start.6 = (f32[1,17,8,128]{3,2,1,0:T(8,128)S(1)}, f32[1,17,8,128]{3,2,1,0:T(8,128)S(1)}, u32[]{:S(2)}, u32[]{:S(2)}) collective-permute-start(f32[1,17,8,128]{3,2,1,0:T(8,128)S(1)} %get-tuple-element.37), channel_id=1, source_target_pairs={{0,28},{4,24},{8,20},{12,16},{16,12},{20,8},{24,4},{28,0},{1,29},{... | collective-permute-start | bytes 208904 | tf_op jit(solution)/shard_map/ppermute | solution.py:640
  17.3 2.3 %shard_map.135.refs_0_ = f32[8,16,8,128]{3,2,1,0:T(8,128)} custom-call(s32[64]{0:T(128)S(1)} %get-tuple-element.46.chosen_ref, f32[1,32,8,256]{3,2,1,0:T(8,128)} %var_hbm.1), custom_call_target="tpu_custom_call" | custom-call | tf_op jit(solution)/shard_map/pallas_call | solution.py:644
  19.7 0.0 collective-permute-done.2.refs_3_
  19.7 0.0 collective-permute-done.3.refs_4_
  19.7 0.0 collective-permute-done.4.refs_5_
  19.7 0.0 collective-permute-done.5.refs_6_
  19.7 1.9 %collective-permute-done.6.refs_7_ = f32[1,17,8,128]{3,2,1,0:T(8,128)S(1)} collective-permute-done((f32[1,17,8,128]{3,2,1,0:T(8,128)S(1)}, f32[1,17,8,128]{3,2,1,0:T(8,128)S(1)}, u32[]{:S(2)}, u32[]{:S(2)}) %collective-permute-start.6) | collective-permute-done | bytes 69664 | tf_op jit(solution)/shard_map/ppermute | solution.py:640
  21.6 4.1 %all-to-all-start = ((f32[8,16,8,128]{3,2,1,0:T(8,128)}), f32[8,16,8,128]{3,2,1,0:T(8,128)S(1)}, u32[]{:S(2)}, u32[]{:S(2)}) async-start(f32[8,16,8,128]{3,2,1,0:T(8,128)} %shard_map.136), calls=%async_computation | async-start | bytes 1048576 | tf_op jit(solution)/shard_map/all_to_all | solution.py:637
  25.7 2.3 %shard_map.132 = (f32[4,64,256]{2,1,0:T(8,128)S(1)}, f32[104,256]{1,0:T(8,128)S(1)}, f32[104,256]{1,0:T(8,128)S(1)}, s32[64]{0:T(128)S(1)}) custom-call(s32[4]{0:T(128)S(1)} %get-tuple-element.28.warp_ref, f32[8,128]{1,0:T(8,128)S(1)} %get-tuple-element.29.stamp_ref, f32[1,17,8,128]{3,2,1,0:T(8,128)S(1)} %get-tuple-element.30.refs_0_, ...), custom_call_target="tpu_custom_call" | custom-call | tf_op jit(solution)/shard_map/pallas_call | solution.py:656
  28.0 0.7 %collective-permute-start.7 = (f32[104,256]{1,0:T(8,128)S(1)}, f32[104,256]{1,0:T(8,128)S(1)}, u32[]{:S(2)}, u32[]{:S(2)}) collective-permute-start(f32[104,256]{1,0:T(8,128)S(1)} %get-tuple-element.40), channel_id=1, source_target_pairs={{1,2},{2,1},{5,6},{6,5},{9,10},{10,9},{13,14},{14,13},{17,18},{18,... | collective-permute-start | bytes 319496 | tf_op jit(solution)/shard_map/ppermute | solution.py:668
  28.7 2.9 %collective-permute-start.8 = (f32[104,256]{1,0:T(8,128)S(1)}, f32[104,256]{1,0:T(8,128)S(1)}, u32[]{:S(2)}, u32[]{:S(2)}) collective-permute-start(f32[104,256]{1,0:T(8,128)S(1)} %get-tuple-element.41), channel_id=1, source_target_pairs={{0,1},{1,0},{2,3},{3,2},{4,5},{5,4},{6,7},{7,6},{8,9},{9,8},{10,11... | collective-permute-start | bytes 319496 | tf_op jit(solution)/shard_map/ppermute | solution.py:669
  31.6 2.5 %shard_map.133 = (bf16[19,2,256,256]{3,2,1,0:T(8,128)(2,1)S(1)}, f32[64,256]{1,0:T(8,128)S(1)}) custom-call(f32[8,128]{1,0:T(8,128)S(1)} %get-tuple-element.29.stamp_ref, bf16[19,2,256,256]{3,2,1,0:T(8,128)(2,1)} %constant.8.clone.fixed_ref), custom_call_target="tpu_custom_call" | custom-call | tf_op jit(solution)/shard_map/pallas_call | solution.py:674
  34.1 0.0 collective-permute-done.7.far_ref
  34.1 0.0 collective-permute-done.8.near_ref
  34.2 3.3 %shard_map.134 = (f32[64,40,256]{2,1,0:T(8,128)S(1)}, f32[64,256]{1,0:T(8,128)S(1)}, bf16[14,128,256]{2,1,0:T(8,128)(2,1)}, bf16[14,128,256]{2,1,0:T(8,128)(2,1)}, f32[4,96,256]{2,1,0:T(8,128)}) custom-call(f32[4,64,256]{2,1,0:T(8,128)S(1)} %get-tuple-element.39.sci_ref, f32[104,256]{1,0:T(8,128)S(1)} %collective-permute-done.7.far_ref, ...), custom_call_target="tpu_custom_call" | custom-call | tf_op jit(solution)/shard_map/pallas_call | solution.py:681
  37.5 0.8 %all-to-all-done.refs_0_ = f32[8,16,8,128]{3,2,1,0:T(8,128)S(1)} async-done(((f32[8,16,8,128]{3,2,1,0:T(8,128)}), f32[8,16,8,128]{3,2,1,0:T(8,128)S(1)}, u32[]{:S(2)}, u32[]{:S(2)}) %all-to-all-start) | async-done | bytes 524320 | tf_op jit(solution)/shard_map/all_to_all | solution.py:637
  38.2 3.9 %shard_map.137 = (f32[4,64,256]{2,1,0:T(8,128)S(1)}, f32[176,128]{1,0:T(8,128)S(1)}, f32[176,128]{1,0:T(8,128)S(1)}, f32[96,128]{1,0:T(8,128)S(1)}) custom-call(s32[4]{0:T(128)S(1)} %get-tuple-element.28.warp_ref, s32[64]{0:T(128)S(1)} %get-tuple-element.38.cells_ref, f32[64,256]{1,0:T(8,128)S(1)} %get-tuple-element.44.mask_ref, ...), custom_call_target="tpu_custom_call" | custom-call | tf_op jit(solution)/shard_map/pallas_call | solution.py:693
  42.2 0.1 collective-permute-start.9
  42.2 1.6 %collective-permute-start.11 = (f32[176,128]{1,0:T(8,128)S(1)}, f32[176,128]{1,0:T(8,128)S(1)}, u32[]{:S(2)}, u32[]{:S(2)}) collective-permute-start(f32[176,128]{1,0:T(8,128)S(1)} %get-tuple-element.50), channel_id=1, source_target_pairs={{0,1},{1,0},{2,3},{3,2},{4,5},{5,4},{6,7},{7,6},{8,9},{9,8},{10,11... | collective-permute-start | bytes 270344 | tf_op jit(solution)/shard_map/ppermute | solution.py:711
  43.8 0.5 %collective-permute-start.10 = (f32[96,128]{1,0:T(8,128)S(1)}, f32[96,128]{1,0:T(8,128)S(1)}, u32[]{:S(2)}, u32[]{:S(2)}) collective-permute-start(f32[96,128]{1,0:T(8,128)S(1)} %get-tuple-element.48.refs_0_), channel_id=1, source_target_pairs={{0,2},{1,3},{2,0},{3,1},{4,6},{5,7},{6,4},{7,5},{8,10},{9,11},{10,... | collective-permute-start | bytes 147464 | tf_op jit(solution)/shard_map/ppermute | solution.py:711
  44.4 3.8 %collective-permute-done.10.refs_2_ = f32[96,128]{1,0:T(8,128)S(1)} collective-permute-done((f32[96,128]{1,0:T(8,128)S(1)}, f32[96,128]{1,0:T(8,128)S(1)}, u32[]{:S(2)}, u32[]{:S(2)}) %collective-permute-start.10) | collective-permute-done | bytes 49184 | tf_op jit(solution)/shard_map/ppermute | solution.py:711
  48.2 0.0 collective-permute-done.9.refs_1_
  48.2 4.5 %shard_map.138 = (f32[4,1,64,256]{3,2,1,0:T(8,128)}, f32[4,1,64,256]{3,2,1,0:T(8,128)}) custom-call(f32[4,64,256]{2,1,0:T(8,128)S(1)} %get-tuple-element.47.var_ref, f32[96,128]{1,0:T(8,128)S(1)} %get-tuple-element.48.refs_0_, f32[176,128]{1,0:T(8,128)S(1)} %collective-permute-done.9.refs_1_, f32[96,128]{1,0:T(8,128)S(1)} %collective-permute-done.10.refs_2_, ...), custom_call_target="tpu_custom_call" | custom-call | tf_op jit(solution)/shard_map/pallas_call | solution.py:716
  (2 shorter events, 0.0 us)
Async XLA Ops:
  3.0 10.0 %collective-permute-start = (f32[1,17,8,128]{3,2,1,0:T(8,128)S(1)}, f32[1,17,8,128]{3,2,1,0:T(8,128)S(1)}, u32[]{:S(2)}, u32[]{:S(2)}) collective-permute-start(f32[1,17,8,128]{3,2,1,0:T(8,128)S(1)} %get-tuple-element.31), channel_id=1, source_target_pairs={{0,16},{4,20},{8,24},{12,28},{16,0},{20,4},{24,8},{28,12},{1,17},{... | collective-permute-start | bytes 208904 | tf_op jit(solution)/shard_map/ppermute | solution.py:640
  7.1 7.5 %collective-permute-start.1 = (f32[1,17,8,128]{3,2,1,0:T(8,128)S(1)}, f32[1,17,8,128]{3,2,1,0:T(8,128)S(1)}, u32[]{:S(2)}, u32[]{:S(2)}) collective-permute-start(f32[1,17,8,128]{3,2,1,0:T(8,128)S(1)} %get-tuple-element.32), channel_id=1, source_target_pairs={{0,4},{4,0},{8,12},{12,8},{16,20},{20,16},{24,28},{28,24},{1,5},{5... | collective-permute-start | bytes 208904 | tf_op jit(solution)/shard_map/ppermute | solution.py:640
  8.6 11.1 %collective-permute-start.2 = (f32[1,17,8,128]{3,2,1,0:T(8,128)S(1)}, f32[1,17,8,128]{3,2,1,0:T(8,128)S(1)}, u32[]{:S(2)}, u32[]{:S(2)}) collective-permute-start(f32[1,17,8,128]{3,2,1,0:T(8,128)S(1)} %get-tuple-element.33), channel_id=1, source_target_pairs={{0,20},{4,16},{8,28},{12,24},{16,4},{20,0},{24,12},{28,8},{1,21},{... | collective-permute-start | bytes 208904 | tf_op jit(solution)/shard_map/ppermute | solution.py:640
  8.6 11.1 %collective-permute-start.3 = (f32[1,17,8,128]{3,2,1,0:T(8,128)S(1)}, f32[1,17,8,128]{3,2,1,0:T(8,128)S(1)}, u32[]{:S(2)}, u32[]{:S(2)}) collective-permute-start(f32[1,17,8,128]{3,2,1,0:T(8,128)S(1)} %get-tuple-element.34), channel_id=1, source_target_pairs={{0,8},{4,12},{8,0},{12,4},{16,24},{20,28},{24,16},{28,20},{1,9},{5... | collective-permute-start | bytes 208904 | tf_op jit(solution)/shard_map/ppermute | solution.py:640
  10.5 9.2 %collective-permute-start.4 = (f32[1,17,8,128]{3,2,1,0:T(8,128)S(1)}, f32[1,17,8,128]{3,2,1,0:T(8,128)S(1)}, u32[]{:S(2)}, u32[]{:S(2)}) collective-permute-start(f32[1,17,8,128]{3,2,1,0:T(8,128)S(1)} %get-tuple-element.35), channel_id=1, source_target_pairs={{0,24},{4,28},{8,16},{12,20},{16,8},{20,12},{24,0},{28,4},{1,25},{... | collective-permute-start | bytes 208904 | tf_op jit(solution)/shard_map/ppermute | solution.py:640
  13.0 6.8 %collective-permute-start.5 = (f32[1,17,8,128]{3,2,1,0:T(8,128)S(1)}, f32[1,17,8,128]{3,2,1,0:T(8,128)S(1)}, u32[]{:S(2)}, u32[]{:S(2)}) collective-permute-start(f32[1,17,8,128]{3,2,1,0:T(8,128)S(1)} %get-tuple-element.36), channel_id=1, source_target_pairs={{0,12},{4,8},{8,4},{12,0},{16,28},{20,24},{24,20},{28,16},{1,13},{... | collective-permute-start | bytes 208904 | tf_op jit(solution)/shard_map/ppermute | solution.py:640
  14.6 7.0 %collective-permute-start.6 = (f32[1,17,8,128]{3,2,1,0:T(8,128)S(1)}, f32[1,17,8,128]{3,2,1,0:T(8,128)S(1)}, u32[]{:S(2)}, u32[]{:S(2)}) collective-permute-start(f32[1,17,8,128]{3,2,1,0:T(8,128)S(1)} %get-tuple-element.37), channel_id=1, source_target_pairs={{0,28},{4,24},{8,20},{12,16},{16,12},{20,8},{24,4},{28,0},{1,29},{... | collective-permute-start | bytes 208904 | tf_op jit(solution)/shard_map/ppermute | solution.py:640
  21.6 16.6 %all-to-all-start = ((f32[8,16,8,128]{3,2,1,0:T(8,128)}), f32[8,16,8,128]{3,2,1,0:T(8,128)S(1)}, u32[]{:S(2)}, u32[]{:S(2)}) async-start(f32[8,16,8,128]{3,2,1,0:T(8,128)} %shard_map.136), calls=%async_computation | async-start | bytes 1048576 | tf_op jit(solution)/shard_map/all_to_all | solution.py:637
  28.0 6.1 %collective-permute-start.7 = (f32[104,256]{1,0:T(8,128)S(1)}, f32[104,256]{1,0:T(8,128)S(1)}, u32[]{:S(2)}, u32[]{:S(2)}) collective-permute-start(f32[104,256]{1,0:T(8,128)S(1)} %get-tuple-element.40), channel_id=1, source_target_pairs={{1,2},{2,1},{5,6},{6,5},{9,10},{10,9},{13,14},{14,13},{17,18},{18,... | collective-permute-start | bytes 319496 | tf_op jit(solution)/shard_map/ppermute | solution.py:668
  28.7 5.5 %collective-permute-start.8 = (f32[104,256]{1,0:T(8,128)S(1)}, f32[104,256]{1,0:T(8,128)S(1)}, u32[]{:S(2)}, u32[]{:S(2)}) collective-permute-start(f32[104,256]{1,0:T(8,128)S(1)} %get-tuple-element.41), channel_id=1, source_target_pairs={{0,1},{1,0},{2,3},{3,2},{4,5},{5,4},{6,7},{7,6},{8,9},{9,8},{10,11... | collective-permute-start | bytes 319496 | tf_op jit(solution)/shard_map/ppermute | solution.py:669
  42.2 6.0 %collective-permute-start.9 = (f32[176,128]{1,0:T(8,128)S(1)}, f32[176,128]{1,0:T(8,128)S(1)}, u32[]{:S(2)}, u32[]{:S(2)}) collective-permute-start(f32[176,128]{1,0:T(8,128)S(1)} %get-tuple-element.49), channel_id=1, source_target_pairs={{0,3},{1,2},{2,1},{3,0},{4,7},{5,6},{6,5},{7,4},{8,11},{9,10},{10,... | collective-permute-start | bytes 270344 | tf_op jit(solution)/shard_map/ppermute | solution.py:711
  42.2 6.0 %collective-permute-start.11 = (f32[176,128]{1,0:T(8,128)S(1)}, f32[176,128]{1,0:T(8,128)S(1)}, u32[]{:S(2)}, u32[]{:S(2)}) collective-permute-start(f32[176,128]{1,0:T(8,128)S(1)} %get-tuple-element.50), channel_id=1, source_target_pairs={{0,1},{1,0},{2,3},{3,2},{4,5},{5,4},{6,7},{7,6},{8,9},{9,8},{10,11... | collective-permute-start | bytes 270344 | tf_op jit(solution)/shard_map/ppermute | solution.py:711
  43.8 4.4 %collective-permute-start.10 = (f32[96,128]{1,0:T(8,128)S(1)}, f32[96,128]{1,0:T(8,128)S(1)}, u32[]{:S(2)}, u32[]{:S(2)}) collective-permute-start(f32[96,128]{1,0:T(8,128)S(1)} %get-tuple-element.48.refs_0_), channel_id=1, source_target_pairs={{0,2},{1,3},{2,0},{3,1},{4,6},{5,7},{6,4},{7,5},{8,10},{9,11},{10,... | collective-permute-start | bytes 147464 | tf_op jit(solution)/shard_map/ppermute | solution.py:711

commit v5 on v4

--- a/solution.py
+++ b/solution.py
@@ -688,7 +688,7 @@
 
     gram_rows = visits // 2 * SLOTS
     tail_rows = visits * PR * (col_count // LANES)
-    step = 32
+    step = row_count
     gram_depth = 2 * visits * (BASIS + 4) + 3 * SLOTS + 16 - 2 * LANES
     variance, to_near, to_far, gram = call(
         functools.partial(gram_kernel, (patches, capacity, visits, row_count, col_count, var_blocks, step)),

time: 53 us -> 52.7 us (level)
  no operation moved by 1% of the time
where the time goes in v5:
time: 52.7 us; the launch traced here: 52.4 us
  starting transfers between devices  24.2 us (46%)
  Pallas kernels  20.2 us (38%)
  waiting for transfers between devices  6.55 us (12%)
  between operations  1.39 us (3%)
    ppermute x7, starting transfers between devices, route(): lax.ppermute(block, 'patch', [(i, i ^ away) for i in range(patches)])  14.3 us
    pallas_call x1, Pallas kernels, local(): call(functools.partial(solve_kernel, (visits, row_count, col_count, subti...  4.49 us
    all_to_all x1, starting transfers between devices, route(): lax.all_to_all(blocks[0], 'patch', split_axis=0, concat_axis=0, tiled=True)  4.12 us
    ppermute x3, waiting for transfers between devices, local(): lax.ppermute(part, 'sub', [(i, i ^ away) for i in range(subtiles)])  3.84 us
    pallas_call x1, Pallas kernels, local(): call(functools.partial(gram_kernel, (patches, capacity, visits, row_count...  3.63 us
    pallas_call x1, Pallas kernels, local(): call(functools.partial(design_kernel, (visits, row_count, col_count)), [s...  3.3 us
    ppermute x1, starting transfers between devices, local(): lax.ppermute(to_near, 'sub', [(i, i ^ 1) for i in range(subtiles)])  2.91 us
    pallas_call x1, Pallas kernels, local(): call(functools.partial(fetch_kernel, (row_count, col_count)), [sds(design...  2.54 us
  transfers between devices with their start and end apart: 13, of which 3 were waited for; matrix products, arithmetic and copies ran while one was open for 0% of the time, Pallas kernels for 20%

profile of v5, /device:TPU:0, one launch (start us, length us, event | category | flops | bytes accessed | tf_op | source)
XLA Modules:
  0.0 52.4 jit_solution(6150241338747571035)
XLA Ops:
  1.3 1.7 %shard_map.131 = (f32[1,17,8,128]{3,2,1,0:T(8,128)S(1)}, f32[1,17,8,128]{3,2,1,0:T(8,128)S(1)}, f32[1,17,8,128]{3,2,1,0:T(8,128)S(1)}, f32[1,17,8,128]{3,2,1,0:T...) custom-call(s32[1,32]{1,0:T(1,128)} %bitcast.1, ...), custom_call_target="tpu_custom_call" | custom-call | tf_op jit(solution)/shard_map/pallas_call | solution.py:608
  3.0 4.1 %collective-permute-start = (f32[1,17,8,128]{3,2,1,0:T(8,128)S(1)}, f32[1,17,8,128]{3,2,1,0:T(8,128)S(1)}, u32[]{:S(2)}, u32[]{:S(2)}) collective-permute-start(f32[1,17,8,128]{3,2,1,0:T(8,128)S(1)} %get-tuple-element.31), channel_id=1, source_target_pairs={{0,16},{4,20},{8,24},{12,28},{16,0},{20,4},{24,8},{28,12},{1,17},{... | collective-permute-start | bytes 208904 | tf_op jit(solution)/shard_map/ppermute | solution.py:640
  7.1 1.5 %collective-permute-start.1 = (f32[1,17,8,128]{3,2,1,0:T(8,128)S(1)}, f32[1,17,8,128]{3,2,1,0:T(8,128)S(1)}, u32[]{:S(2)}, u32[]{:S(2)}) collective-permute-start(f32[1,17,8,128]{3,2,1,0:T(8,128)S(1)} %get-tuple-element.32), channel_id=1, source_target_pairs={{0,4},{4,0},{8,12},{12,8},{16,20},{20,16},{24,28},{28,24},{1,5},{5... | collective-permute-start | bytes 208904 | tf_op jit(solution)/shard_map/ppermute | solution.py:640
  8.6 0.0 collective-permute-start.2
  8.6 1.8 %collective-permute-start.3 = (f32[1,17,8,128]{3,2,1,0:T(8,128)S(1)}, f32[1,17,8,128]{3,2,1,0:T(8,128)S(1)}, u32[]{:S(2)}, u32[]{:S(2)}) collective-permute-start(f32[1,17,8,128]{3,2,1,0:T(8,128)S(1)} %get-tuple-element.34), channel_id=1, source_target_pairs={{0,8},{4,12},{8,0},{12,4},{16,24},{20,28},{24,16},{28,20},{1,9},{5... | collective-permute-start | bytes 208904 | tf_op jit(solution)/shard_map/ppermute | solution.py:640
  10.5 2.5 %collective-permute-start.4 = (f32[1,17,8,128]{3,2,1,0:T(8,128)S(1)}, f32[1,17,8,128]{3,2,1,0:T(8,128)S(1)}, u32[]{:S(2)}, u32[]{:S(2)}) collective-permute-start(f32[1,17,8,128]{3,2,1,0:T(8,128)S(1)} %get-tuple-element.35), channel_id=1, source_target_pairs={{0,24},{4,28},{8,16},{12,20},{16,8},{20,12},{24,0},{28,4},{1,25},{... | collective-permute-start | bytes 208904 | tf_op jit(solution)/shard_map/ppermute | solution.py:640
  13.0 0.0 collective-permute-done.refs_1_
  13.0 1.6 %collective-permute-start.5 = (f32[1,17,8,128]{3,2,1,0:T(8,128)S(1)}, f32[1,17,8,128]{3,2,1,0:T(8,128)S(1)}, u32[]{:S(2)}, u32[]{:S(2)}) collective-permute-start(f32[1,17,8,128]{3,2,1,0:T(8,128)S(1)} %get-tuple-element.36), channel_id=1, source_target_pairs={{0,12},{4,8},{8,4},{12,0},{16,28},{20,24},{24,20},{28,16},{1,13},{... | collective-permute-start | bytes 208904 | tf_op jit(solution)/shard_map/ppermute | solution.py:640
  14.6 0.0 collective-permute-done.1.refs_2_
  14.6 2.7 %collective-permute-start.6 = (f32[1,17,8,128]{3,2,1,0:T(8,128)S(1)}, f32[1,17,8,128]{3,2,1,0:T(8,128)S(1)}, u32[]{:S(2)}, u32[]{:S(2)}) collective-permute-start(f32[1,17,8,128]{3,2,1,0:T(8,128)S(1)} %get-tuple-element.37), channel_id=1, source_target_pairs={{0,28},{4,24},{8,20},{12,16},{16,12},{20,8},{24,4},{28,0},{1,29},{... | collective-permute-start | bytes 208904 | tf_op jit(solution)/shard_map/ppermute | solution.py:640
  17.3 2.3 %shard_map.135.refs_0_ = f32[8,16,8,128]{3,2,1,0:T(8,128)} custom-call(s32[64]{0:T(128)S(1)} %get-tuple-element.46.chosen_ref, f32[1,32,8,256]{3,2,1,0:T(8,128)} %var_hbm.1), custom_call_target="tpu_custom_call" | custom-call | tf_op jit(solution)/shard_map/pallas_call | solution.py:644
  19.7 0.0 collective-permute-done.2.refs_3_
  19.7 0.0 collective-permute-done.3.refs_4_
  19.7 0.0 collective-permute-done.4.refs_5_
  19.7 0.0 collective-permute-done.5.refs_6_
  19.7 1.9 %collective-permute-done.6.refs_7_ = f32[1,17,8,128]{3,2,1,0:T(8,128)S(1)} collective-permute-done((f32[1,17,8,128]{3,2,1,0:T(8,128)S(1)}, f32[1,17,8,128]{3,2,1,0:T(8,128)S(1)}, u32[]{:S(2)}, u32[]{:S(2)}) %collective-permute-start.6) | collective-permute-done | bytes 69664 | tf_op jit(solution)/shard_map/ppermute | solution.py:640
  21.6 4.1 %all-to-all-start = ((f32[8,16,8,128]{3,2,1,0:T(8,128)}), f32[8,16,8,128]{3,2,1,0:T(8,128)S(1)}, u32[]{:S(2)}, u32[]{:S(2)}) async-start(f32[8,16,8,128]{3,2,1,0:T(8,128)} %shard_map.136), calls=%async_computation | async-start | bytes 1048576 | tf_op jit(solution)/shard_map/all_to_all | solution.py:637
  25.7 2.2 %shard_map.132 = (f32[4,64,256]{2,1,0:T(8,128)S(1)}, f32[104,256]{1,0:T(8,128)S(1)}, f32[104,256]{1,0:T(8,128)S(1)}, s32[64]{0:T(128)S(1)}) custom-call(s32[4]{0:T(128)S(1)} %get-tuple-element.28.warp_ref, f32[8,128]{1,0:T(8,128)S(1)} %get-tuple-element.29.stamp_ref, f32[1,17,8,128]{3,2,1,0:T(8,128)S(1)} %get-tuple-element.30.refs_0_, ...), custom_call_target="tpu_custom_call" | custom-call | tf_op jit(solution)/shard_map/pallas_call | solution.py:656
  27.9 0.7 %collective-permute-start.7 = (f32[104,256]{1,0:T(8,128)S(1)}, f32[104,256]{1,0:T(8,128)S(1)}, u32[]{:S(2)}, u32[]{:S(2)}) collective-permute-start(f32[104,256]{1,0:T(8,128)S(1)} %get-tuple-element.40), channel_id=1, source_target_pairs={{1,2},{2,1},{5,6},{6,5},{9,10},{10,9},{13,14},{14,13},{17,18},{18,... | collective-permute-start | bytes 319496 | tf_op jit(solution)/shard_map/ppermute | solution.py:668
  28.6 2.9 %collective-permute-start.8 = (f32[104,256]{1,0:T(8,128)S(1)}, f32[104,256]{1,0:T(8,128)S(1)}, u32[]{:S(2)}, u32[]{:S(2)}) collective-permute-start(f32[104,256]{1,0:T(8,128)S(1)} %get-tuple-element.41), channel_id=1, source_target_pairs={{0,1},{1,0},{2,3},{3,2},{4,5},{5,4},{6,7},{7,6},{8,9},{9,8},{10,11... | collective-permute-start | bytes 319496 | tf_op jit(solution)/shard_map/ppermute | solution.py:669
  31.5 2.5 %shard_map.133 = (bf16[19,2,256,256]{3,2,1,0:T(8,128)(2,1)S(1)}, f32[64,256]{1,0:T(8,128)S(1)}) custom-call(f32[8,128]{1,0:T(8,128)S(1)} %get-tuple-element.29.stamp_ref, bf16[19,2,256,256]{3,2,1,0:T(8,128)(2,1)} %constant.8.clone.fixed_ref), custom_call_target="tpu_custom_call" | custom-call | tf_op jit(solution)/shard_map/pallas_call | solution.py:674
  34.1 0.0 collective-permute-done.8.near_ref
  34.1 3.3 %shard_map.134 = (f32[64,40,256]{2,1,0:T(8,128)S(1)}, f32[64,256]{1,0:T(8,128)S(1)}, bf16[14,128,256]{2,1,0:T(8,128)(2,1)}, bf16[14,128,256]{2,1,0:T(8,128)(2,1)}, f32[4,96,256]{2,1,0:T(8,128)}) custom-call(f32[4,64,256]{2,1,0:T(8,128)S(1)} %get-tuple-element.39.sci_ref, f32[104,256]{1,0:T(8,128)S(1)} %collective-permute-done.7.far_ref, ...), custom_call_target="tpu_custom_call" | custom-call | tf_op jit(solution)/shard_map/pallas_call | solution.py:681
  37.4 0.8 %all-to-all-done.refs_0_ = f32[8,16,8,128]{3,2,1,0:T(8,128)S(1)} async-done(((f32[8,16,8,128]{3,2,1,0:T(8,128)}), f32[8,16,8,128]{3,2,1,0:T(8,128)S(1)}, u32[]{:S(2)}, u32[]{:S(2)}) %all-to-all-start) | async-done | bytes 524320 | tf_op jit(solution)/shard_map/all_to_all | solution.py:637
  38.2 3.6 %shard_map.137 = (f32[4,64,256]{2,1,0:T(8,128)S(1)}, f32[176,128]{1,0:T(8,128)S(1)}, f32[176,128]{1,0:T(8,128)S(1)}, f32[96,128]{1,0:T(8,128)S(1)}) custom-call(s32[4]{0:T(128)S(1)} %get-tuple-element.28.warp_ref, s32[64]{0:T(128)S(1)} %get-tuple-element.38.cells_ref, f32[64,256]{1,0:T(8,128)S(1)} %get-tuple-element.44.mask_ref, ...), custom_call_target="tpu_custom_call" | custom-call | tf_op jit(solution)/shard_map/pallas_call | solution.py:693
  41.9 0.1 collective-permute-start.9
  41.9 1.6 %collective-permute-start.11 = (f32[176,128]{1,0:T(8,128)S(1)}, f32[176,128]{1,0:T(8,128)S(1)}, u32[]{:S(2)}, u32[]{:S(2)}) collective-permute-start(f32[176,128]{1,0:T(8,128)S(1)} %get-tuple-element.50), channel_id=1, source_target_pairs={{0,1},{1,0},{2,3},{3,2},{4,5},{5,4},{6,7},{7,6},{8,9},{9,8},{10,11... | collective-permute-start | bytes 270344 | tf_op jit(solution)/shard_map/ppermute | solution.py:711
  43.5 0.5 %collective-permute-start.10 = (f32[96,128]{1,0:T(8,128)S(1)}, f32[96,128]{1,0:T(8,128)S(1)}, u32[]{:S(2)}, u32[]{:S(2)}) collective-permute-start(f32[96,128]{1,0:T(8,128)S(1)} %get-tuple-element.48.refs_0_), channel_id=1, source_target_pairs={{0,2},{1,3},{2,0},{3,1},{4,6},{5,7},{6,4},{7,5},{8,10},{9,11},{10,... | collective-permute-start | bytes 147464 | tf_op jit(solution)/shard_map/ppermute | solution.py:711
  44.1 3.8 %collective-permute-done.10.refs_2_ = f32[96,128]{1,0:T(8,128)S(1)} collective-permute-done((f32[96,128]{1,0:T(8,128)S(1)}, f32[96,128]{1,0:T(8,128)S(1)}, u32[]{:S(2)}, u32[]{:S(2)}) %collective-permute-start.10) | collective-permute-done | bytes 49184 | tf_op jit(solution)/shard_map/ppermute | solution.py:711
  47.9 0.0 collective-permute-done.9.refs_1_
  47.9 0.0 collective-permute-done.11.refs_3_
  47.9 4.5 %shard_map.138 = (f32[4,1,64,256]{3,2,1,0:T(8,128)}, f32[4,1,64,256]{3,2,1,0:T(8,128)}) custom-call(f32[4,64,256]{2,1,0:T(8,128)S(1)} %get-tuple-element.47.var_ref, f32[96,128]{1,0:T(8,128)S(1)} %get-tuple-element.48.refs_0_, f32[176,128]{1,0:T(8,128)S(1)} %collective-permute-done.9.refs_1_, f32[96,128]{1,0:T(8,128)S(1)} %collective-permute-done.10.refs_2_, ...), custom_call_target="tpu_custom_call" | custom-call | tf_op jit(solution)/shard_map/pallas_call | solution.py:716
  (2 shorter events, 0.0 us)
Async XLA Ops:
  3.0 10.0 %collective-permute-start = (f32[1,17,8,128]{3,2,1,0:T(8,128)S(1)}, f32[1,17,8,128]{3,2,1,0:T(8,128)S(1)}, u32[]{:S(2)}, u32[]{:S(2)}) collective-permute-start(f32[1,17,8,128]{3,2,1,0:T(8,128)S(1)} %get-tuple-element.31), channel_id=1, source_target_pairs={{0,16},{4,20},{8,24},{12,28},{16,0},{20,4},{24,8},{28,12},{1,17},{... | collective-permute-start | bytes 208904 | tf_op jit(solution)/shard_map/ppermute | solution.py:640
  7.1 7.5 %collective-permute-start.1 = (f32[1,17,8,128]{3,2,1,0:T(8,128)S(1)}, f32[1,17,8,128]{3,2,1,0:T(8,128)S(1)}, u32[]{:S(2)}, u32[]{:S(2)}) collective-permute-start(f32[1,17,8,128]{3,2,1,0:T(8,128)S(1)} %get-tuple-element.32), channel_id=1, source_target_pairs={{0,4},{4,0},{8,12},{12,8},{16,20},{20,16},{24,28},{28,24},{1,5},{5... | collective-permute-start | bytes 208904 | tf_op jit(solution)/shard_map/ppermute | solution.py:640
  8.6 11.1 %collective-permute-start.2 = (f32[1,17,8,128]{3,2,1,0:T(8,128)S(1)}, f32[1,17,8,128]{3,2,1,0:T(8,128)S(1)}, u32[]{:S(2)}, u32[]{:S(2)}) collective-permute-start(f32[1,17,8,128]{3,2,1,0:T(8,128)S(1)} %get-tuple-element.33), channel_id=1, source_target_pairs={{0,20},{4,16},{8,28},{12,24},{16,4},{20,0},{24,12},{28,8},{1,21},{... | collective-permute-start | bytes 208904 | tf_op jit(solution)/shard_map/ppermute | solution.py:640
  8.6 11.1 %collective-permute-start.3 = (f32[1,17,8,128]{3,2,1,0:T(8,128)S(1)}, f32[1,17,8,128]{3,2,1,0:T(8,128)S(1)}, u32[]{:S(2)}, u32[]{:S(2)}) collective-permute-start(f32[1,17,8,128]{3,2,1,0:T(8,128)S(1)} %get-tuple-element.34), channel_id=1, source_target_pairs={{0,8},{4,12},{8,0},{12,4},{16,24},{20,28},{24,16},{28,20},{1,9},{5... | collective-permute-start | bytes 208904 | tf_op jit(solution)/shard_map/ppermute | solution.py:640
  10.5 9.2 %collective-permute-start.4 = (f32[1,17,8,128]{3,2,1,0:T(8,128)S(1)}, f32[1,17,8,128]{3,2,1,0:T(8,128)S(1)}, u32[]{:S(2)}, u32[]{:S(2)}) collective-permute-start(f32[1,17,8,128]{3,2,1,0:T(8,128)S(1)} %get-tuple-element.35), channel_id=1, source_target_pairs={{0,24},{4,28},{8,16},{12,20},{16,8},{20,12},{24,0},{28,4},{1,25},{... | collective-permute-start | bytes 208904 | tf_op jit(solution)/shard_map/ppermute | solution.py:640
  13.0 6.8 %collective-permute-start.5 = (f32[1,17,8,128]{3,2,1,0:T(8,128)S(1)}, f32[1,17,8,128]{3,2,1,0:T(8,128)S(1)}, u32[]{:S(2)}, u32[]{:S(2)}) collective-permute-start(f32[1,17,8,128]{3,2,1,0:T(8,128)S(1)} %get-tuple-element.36), channel_id=1, source_target_pairs={{0,12},{4,8},{8,4},{12,0},{16,28},{20,24},{24,20},{28,16},{1,13},{... | collective-permute-start | bytes 208904 | tf_op jit(solution)/shard_map/ppermute | solution.py:640
  14.6 7.0 %collective-permute-start.6 = (f32[1,17,8,128]{3,2,1,0:T(8,128)S(1)}, f32[1,17,8,128]{3,2,1,0:T(8,128)S(1)}, u32[]{:S(2)}, u32[]{:S(2)}) collective-permute-start(f32[1,17,8,128]{3,2,1,0:T(8,128)S(1)} %get-tuple-element.37), channel_id=1, source_target_pairs={{0,28},{4,24},{8,20},{12,16},{16,12},{20,8},{24,4},{28,0},{1,29},{... | collective-permute-start | bytes 208904 | tf_op jit(solution)/shard_map/ppermute | solution.py:640
  21.6 16.6 %all-to-all-start = ((f32[8,16,8,128]{3,2,1,0:T(8,128)}), f32[8,16,8,128]{3,2,1,0:T(8,128)S(1)}, u32[]{:S(2)}, u32[]{:S(2)}) async-start(f32[8,16,8,128]{3,2,1,0:T(8,128)} %shard_map.136), calls=%async_computation | async-start | bytes 1048576 | tf_op jit(solution)/shard_map/all_to_all | solution.py:637
  27.9 6.1 %collective-permute-start.7 = (f32[104,256]{1,0:T(8,128)S(1)}, f32[104,256]{1,0:T(8,128)S(1)}, u32[]{:S(2)}, u32[]{:S(2)}) collective-permute-start(f32[104,256]{1,0:T(8,128)S(1)} %get-tuple-element.40), channel_id=1, source_target_pairs={{1,2},{2,1},{5,6},{6,5},{9,10},{10,9},{13,14},{14,13},{17,18},{18,... | collective-permute-start | bytes 319496 | tf_op jit(solution)/shard_map/ppermute | solution.py:668
  28.6 5.5 %collective-permute-start.8 = (f32[104,256]{1,0:T(8,128)S(1)}, f32[104,256]{1,0:T(8,128)S(1)}, u32[]{:S(2)}, u32[]{:S(2)}) collective-permute-start(f32[104,256]{1,0:T(8,128)S(1)} %get-tuple-element.41), channel_id=1, source_target_pairs={{0,1},{1,0},{2,3},{3,2},{4,5},{5,4},{6,7},{7,6},{8,9},{9,8},{10,11... | collective-permute-start | bytes 319496 | tf_op jit(solution)/shard_map/ppermute | solution.py:669
  41.9 6.0 %collective-permute-start.9 = (f32[176,128]{1,0:T(8,128)S(1)}, f32[176,128]{1,0:T(8,128)S(1)}, u32[]{:S(2)}, u32[]{:S(2)}) collective-permute-start(f32[176,128]{1,0:T(8,128)S(1)} %get-tuple-element.49), channel_id=1, source_target_pairs={{0,3},{1,2},{2,1},{3,0},{4,7},{5,6},{6,5},{7,4},{8,11},{9,10},{10,... | collective-permute-start | bytes 270344 | tf_op jit(solution)/shard_map/ppermute | solution.py:711
  41.9 6.0 %collective-permute-start.11 = (f32[176,128]{1,0:T(8,128)S(1)}, f32[176,128]{1,0:T(8,128)S(1)}, u32[]{:S(2)}, u32[]{:S(2)}) collective-permute-start(f32[176,128]{1,0:T(8,128)S(1)} %get-tuple-element.50), channel_id=1, source_target_pairs={{0,1},{1,0},{2,3},{3,2},{4,5},{5,4},{6,7},{7,6},{8,9},{9,8},{10,11... | collective-permute-start | bytes 270344 | tf_op jit(solution)/shard_map/ppermute | solution.py:711
  43.5 4.4 %collective-permute-start.10 = (f32[96,128]{1,0:T(8,128)S(1)}, f32[96,128]{1,0:T(8,128)S(1)}, u32[]{:S(2)}, u32[]{:S(2)}) collective-permute-start(f32[96,128]{1,0:T(8,128)S(1)} %get-tuple-element.48.refs_0_), channel_id=1, source_target_pairs={{0,2},{1,3},{2,0},{3,1},{4,6},{5,7},{6,4},{7,5},{8,10},{9,11},{10,... | collective-permute-start | bytes 147464 | tf_op jit(solution)/shard_map/ppermute | solution.py:711

commit v6 on v5

--- a/solution.py
+++ b/solution.py
@@ -343,7 +343,7 @@
 
 
 def gram_kernel(cfg, warp_ref, cells_ref, mask_ref, sci_ref, design_ref, *refs):
-    patches, capacity, visits, row_count, col_count, block_count, step = cfg
+    patches, capacity, visits, row_count, col_count, block_count = cfg
     blocks = refs[:block_count]
     var_ref, near_ref, far_ref, gram_ref, total_ref, weight_ref, sum_ref = refs[block_count:]
     me = lax.axis_index("patch")
@@ -357,33 +357,27 @@
     mask = mask_ref[...]
     for visit in range(visits):
         weight_ref[visit] = mask / (var_ref[visit] + shared)
-    sum_ref[...] = jnp.zeros(sum_ref.shape, F32)
 
     rows = visits * BASIS + visits // 2 * 8
     kept = 2 * LANES - 2 * SLOTS - 16
     line = lax.broadcasted_iota(jnp.int32, (8, col_count), 0)
 
-    def body(number, carry):
-        left, right = [], []
-        for extra in range(step):
-            row = number * step + extra
-            design = design_ref[row]
-            last = jnp.ones((8, col_count), F32)
-            for visit in range(visits):
-                last = jnp.where(line == SCI_SLOT - BASIS + visit, sci_ref[visit, pl.ds(row, 1), :], last)
-            high, low = split(jnp.concatenate([design, last], axis=0))
-            weights = [weight_ref[visit, pl.ds(row, 1), :] for visit in range(visits)]
-            scaled = [design * weight for weight in weights]
-            for pair in range(visits // 2):
-                scaled.append(jnp.where(line == 0, weights[2 * pair], weights[2 * pair + 1]))
-            scaled_high, scaled_low = split(jnp.concatenate(scaled, axis=0))
-            blank = jnp.zeros((16, col_count), BF16)
-            right.append(jnp.concatenate([high, low, scaled_low[:kept], blank], axis=0))
-            left.append(jnp.concatenate([scaled_high, high, scaled_low[kept:]], axis=0))
-        sum_ref[...] += mul_nt(jnp.concatenate(left, axis=1), jnp.concatenate(right, axis=1))
-        return carry
-
-    lax.fori_loop(0, row_count // step, body, 0)
+    left, right = [], []
+    for row in range(row_count):
+        design = design_ref[row]
+        last = jnp.ones((8, col_count), F32)
+        for visit in range(visits):
+            last = jnp.where(line == SCI_SLOT - BASIS + visit, sci_ref[visit, pl.ds(row, 1), :], last)
+        high, low = split(jnp.concatenate([design, last], axis=0))
+        weights = [weight_ref[visit, pl.ds(row, 1), :] for visit in range(visits)]
+        scaled = [design * weight for weight in weights]
+        for pair in range(visits // 2):
+            scaled.append(jnp.where(line == 0, weights[2 * pair], weights[2 * pair + 1]))
+        scaled_high, scaled_low = split(jnp.concatenate(scaled, axis=0))
+        blank = jnp.zeros((16, col_count), BF16)
+        right.append(jnp.concatenate([high, low, scaled_low[:kept], blank], axis=0))
+        left.append(jnp.concatenate([scaled_high, high, scaled_low[kept:]], axis=0))
+    sum_ref[...] = mul_nt(jnp.concatenate(left, axis=1), jnp.concatenate(right, axis=1))
     depth = sum_ref.shape[0]
     main = sum_ref[:rows, :LANES]
     turned = jnp.transpose(sum_ref[depth - LANES :, :])[2 * SLOTS : 2 * SLOTS + kept]
@@ -688,10 +682,9 @@
 
     gram_rows = visits // 2 * SLOTS
     tail_rows = visits * PR * (col_count // LANES)
-    step = row_count
     gram_depth = 2 * visits * (BASIS + 4) + 3 * SLOTS + 16 - 2 * LANES
     variance, to_near, to_far, gram = call(
-        functools.partial(gram_kernel, (patches, capacity, visits, row_count, col_count, var_blocks, step)),
+        functools.partial(gram_kernel, (patches, capacity, visits, row_count, col_count, var_blocks)),
         [
             sds((visits, row_count, col_count), F32),
             sds((gram_rows + tail_rows, LANES), F32),

time: 52.7 us -> 52.7 us (level)
  no operation moved by 1% of the time
where the time goes in v6:
time: 52.7 us; the launch traced here: 52.4 us
  starting transfers between devices  24.2 us (46%)
  Pallas kernels  20.3 us (39%)
  waiting for transfers between devices  6.49 us (12%)
  between operations  1.39 us (3%)
    ppermute x7, starting transfers between devices, route(): lax.ppermute(block, 'patch', [(i, i ^ away) for i in range(patches)])  14.3 us
    pallas_call x1, Pallas kernels, local(): call(functools.partial(solve_kernel, (visits, row_count, col_count, subti...  4.5 us
    all_to_all x1, starting transfers between devices, route(): lax.all_to_all(blocks[0], 'patch', split_axis=0, concat_axis=0, tiled=True)  4.12 us
    ppermute x3, waiting for transfers between devices, local(): lax.ppermute(part, 'sub', [(i, i ^ away) for i in range(subtiles)])  3.84 us
    pallas_call x1, Pallas kernels, local(): call(functools.partial(gram_kernel, (patches, capacity, visits, row_count...  3.66 us
    pallas_call x1, Pallas kernels, local(): call(functools.partial(design_kernel, (visits, row_count, col_count)), [s...  3.3 us
    ppermute x1, starting transfers between devices, local(): lax.ppermute(to_near, 'sub', [(i, i ^ 1) for i in range(subtiles)])  2.91 us
    pallas_call x1, Pallas kernels, local(): call(functools.partial(fetch_kernel, (row_count, col_count)), [sds(design...  2.54 us
  transfers between devices with their start and end apart: 13, of which 3 were waited for; matrix products, arithmetic and copies ran while one was open for 0% of the time, Pallas kernels for 20%

profile of v6, /device:TPU:0, one launch (start us, length us, event | category | flops | bytes accessed | tf_op | source)
XLA Modules:
  0.0 52.4 jit_solution(6150241338747571035)
XLA Ops:
  1.3 1.7 %shard_map.131 = (f32[1,17,8,128]{3,2,1,0:T(8,128)S(1)}, f32[1,17,8,128]{3,2,1,0:T(8,128)S(1)}, f32[1,17,8,128]{3,2,1,0:T(8,128)S(1)}, f32[1,17,8,128]{3,2,1,0:T...) custom-call(s32[1,32]{1,0:T(1,128)} %bitcast.1, ...), custom_call_target="tpu_custom_call" | custom-call | tf_op jit(solution)/shard_map/pallas_call | solution.py:602
  3.0 4.1 %collective-permute-start = (f32[1,17,8,128]{3,2,1,0:T(8,128)S(1)}, f32[1,17,8,128]{3,2,1,0:T(8,128)S(1)}, u32[]{:S(2)}, u32[]{:S(2)}) collective-permute-start(f32[1,17,8,128]{3,2,1,0:T(8,128)S(1)} %get-tuple-element.31), channel_id=1, source_target_pairs={{0,16},{4,20},{8,24},{12,28},{16,0},{20,4},{24,8},{28,12},{1,17},{... | collective-permute-start | bytes 208904 | tf_op jit(solution)/shard_map/ppermute | solution.py:634
  7.1 1.5 %collective-permute-start.1 = (f32[1,17,8,128]{3,2,1,0:T(8,128)S(1)}, f32[1,17,8,128]{3,2,1,0:T(8,128)S(1)}, u32[]{:S(2)}, u32[]{:S(2)}) collective-permute-start(f32[1,17,8,128]{3,2,1,0:T(8,128)S(1)} %get-tuple-element.32), channel_id=1, source_target_pairs={{0,4},{4,0},{8,12},{12,8},{16,20},{20,16},{24,28},{28,24},{1,5},{5... | collective-permute-start | bytes 208904 | tf_op jit(solution)/shard_map/ppermute | solution.py:634
  8.6 0.0 collective-permute-start.2
  8.6 1.8 %collective-permute-start.3 = (f32[1,17,8,128]{3,2,1,0:T(8,128)S(1)}, f32[1,17,8,128]{3,2,1,0:T(8,128)S(1)}, u32[]{:S(2)}, u32[]{:S(2)}) collective-permute-start(f32[1,17,8,128]{3,2,1,0:T(8,128)S(1)} %get-tuple-element.34), channel_id=1, source_target_pairs={{0,8},{4,12},{8,0},{12,4},{16,24},{20,28},{24,16},{28,20},{1,9},{5... | collective-permute-start | bytes 208904 | tf_op jit(solution)/shard_map/ppermute | solution.py:634
  10.5 2.5 %collective-permute-start.4 = (f32[1,17,8,128]{3,2,1,0:T(8,128)S(1)}, f32[1,17,8,128]{3,2,1,0:T(8,128)S(1)}, u32[]{:S(2)}, u32[]{:S(2)}) collective-permute-start(f32[1,17,8,128]{3,2,1,0:T(8,128)S(1)} %get-tuple-element.35), channel_id=1, source_target_pairs={{0,24},{4,28},{8,16},{12,20},{16,8},{20,12},{24,0},{28,4},{1,25},{... | collective-permute-start | bytes 208904 | tf_op jit(solution)/shard_map/ppermute | solution.py:634
  13.0 0.0 collective-permute-done.refs_1_
  13.0 1.6 %collective-permute-start.5 = (f32[1,17,8,128]{3,2,1,0:T(8,128)S(1)}, f32[1,17,8,128]{3,2,1,0:T(8,128)S(1)}, u32[]{:S(2)}, u32[]{:S(2)}) collective-permute-start(f32[1,17,8,128]{3,2,1,0:T(8,128)S(1)} %get-tuple-element.36), channel_id=1, source_target_pairs={{0,12},{4,8},{8,4},{12,0},{16,28},{20,24},{24,20},{28,16},{1,13},{... | collective-permute-start | bytes 208904 | tf_op jit(solution)/shard_map/ppermute | solution.py:634
  14.6 0.0 collective-permute-done.1.refs_2_
  14.6 2.7 %collective-permute-start.6 = (f32[1,17,8,128]{3,2,1,0:T(8,128)S(1)}, f32[1,17,8,128]{3,2,1,0:T(8,128)S(1)}, u32[]{:S(2)}, u32[]{:S(2)}) collective-permute-start(f32[1,17,8,128]{3,2,1,0:T(8,128)S(1)} %get-tuple-element.37), channel_id=1, source_target_pairs={{0,28},{4,24},{8,20},{12,16},{16,12},{20,8},{24,4},{28,0},{1,29},{... | collective-permute-start | bytes 208904 | tf_op jit(solution)/shard_map/ppermute | solution.py:634
  17.3 2.3 %shard_map.135.refs_0_ = f32[8,16,8,128]{3,2,1,0:T(8,128)} custom-call(s32[64]{0:T(128)S(1)} %get-tuple-element.46.chosen_ref, f32[1,32,8,256]{3,2,1,0:T(8,128)} %var_hbm.1), custom_call_target="tpu_custom_call" | custom-call | tf_op jit(solution)/shard_map/pallas_call | solution.py:638
  19.7 0.0 collective-permute-done.2.refs_3_
  19.7 0.0 collective-permute-done.3.refs_4_
  19.7 0.0 collective-permute-done.4.refs_5_
  19.7 0.0 collective-permute-done.5.refs_6_
  19.7 1.9 %collective-permute-done.6.refs_7_ = f32[1,17,8,128]{3,2,1,0:T(8,128)S(1)} collective-permute-done((f32[1,17,8,128]{3,2,1,0:T(8,128)S(1)}, f32[1,17,8,128]{3,2,1,0:T(8,128)S(1)}, u32[]{:S(2)}, u32[]{:S(2)}) %collective-permute-start.6) | collective-permute-done | bytes 69664 | tf_op jit(solution)/shard_map/ppermute | solution.py:634
  21.6 4.1 %all-to-all-start = ((f32[8,16,8,128]{3,2,1,0:T(8,128)}), f32[8,16,8,128]{3,2,1,0:T(8,128)S(1)}, u32[]{:S(2)}, u32[]{:S(2)}) async-start(f32[8,16,8,128]{3,2,1,0:T(8,128)} %shard_map.136), calls=%async_computation | async-start | bytes 1048576 | tf_op jit(solution)/shard_map/all_to_all | solution.py:631
  25.7 2.3 %shard_map.132 = (f32[4,64,256]{2,1,0:T(8,128)S(1)}, f32[104,256]{1,0:T(8,128)S(1)}, f32[104,256]{1,0:T(8,128)S(1)}, s32[64]{0:T(128)S(1)}) custom-call(s32[4]{0:T(128)S(1)} %get-tuple-element.28.warp_ref, f32[8,128]{1,0:T(8,128)S(1)} %get-tuple-element.29.stamp_ref, f32[1,17,8,128]{3,2,1,0:T(8,128)S(1)} %get-tuple-element.30.refs_0_, ...), custom_call_target="tpu_custom_call" | custom-call | tf_op jit(solution)/shard_map/pallas_call | solution.py:650
  28.0 0.7 %collective-permute-start.7 = (f32[104,256]{1,0:T(8,128)S(1)}, f32[104,256]{1,0:T(8,128)S(1)}, u32[]{:S(2)}, u32[]{:S(2)}) collective-permute-start(f32[104,256]{1,0:T(8,128)S(1)} %get-tuple-element.40), channel_id=1, source_target_pairs={{1,2},{2,1},{5,6},{6,5},{9,10},{10,9},{13,14},{14,13},{17,18},{18,... | collective-permute-start | bytes 319496 | tf_op jit(solution)/shard_map/ppermute | solution.py:662
  28.7 2.9 %collective-permute-start.8 = (f32[104,256]{1,0:T(8,128)S(1)}, f32[104,256]{1,0:T(8,128)S(1)}, u32[]{:S(2)}, u32[]{:S(2)}) collective-permute-start(f32[104,256]{1,0:T(8,128)S(1)} %get-tuple-element.41), channel_id=1, source_target_pairs={{0,1},{1,0},{2,3},{3,2},{4,5},{5,4},{6,7},{7,6},{8,9},{9,8},{10,11... | collective-permute-start | bytes 319496 | tf_op jit(solution)/shard_map/ppermute | solution.py:663
  31.6 2.5 %shard_map.133 = (bf16[19,2,256,256]{3,2,1,0:T(8,128)(2,1)S(1)}, f32[64,256]{1,0:T(8,128)S(1)}) custom-call(f32[8,128]{1,0:T(8,128)S(1)} %get-tuple-element.29.stamp_ref, bf16[19,2,256,256]{3,2,1,0:T(8,128)(2,1)} %constant.8.clone.fixed_ref), custom_call_target="tpu_custom_call" | custom-call | tf_op jit(solution)/shard_map/pallas_call | solution.py:668
  34.1 0.0 collective-permute-done.7.far_ref
  34.2 3.3 %shard_map.134 = (f32[64,40,256]{2,1,0:T(8,128)S(1)}, f32[64,256]{1,0:T(8,128)S(1)}, bf16[14,128,256]{2,1,0:T(8,128)(2,1)}, bf16[14,128,256]{2,1,0:T(8,128)(2,1)}, f32[4,96,256]{2,1,0:T(8,128)}) custom-call(f32[4,64,256]{2,1,0:T(8,128)S(1)} %get-tuple-element.39.sci_ref, f32[104,256]{1,0:T(8,128)S(1)} %collective-permute-done.7.far_ref, ...), custom_call_target="tpu_custom_call" | custom-call | tf_op jit(solution)/shard_map/pallas_call | solution.py:675
  37.5 0.8 %all-to-all-done.refs_0_ = f32[8,16,8,128]{3,2,1,0:T(8,128)S(1)} async-done(((f32[8,16,8,128]{3,2,1,0:T(8,128)}), f32[8,16,8,128]{3,2,1,0:T(8,128)S(1)}, u32[]{:S(2)}, u32[]{:S(2)}) %all-to-all-start) | async-done | bytes 524320 | tf_op jit(solution)/shard_map/all_to_all | solution.py:631
  38.2 3.7 %shard_map.137 = (f32[4,64,256]{2,1,0:T(8,128)S(1)}, f32[176,128]{1,0:T(8,128)S(1)}, f32[176,128]{1,0:T(8,128)S(1)}, f32[96,128]{1,0:T(8,128)S(1)}) custom-call(s32[4]{0:T(128)S(1)} %get-tuple-element.28.warp_ref, s32[64]{0:T(128)S(1)} %get-tuple-element.38.cells_ref, f32[64,256]{1,0:T(8,128)S(1)} %get-tuple-element.44.mask_ref, ...), custom_call_target="tpu_custom_call" | custom-call | tf_op jit(solution)/shard_map/pallas_call | solution.py:686
  41.9 0.1 collective-permute-start.9
  42.0 1.6 %collective-permute-start.11 = (f32[176,128]{1,0:T(8,128)S(1)}, f32[176,128]{1,0:T(8,128)S(1)}, u32[]{:S(2)}, u32[]{:S(2)}) collective-permute-start(f32[176,128]{1,0:T(8,128)S(1)} %get-tuple-element.50), channel_id=1, source_target_pairs={{0,1},{1,0},{2,3},{3,2},{4,5},{5,4},{6,7},{7,6},{8,9},{9,8},{10,11... | collective-permute-start | bytes 270344 | tf_op jit(solution)/shard_map/ppermute | solution.py:704
  43.6 0.5 %collective-permute-start.10 = (f32[96,128]{1,0:T(8,128)S(1)}, f32[96,128]{1,0:T(8,128)S(1)}, u32[]{:S(2)}, u32[]{:S(2)}) collective-permute-start(f32[96,128]{1,0:T(8,128)S(1)} %get-tuple-element.48.refs_0_), channel_id=1, source_target_pairs={{0,2},{1,3},{2,0},{3,1},{4,6},{5,7},{6,4},{7,5},{8,10},{9,11},{10,... | collective-permute-start | bytes 147464 | tf_op jit(solution)/shard_map/ppermute | solution.py:704
  44.1 3.8 %collective-permute-done.10.refs_2_ = f32[96,128]{1,0:T(8,128)S(1)} collective-permute-done((f32[96,128]{1,0:T(8,128)S(1)}, f32[96,128]{1,0:T(8,128)S(1)}, u32[]{:S(2)}, u32[]{:S(2)}) %collective-permute-start.10) | collective-permute-done | bytes 49184 | tf_op jit(solution)/shard_map/ppermute | solution.py:704
  47.9 0.0 collective-permute-done.9.refs_1_
  47.9 0.0 collective-permute-done.11.refs_3_
  47.9 4.5 %shard_map.138 = (f32[4,1,64,256]{3,2,1,0:T(8,128)}, f32[4,1,64,256]{3,2,1,0:T(8,128)}) custom-call(f32[4,64,256]{2,1,0:T(8,128)S(1)} %get-tuple-element.47.var_ref, f32[96,128]{1,0:T(8,128)S(1)} %get-tuple-element.48.refs_0_, f32[176,128]{1,0:T(8,128)S(1)} %collective-permute-done.9.refs_1_, f32[96,128]{1,0:T(8,128)S(1)} %collective-permute-done.10.refs_2_, ...), custom_call_target="tpu_custom_call" | custom-call | tf_op jit(solution)/shard_map/pallas_call | solution.py:709
  (2 shorter events, 0.0 us)
Async XLA Ops:
  3.0 10.0 %collective-permute-start = (f32[1,17,8,128]{3,2,1,0:T(8,128)S(1)}, f32[1,17,8,128]{3,2,1,0:T(8,128)S(1)}, u32[]{:S(2)}, u32[]{:S(2)}) collective-permute-start(f32[1,17,8,128]{3,2,1,0:T(8,128)S(1)} %get-tuple-element.31), channel_id=1, source_target_pairs={{0,16},{4,20},{8,24},{12,28},{16,0},{20,4},{24,8},{28,12},{1,17},{... | collective-permute-start | bytes 208904 | tf_op jit(solution)/shard_map/ppermute | solution.py:634
  7.1 7.5 %collective-permute-start.1 = (f32[1,17,8,128]{3,2,1,0:T(8,128)S(1)}, f32[1,17,8,128]{3,2,1,0:T(8,128)S(1)}, u32[]{:S(2)}, u32[]{:S(2)}) collective-permute-start(f32[1,17,8,128]{3,2,1,0:T(8,128)S(1)} %get-tuple-element.32), channel_id=1, source_target_pairs={{0,4},{4,0},{8,12},{12,8},{16,20},{20,16},{24,28},{28,24},{1,5},{5... | collective-permute-start | bytes 208904 | tf_op jit(solution)/shard_map/ppermute | solution.py:634
  8.6 11.1 %collective-permute-start.2 = (f32[1,17,8,128]{3,2,1,0:T(8,128)S(1)}, f32[1,17,8,128]{3,2,1,0:T(8,128)S(1)}, u32[]{:S(2)}, u32[]{:S(2)}) collective-permute-start(f32[1,17,8,128]{3,2,1,0:T(8,128)S(1)} %get-tuple-element.33), channel_id=1, source_target_pairs={{0,20},{4,16},{8,28},{12,24},{16,4},{20,0},{24,12},{28,8},{1,21},{... | collective-permute-start | bytes 208904 | tf_op jit(solution)/shard_map/ppermute | solution.py:634
  8.6 11.1 %collective-permute-start.3 = (f32[1,17,8,128]{3,2,1,0:T(8,128)S(1)}, f32[1,17,8,128]{3,2,1,0:T(8,128)S(1)}, u32[]{:S(2)}, u32[]{:S(2)}) collective-permute-start(f32[1,17,8,128]{3,2,1,0:T(8,128)S(1)} %get-tuple-element.34), channel_id=1, source_target_pairs={{0,8},{4,12},{8,0},{12,4},{16,24},{20,28},{24,16},{28,20},{1,9},{5... | collective-permute-start | bytes 208904 | tf_op jit(solution)/shard_map/ppermute | solution.py:634
  10.5 9.2 %collective-permute-start.4 = (f32[1,17,8,128]{3,2,1,0:T(8,128)S(1)}, f32[1,17,8,128]{3,2,1,0:T(8,128)S(1)}, u32[]{:S(2)}, u32[]{:S(2)}) collective-permute-start(f32[1,17,8,128]{3,2,1,0:T(8,128)S(1)} %get-tuple-element.35), channel_id=1, source_target_pairs={{0,24},{4,28},{8,16},{12,20},{16,8},{20,12},{24,0},{28,4},{1,25},{... | collective-permute-start | bytes 208904 | tf_op jit(solution)/shard_map/ppermute | solution.py:634
  13.0 6.8 %collective-permute-start.5 = (f32[1,17,8,128]{3,2,1,0:T(8,128)S(1)}, f32[1,17,8,128]{3,2,1,0:T(8,128)S(1)}, u32[]{:S(2)}, u32[]{:S(2)}) collective-permute-start(f32[1,17,8,128]{3,2,1,0:T(8,128)S(1)} %get-tuple-element.36), channel_id=1, source_target_pairs={{0,12},{4,8},{8,4},{12,0},{16,28},{20,24},{24,20},{28,16},{1,13},{... | collective-permute-start | bytes 208904 | tf_op jit(solution)/shard_map/ppermute | solution.py:634
  14.6 7.0 %collective-permute-start.6 = (f32[1,17,8,128]{3,2,1,0:T(8,128)S(1)}, f32[1,17,8,128]{3,2,1,0:T(8,128)S(1)}, u32[]{:S(2)}, u32[]{:S(2)}) collective-permute-start(f32[1,17,8,128]{3,2,1,0:T(8,128)S(1)} %get-tuple-element.37), channel_id=1, source_target_pairs={{0,28},{4,24},{8,20},{12,16},{16,12},{20,8},{24,4},{28,0},{1,29},{... | collective-permute-start | bytes 208904 | tf_op jit(solution)/shard_map/ppermute | solution.py:634
  21.6 16.6 %all-to-all-start = ((f32[8,16,8,128]{3,2,1,0:T(8,128)}), f32[8,16,8,128]{3,2,1,0:T(8,128)S(1)}, u32[]{:S(2)}, u32[]{:S(2)}) async-start(f32[8,16,8,128]{3,2,1,0:T(8,128)} %shard_map.136), calls=%async_computation | async-start | bytes 1048576 | tf_op jit(solution)/shard_map/all_to_all | solution.py:631
  28.0 6.1 %collective-permute-start.7 = (f32[104,256]{1,0:T(8,128)S(1)}, f32[104,256]{1,0:T(8,128)S(1)}, u32[]{:S(2)}, u32[]{:S(2)}) collective-permute-start(f32[104,256]{1,0:T(8,128)S(1)} %get-tuple-element.40), channel_id=1, source_target_pairs={{1,2},{2,1},{5,6},{6,5},{9,10},{10,9},{13,14},{14,13},{17,18},{18,... | collective-permute-start | bytes 319496 | tf_op jit(solution)/shard_map/ppermute | solution.py:662
  28.7 5.5 %collective-permute-start.8 = (f32[104,256]{1,0:T(8,128)S(1)}, f32[104,256]{1,0:T(8,128)S(1)}, u32[]{:S(2)}, u32[]{:S(2)}) collective-permute-start(f32[104,256]{1,0:T(8,128)S(1)} %get-tuple-element.41), channel_id=1, source_target_pairs={{0,1},{1,0},{2,3},{3,2},{4,5},{5,4},{6,7},{7,6},{8,9},{9,8},{10,11... | collective-permute-start | bytes 319496 | tf_op jit(solution)/shard_map/ppermute | solution.py:663
  41.9 6.0 %collective-permute-start.9 = (f32[176,128]{1,0:T(8,128)S(1)}, f32[176,128]{1,0:T(8,128)S(1)}, u32[]{:S(2)}, u32[]{:S(2)}) collective-permute-start(f32[176,128]{1,0:T(8,128)S(1)} %get-tuple-element.49), channel_id=1, source_target_pairs={{0,3},{1,2},{2,1},{3,0},{4,7},{5,6},{6,5},{7,4},{8,11},{9,10},{10,... | collective-permute-start | bytes 270344 | tf_op jit(solution)/shard_map/ppermute | solution.py:704
  42.0 6.0 %collective-permute-start.11 = (f32[176,128]{1,0:T(8,128)S(1)}, f32[176,128]{1,0:T(8,128)S(1)}, u32[]{:S(2)}, u32[]{:S(2)}) collective-permute-start(f32[176,128]{1,0:T(8,128)S(1)} %get-tuple-element.50), channel_id=1, source_target_pairs={{0,1},{1,0},{2,3},{3,2},{4,5},{5,4},{6,7},{7,6},{8,9},{9,8},{10,11... | collective-permute-start | bytes 270344 | tf_op jit(solution)/shard_map/ppermute | solution.py:704
  43.6 4.4 %collective-permute-start.10 = (f32[96,128]{1,0:T(8,128)S(1)}, f32[96,128]{1,0:T(8,128)S(1)}, u32[]{:S(2)}, u32[]{:S(2)}) collective-permute-start(f32[96,128]{1,0:T(8,128)S(1)} %get-tuple-element.48.refs_0_), channel_id=1, source_target_pairs={{0,2},{1,3},{2,0},{3,1},{4,6},{5,7},{6,4},{7,5},{8,10},{9,11},{10,... | collective-permute-start | bytes 147464 | tf_op jit(solution)/shard_map/ppermute | solution.py:704
